TPU v7x, 32 devices: a whole 2x2x4 slice. The times are simulated.
32 devices in a mesh: groups: 2 (over x), seq: 8 (over z, y), head: 2 (over core).
Axes of the slice: x: 2, y: 2, z: 4, core: 2. Of those that a mesh axis runs over, the one named last changes fastest.
Arguments:
- queries: bfloat16 [8192, 2048], P(('groups', 'seq'), 'head'), parts along dimension 0, may hold values from -6 to 6
- keys: bfloat16 [8192, 1024], P(('groups', 'seq'), 'head'), parts along dimension 0, may hold values from -6 to 6
- values: bfloat16 [8192, 1024], P(('groups', 'seq'), 'head'), parts along dimension 0, may hold values from -6 to 6
- segments: int32 [8192], P('groups'), parts along dimension 0, may hold values from 0 to 7, never falling along the last dimension, each value on 1 to 1024 neighbouring positions
- out_weight: bfloat16 [2048, 5376], P('head'), may hold values from -0.125 to 0.125
Outputs:
- mixed: bfloat16 [8192, 5376], P(('groups', 'seq')), parts along dimension 0
There are 2 independent parts, one for each index of `groups`. A program takes and returns all parts, laid end to end along the dimension named above; an argument that names none is the same for every part. Nothing has to cross between parts.
Inputs may be any that keep to these rules, and one draw needn't show every extreme that they name: `segments`: document ids never fall along the slab; each document has 1 to 1024 tokens, one exactly 1024.
All inputs are finite; a program needn't handle non-finite values.
Results may differ from a plain program's by a relative error of at most 0.011.
Values may be sent and summed in bfloat16 or wider, within the bound.
No kernel may reach another device: no remote copies, remote signals or barrier semaphores. Data moves between devices by JAX's collectives and lax.ppermute only.
A program may use at most 128 MiB of HBM per device.

v0:
```python
import math

import jax
import jax.numpy as jnp
from jax import lax
from jax.sharding import PartitionSpec as P

HEAD_SIZE = 128
SCALAR = 168
ATTENTION_SPAN = 1024
HALO = 2


def from_behind(value, axis, by):
    peers = lax.axis_size(axis)
    pairs = [(i, i + by) for i in range(peers) if 0 <= i + by < peers]
    return lax.ppermute(value, axis, pairs)


def shards(queries, keys, values, segments, out_weight):
    tok_rows = queries.shape[0]
    heads_kv = keys.shape[1] // HEAD_SIZE
    query_group = queries.shape[1] // keys.shape[1]
    seq_index = lax.axis_index("seq")
    pieces = []
    for distance in range(HALO, 0, -1):
        pieces.append(from_behind((keys, values), "seq", distance))
    keys_ext = jnp.concatenate([piece[0] for piece in pieces] + [keys], axis=0)
    values_ext = jnp.concatenate([piece[1] for piece in pieces] + [values], axis=0)
    window_span = keys_ext.shape[0]
    first_row = seq_index * tok_rows
    pad_segments = jnp.concatenate([jnp.full((HALO * tok_rows,), -1, jnp.int32), segments])
    seg_key = lax.dynamic_slice_in_dim(pad_segments, first_row, window_span, 0)
    seg_query = lax.dynamic_slice_in_dim(segments, first_row, tok_rows, 0)
    key_pos = first_row - HALO * tok_rows + jnp.arange(window_span, dtype=jnp.int32)
    key_mat = keys_ext.reshape(window_span, heads_kv, HEAD_SIZE)
    value_mat = values_ext.reshape(window_span, heads_kv, HEAD_SIZE)
    token_block = math.gcd(tok_rows, 512)

    def one_block(block_id):
        start = block_id * token_block
        query_block = queries.reshape(token_block, heads_kv, query_group, HEAD_SIZE)
        query_pos = first_row + start + jnp.arange(token_block, dtype=jnp.int32)
        allowed = (
            (key_pos[None, :] <= query_pos[:, None])
            & (query_pos[:, None] - key_pos[None, :] < ATTENTION_SPAN)
            & (seg_key[None, :] == seg_query[:, None])
        )
        scores = jnp.einsum(
            "qkgd,pkd->kgqp", query_block, key_mat, preferred_element_type=jnp.float32
        ) * SCALAR ** (-0.5)
        masked = jnp.where(allowed, scores, -1e30)
        row_max = jnp.max(masked, axis=-1, keepdims=True)
        expo = jnp.where(allowed, jnp.exp(masked - row_max), 0.0)
        weights = (expo / jnp.sum(expo, axis=-1, keepdims=True)).astype(jnp.bfloat16)
        heads_out = jnp.einsum(
            "kgqp,pkd->qkgd", weights, value_mat, preferred_element_type=jnp.float32
        )
        return heads_out.astype(jnp.bfloat16).reshape(
            token_block, heads_kv * query_group * HEAD_SIZE
        )

    attended = lax.map(one_block, jnp.arange(tok_rows // token_block, dtype=jnp.int32)).reshape(
        tok_rows, -1
    )
    partial_terms = jnp.dot(attended, out_weight, preferred_element_type=jnp.float32)
    mixed = lax.psum(partial_terms, "head").astype(jnp.bfloat16)
    return mixed


def solution(mesh):
    placed = (
        P(("groups", "seq"), "head"),
        P(("groups", "seq"), "head"),
        P(("groups", "seq"), "head"),
        P("groups"),
        P("head", None),
    )
    return jax.shard_map(
        shards, mesh=mesh, in_specs=placed, out_specs=P(("groups", "seq"), None), check_vma=False
    )
```

profile of v0, /device:TPU:25, one launch (start us, length us, event | category | flops | bytes accessed | tf_op | source)
XLA Modules:
  0.0 131.4 jit_solution(17479699707473325721)
XLA Ops:
  0.0 1.3 copy.10
  1.3 3.1 %collective-permute-start.3 = (bf16[512,512]{0,1:T(8,128)(2,1)S(1)}, bf16[512,512]{0,1:T(8,128)(2,1)}, u32[]{:S(2)}, u32[]{:S(2)}) collective-permute-start(bf16[512,512]{0,1:T(8,128)(2,1)S(1)} %copy.10), channel_id=1, source_target_pairs={{0,2},{2,4},{4,6},{6,8},{8,10},{10,12},{12,14},{1,3},{3,5},{5,7},{... | collective-permute-start | bytes 1572872 | tf_op jit(solution)/shard_map/ppermute | solution.py:17
  4.4 1.3 collective-permute-start.2
  5.7 1.3 collective-permute-start
  7.0 1.9 %collective-permute-start.1 = (bf16[512,512]{1,0:T(8,128)(2,1)}, bf16[512,512]{1,0:T(8,128)(2,1)}, u32[]{:S(2)}, u32[]{:S(2)}) collective-permute-start(bf16[512,512]{1,0:T(8,128)(2,1)} %param.7), channel_id=1, source_target_pairs={{0,2},{2,4},{4,6},{6,8},{8,10},{10,12},{12,14},{1,3},{3,5},{5,7},{... | collective-permute-start | bytes 1572872 | tf_op jit(solution)/shard_map/ppermute | solution.py:17
  9.0 0.8 pad_dynamic-slice_fusion
  9.7 0.8 dynamic_slice.10
  10.5 1.9 %fusion.9 = pred[512,1536]{0,1:T(8,128)(4,1)} fusion(s32[512]{0:T(512)S(1)} %dynamic_slice.10, s32[512]{0:T(512)S(1)} %iota_add_fusion.1, s32[1536]{0:T(1024)S(1)} %get-tuple-element.21, s32[1536]{0:T(1024)S(1)} %get-tuple-element.22), kind=kLoop, calls=%fused_computation.12 | loop fusion | flops 4718592 | bytes 802816 | tf_op jit(solution)/shard_map/while/body/eval_jaxpr/and | solution.py:45
  12.4 1.8 %reshape.31 = bf16[512,4,2,128]{3,2,1,0:T(2,128)(2,1)S(1)} reshape(bf16[512,1024]{1,0:T(8,128)(2,1)} %param.5) | data formatting | bytes 2097152 | tf_op jit(solution)/shard_map/while/body/eval_jaxpr/reshape | solution.py:42
  14.2 0.0 copy-start.1
  14.2 15.8 %collective-permute-done = bf16[512,512]{1,0:T(8,128)(2,1)S(1)} collective-permute-done((bf16[512,512]{1,0:T(8,128)(2,1)}, bf16[512,512]{1,0:T(8,128)(2,1)S(1)}, u32[]{:S(2)}, u32[]{:S(2)}) %collective-permute-start) | collective-permute-done | bytes 524320 | tf_op jit(solution)/shard_map/ppermute | solution.py:17
  30.0 0.0 copy-start.2
  30.0 0.8 copy-done.2
  30.8 19.8 %collective-permute-done.1 = bf16[512,512]{1,0:T(8,128)(2,1)} collective-permute-done((bf16[512,512]{1,0:T(8,128)(2,1)}, bf16[512,512]{1,0:T(8,128)(2,1)}, u32[]{:S(2)}, u32[]{:S(2)}) %collective-permute-start.1) | collective-permute-done | bytes 524320 | tf_op jit(solution)/shard_map/ppermute | solution.py:17
  50.7 1.5 %pad_maximum_fusion = bf16[1536,512]{1,0:T(8,128)(2,1)S(1)} fusion(bf16[512,512]{1,0:T(8,128)(2,1)} %param.7, bf16[512,512]{1,0:T(8,128)(2,1)} %collective-permute-done.1, bf16[512,512]{1,0:T(8,128)(2,1)} %copy-done.2), kind=kLoop, calls=%fused_computation.13 | loop fusion | flops 4718592 | bytes 3145728 | tf_op jit(solution)/shard_map/concatenate | solution.py:29
  52.1 1.6 %copy.9 = bf16[1536,512]{0,1:T(8,128)(2,1)} copy(bf16[1536,512]{1,0:T(8,128)(2,1)S(1)} %pad_maximum_fusion) | data formatting | bytes 3145728 | tf_op jit(solution)/shard_map/concatenate | solution.py:29
  53.7 0.0 collective-permute-done.3
  53.7 0.0 collective-permute-done.2
  53.7 2.5 %pad_maximum_fusion.1 = bf16[1536,512]{0,1:T(8,128)(2,1)} fusion(bf16[512,512]{0,1:T(8,128)(2,1)S(1)} %copy.10, bf16[512,512]{0,1:T(8,128)(2,1)} %collective-permute-done.3, bf16[512,512]{0,1:T(8,128)(2,1)} %collective-permute-done.2), kind=kLoop, calls=%fused_computation.14 | loop fusion | flops 4718592 | bytes 3145728 | tf_op jit(solution)/shard_map/concatenate | solution.py:28
  56.2 0.0 copy-done.1
  56.2 0.0 copy-start
  56.2 13.4 %fusion.28 = f32[4,2,512]{2,1,0:T(2,128)S(1)} fusion(pred[512,1536]{0,1:T(8,128)(4,1)} %fusion.9, bf16[1536,4,128,1]{0,2,3,1:T(8,128)(2,1)} %bitcast.32, bf16[512,4,2,128]{3,2,1,0:T(2,128)(2,1)S(1)} %reshape.31), kind=kOutput, calls=%fused_computation.29 | convolution fusion | flops 1642071552 | bytes 3424256 | tf_op jit(solution)/shard_map/while/body/eval_jaxpr/sub | solution.py:54
  69.6 0.0 copy-done
  69.6 15.7 %fusion.10 = bf16[4,128,2,512]{3,1,2,0:T(8,128)(2,1)S(1)} fusion(bf16[1536,4,128,1]{0,2,3,1:T(8,128)(2,1)S(1)} %bitcast.31, f32[4,2,512]{2,1,0:T(2,128)S(1)} %fusion.28, pred[512,1536]{0,1:T(8,128)(4,1)} %fusion.9, bf16[1536,4,128,1]{0,2,3,1:T(8,128)(2,1)} %bitcast.33, bf16[512,4,2,128]{3,2,1,0:T(2,128)(2,1)} %copy-done.1), kind=kOutput, calls=%fused_computation.15 | convolution fusion | flops 3259504128 | bytes 6045696 | tf_op jit(solution)/shard_map/while/body/eval_jaxpr/kgqp,pkd->qkgd/dot_general | solution.py:56
  85.3 12.7 %fusion.31 = f32[512,5376]{1,0:T(8,128)} fusion(bf16[512,1024]{0,1:T(8,128)(2,1)S(1)} %bitcast.34, bf16[1024,5376]{1,0:T(8,128)(2,1)} %param.9), kind=kOutput, calls=%fused_computation.30 | convolution fusion | flops 5637144576 | bytes 23068672 | tf_op jit(solution)/shard_map/dot_general | solution.py:66
  98.1 33.3 %all-reduce.2 = bf16[512,5376]{1,0:T(8,128)(2,1)} all-reduce(f32[512,5376]{1,0:T(8,128)} %fusion.31), channel_id=1, replica_groups=mesh['groups'=2,'seq'=8,'head'=2] {'head'}, use_global_device_ids=true, to_apply=%region_2.3 | all-reduce | flops 2752512 | bytes 16515072 | tf_op jit(solution)/shard_map/psum | solution.py:67
  (1 shorter events, 0.0 us)
Async XLA Ops:
  1.3 52.4 %collective-permute-start.3 = (bf16[512,512]{0,1:T(8,128)(2,1)S(1)}, bf16[512,512]{0,1:T(8,128)(2,1)}, u32[]{:S(2)}, u32[]{:S(2)}) collective-permute-start(bf16[512,512]{0,1:T(8,128)(2,1)S(1)} %copy.10), channel_id=1, source_target_pairs={{0,2},{2,4},{4,6},{6,8},{8,10},{10,12},{12,14},{1,3},{3,5},{5,7},{... | collective-permute-start | bytes 1572872 | tf_op jit(solution)/shard_map/ppermute | solution.py:17
  4.4 49.3 %collective-permute-start.2 = (bf16[512,512]{0,1:T(8,128)(2,1)S(1)}, bf16[512,512]{0,1:T(8,128)(2,1)}, u32[]{:S(2)}, u32[]{:S(2)}) collective-permute-start(bf16[512,512]{0,1:T(8,128)(2,1)S(1)} %copy.10), channel_id=1, source_target_pairs={{0,4},{2,6},{4,8},{6,10},{8,12},{10,14},{1,5},{3,7},{5,9},{7,11},{... | collective-permute-start | bytes 1572872 | tf_op jit(solution)/shard_map/ppermute | solution.py:17
  5.7 24.3 %collective-permute-start = (bf16[512,512]{1,0:T(8,128)(2,1)}, bf16[512,512]{1,0:T(8,128)(2,1)S(1)}, u32[]{:S(2)}, u32[]{:S(2)}) collective-permute-start(bf16[512,512]{1,0:T(8,128)(2,1)} %param.7), channel_id=1, source_target_pairs={{0,4},{2,6},{4,8},{6,10},{8,12},{10,14},{1,5},{3,7},{5,9},{7,11},{... | collective-permute-start | bytes 1572872 | tf_op jit(solution)/shard_map/ppermute | solution.py:17
  7.0 43.6 %collective-permute-start.1 = (bf16[512,512]{1,0:T(8,128)(2,1)}, bf16[512,512]{1,0:T(8,128)(2,1)}, u32[]{:S(2)}, u32[]{:S(2)}) collective-permute-start(bf16[512,512]{1,0:T(8,128)(2,1)} %param.7), channel_id=1, source_target_pairs={{0,2},{2,4},{4,6},{6,8},{8,10},{10,12},{12,14},{1,3},{3,5},{5,7},{... | collective-permute-start | bytes 1572872 | tf_op jit(solution)/shard_map/ppermute | solution.py:17
  14.2 42.0 %copy-start.1 = (bf16[512,4,2,128]{3,2,1,0:T(2,128)(2,1)}, bf16[512,4,2,128]{3,2,1,0:T(2,128)(2,1)S(1)}, u32[]{:S(2)}) copy-start(bf16[512,4,2,128]{3,2,1,0:T(2,128)(2,1)S(1)} %reshape.31) | copy-start | bytes 3145732
  30.0 0.8 copy-start.2
  56.2 13.4 %copy-start = (bf16[1536,512]{0,1:T(8,128)(2,1)S(1)}, bf16[1536,512]{0,1:T(8,128)(2,1)}, u32[]{:S(2)}) copy-start(bf16[1536,512]{0,1:T(8,128)(2,1)} %copy.9) | copy-start | bytes 4718596
where the time goes:
time: 132 us; the launch traced here: 131 us
  matrix products  41.9 us (32%)
  waiting for transfers between devices  35.7 us (27%)
  blocking collectives  33.3 us (25%)
  starting transfers between devices  7.66 us (6%)
  other arithmetic  6.59 us (5%)
  local copies, waits for them, and re-layouts  6.17 us (5%)
    ppermute x4, waiting for transfers between devices, from_behind(): return lax.ppermute(value, axis, pairs)  35.7 us
    psum x1, blocking collectives, shards(): mixed = lax.psum(partial_terms, 'head').astype(jnp.bfloat16)  33.3 us
    dot_general x1, matrix products, one_block(): jnp.einsum('kgqp,pkd->qkgd', weights, value_mat, preferred_element_type=j...  15.7 us
    sub x1, matrix products, one_block(): expo = jnp.where(allowed, jnp.exp(masked - row_max), 0.0)  13.4 us
    dot_general x1, matrix products, shards(): jnp.dot(attended, out_weight, preferred_element_type=jnp.float32)  12.7 us
    ppermute x4, starting transfers between devices, from_behind(): return lax.ppermute(value, axis, pairs)  7.66 us
  transfers between devices with their start and end apart: 4, of which 2 were waited for; matrix products, arithmetic and copies ran while one was open for 6% of the time, Pallas kernels for 0%

commit v1 on v0

v1 whole, which is shorter than its diff:
```python
import jax
import jax.numpy as jnp
from jax import lax
from jax.experimental import pallas as pl
from jax.experimental.pallas import tpu as pltpu
from jax.sharding import PartitionSpec as P

HEAD_SIZE = 128
SCALAR = 168
ATTENTION_SPAN = 1024
TILE = 128
MARK = 128.0
LOG2E = 1.4426950408889634
MIB = 1 << 20


def joined(*parts):
    parts = [part for part in parts if part.shape[1]]
    return parts[0] if len(parts) == 1 else jnp.concatenate(parts, axis=1)


def attend_kernel(q_ref, own_ref, near_ref, far_ref, mark_ref, out_ref):
    rows = own_ref.shape[0]
    group = q_ref.shape[1] // HEAD_SIZE
    factor = LOG2E * SCALAR ** (-0.5)
    ones = jnp.ones((rows, HEAD_SIZE), jnp.bfloat16)

    def keys_of(ref, block):
        marks = mark_ref[block * rows : (block + 1) * rows, :]
        return jnp.concatenate([ref[:, :HEAD_SIZE], marks], axis=1)

    def values_of(ref):
        return jnp.concatenate([ref[:, HEAD_SIZE:], ones], axis=1)

    keys = [keys_of(far_ref, 0), keys_of(near_ref, 1), keys_of(own_ref, 2)]
    values = [values_of(far_ref), values_of(near_ref), values_of(own_ref)]
    row = lax.broadcasted_iota(jnp.int32, (TILE, TILE), 0)
    col = lax.broadcasted_iota(jnp.int32, (TILE, TILE), 1)
    inside = jnp.concatenate([col > row] * group, axis=0)
    causal = jnp.concatenate([col <= row] * group, axis=0)
    for t in range(rows // TILE):
        span = slice(t * TILE, (t + 1) * TILE)
        marks = mark_ref[2 * rows + t * TILE : 2 * rows + (t + 1) * TILE, :]
        query = jnp.concatenate(
            [
                jnp.concatenate([q_ref[span, g * HEAD_SIZE : (g + 1) * HEAD_SIZE], marks], axis=1)
                for g in range(group)
            ],
            axis=0,
        )
        parts = [
            (keys[0][t * TILE :], values[0][t * TILE :]),
            (keys[1], values[1]),
            (keys[2][: (t + 1) * TILE], values[2][: (t + 1) * TILE]),
        ]
        scores = [
            lax.dot_general(
                query, key, (((1,), (1,)), ((), ())), preferred_element_type=jnp.float32
            )
            for key, _ in parts
        ]
        first = jnp.where(inside, scores[0][:, :TILE], -1e30)
        scores[0] = joined(first, *([scores[0][:, TILE:]] if scores[0].shape[1] > TILE else []))
        last = jnp.where(causal, scores[2][:, t * TILE :], -1e30)
        scores[2] = joined(*([scores[2][:, : t * TILE]] if t else []), last)
        top = jnp.maximum(
            jnp.maximum(
                jnp.max(scores[0], axis=1, keepdims=True),
                jnp.max(scores[1], axis=1, keepdims=True),
            ),
            jnp.max(scores[2], axis=1, keepdims=True),
        )
        total = None
        for score, (_, value) in zip(scores, parts):
            weight = jnp.exp2((score - top) * factor).astype(jnp.bfloat16)
            term = jnp.dot(weight, value, preferred_element_type=jnp.float32)
            total = term if total is None else total + term
        result = (total[:, :HEAD_SIZE] / total[:, HEAD_SIZE:]).astype(jnp.bfloat16)
        for g in range(group):
            out_ref[span, g * HEAD_SIZE : (g + 1) * HEAD_SIZE] = result[
                g * TILE : (g + 1) * TILE
            ]


def attend(queries, own, near, far, marks, head):
    rows = own.shape[0]
    heads_kv = queries.shape[1] // 256
    width = queries.shape[1] // heads_kv
    whole = lambda a: pl.BlockSpec(a.shape, lambda i: (0,) * a.ndim)
    return pl.pallas_call(
        attend_kernel,
        grid=(1,),
        in_specs=[
            pl.BlockSpec((rows, width), lambda i: (0, head)),
            whole(own),
            whole(near),
            whole(far),
            whole(marks),
        ],
        out_specs=pl.BlockSpec((rows, width), lambda i: (0, 0)),
        out_shape=jax.ShapeDtypeStruct((rows, width), jnp.bfloat16),
        compiler_params=pltpu.CompilerParams(vmem_limit_bytes=12 * MIB),
        cost_estimate=pl.CostEstimate(
            flops=4 * 1024 * 1152 * 256, bytes_accessed=2 * MIB, transcendentals=1024 * 1152
        ),
    )(queries, own, near, far, marks)


def project_kernel(core_ref, *refs, pieces, has_base):
    own, other = refs[:pieces], refs[pieces : 2 * pieces]
    own_w, other_w = refs[2 * pieces], refs[2 * pieces + 1]
    base_ref = refs[2 * pieces + 2] if has_base else None
    out_ref = refs[-1]

    def run(sides):
        total = base_ref[...] if has_base else None
        for arrays, weight in sides:
            for i, array in enumerate(arrays):
                depth = array.shape[1]
                term = jnp.dot(
                    array[...],
                    weight[i * depth : (i + 1) * depth, :],
                    preferred_element_type=jnp.float32,
                )
                total = term if total is None else total + term
        out_ref[...] = total.astype(out_ref.dtype)

    @pl.when(core_ref[0] == 0)
    def _():
        run([(own, own_w), (other, other_w)])

    @pl.when(core_ref[0] != 0)
    def _():
        run([(other, other_w), (own, own_w)])


def project(core, own, other, own_w, other_w, row_block, base, dtype):
    rows, depth = own[0].shape
    pieces = len(own)
    columns = own_w.shape[1]
    tile = 768 if columns % 768 == 0 else 128
    small = pl.BlockSpec((rows, depth), lambda n, c: (0, 0))
    weight = pl.BlockSpec((pieces * depth, tile), lambda n, c: (row_block, n))
    block = pl.BlockSpec((rows, tile), lambda n, c: (0, n))
    has_base = base is not None
    return pl.pallas_call(
        lambda *refs: project_kernel(*refs, pieces=pieces, has_base=has_base),
        grid_spec=pltpu.PrefetchScalarGridSpec(
            num_scalar_prefetch=1,
            grid=(columns // tile,),
            in_specs=[small] * (2 * pieces) + [weight, weight] + [block] * has_base,
            out_specs=block,
        ),
        out_shape=jax.ShapeDtypeStruct((rows, columns), dtype),
        compiler_params=pltpu.CompilerParams(vmem_limit_bytes=24 * MIB),
        cost_estimate=pl.CostEstimate(
            flops=4 * rows * pieces * depth * columns,
            bytes_accessed=16 * MIB,
            transcendentals=0,
        ),
    )(core, *own, *other, own_w, other_w, *([base] if has_base else []))


def shards(queries, keys, values, segments, out_weight):
    rows = queries.shape[0]
    heads_kv = keys.shape[1] // HEAD_SIZE
    peers = lax.axis_size("seq")
    seq_index = lax.axis_index("seq")
    core = lax.axis_index("head").astype(jnp.int32).reshape(1)
    swap = [(0, 1), (1, 0)]

    def packed(h):
        part = slice(h * HEAD_SIZE, (h + 1) * HEAD_SIZE)
        return jnp.concatenate([keys[:, part], values[:, part]], axis=1)

    own = [packed(h) for h in range(heads_kv)]
    two_on = [(i, i + 2) for i in range(peers - 2)]
    one_on = [(i, i + 1) for i in range(peers - 1)]
    pair = [(i, i ^ 1) for i in range(peers)]
    odd = seq_index % 2 == 1
    far = [lax.ppermute(x, "seq", two_on) for x in own]
    near = [
        lax.ppermute(jnp.where(odd, f, x), "seq", pair) for f, x in zip(far[:-1], own[:-1])
    ]
    near.append(lax.ppermute(own[-1], "seq", one_on))
    other_w = lax.ppermute(out_weight, "head", swap)

    halo = 2 * rows
    padded = jnp.concatenate([jnp.full((halo,), -1, jnp.int32), segments])
    seen = lax.dynamic_slice_in_dim(padded, seq_index * rows, halo + rows, 0)
    ids = lax.broadcasted_iota(jnp.int32, (halo + rows, HEAD_SIZE), 1)
    marks = jnp.where(seen[:, None] == ids, MARK, 0.0).astype(jnp.bfloat16)

    mine = [
        attend(queries, own[h], near[h], far[h], marks, h) for h in range(heads_kv)
    ]
    theirs = [lax.ppermute(x, "head", swap) for x in mine]
    half = heads_kv // 2
    base = project(
        core, mine[:half], theirs[:half], out_weight, other_w, 0, None, jnp.float32
    )
    return project(
        core, mine[half:], theirs[half:], out_weight, other_w, 1, base, jnp.bfloat16
    )


def solution(mesh):
    placed = (
        P(("groups", "seq"), "head"),
        P(("groups", "seq"), "head"),
        P(("groups", "seq"), "head"),
        P("groups"),
        P("head", None),
    )
    return jax.shard_map(
        shards, mesh=mesh, in_specs=placed, out_specs=P(("groups", "seq"), None), check_vma=False
    )
```

time: 132 us -> 84.6 us (0.64)
  the two profiles are of different devices: /device:TPU:25 before, /device:TPU:0 now
where the time goes in v1:
time: 84.6 us; the launch traced here: 83.7 us
  Pallas kernels  32.5 us (38%)
  starting transfers between devices  32.3 us (38%)
  local copies, waits for them, and re-layouts  11.6 us (14%)
  waiting for transfers between devices  3.78 us (4%)
  other arithmetic  3.24 us (4%)
    pallas_call x2, Pallas kernels, project(): pl.pallas_call(lambda *refs: project_kernel(*refs, pieces=pieces, has_bas...  22 us
    ppermute x4, starting transfers between devices, shards(): far = [lax.ppermute(x, 'seq', two_on) for x in own]  15.3 us
    ppermute x3, starting transfers between devices, shards(): lax.ppermute(jnp.where(odd, f, x), 'seq', pair)  11.3 us
    pallas_call x4, Pallas kernels, attend(): pl.pallas_call(attend_kernel, grid=(1,), in_specs=[pl.BlockSpec((rows, wi...  10.5 us
    unnamed x22, local copies, waits for them, and re-layouts  9.44 us
    ppermute x1, starting transfers between devices, shards(): near.append(lax.ppermute(own[-1], 'seq', one_on))  4.12 us
    select_n x3, other arithmetic, shards(): jnp.where(odd, f, x)  2.85 us
    ppermute x4, waiting for transfers between devices, shards(): far = [lax.ppermute(x, 'seq', two_on) for x in own]  2.17 us
  transfers between devices with their start and end apart: 13, of which 3 were waited for; matrix products, arithmetic and copies ran while one was open for 6% of the time, Pallas kernels for 24%

profile of v1, /device:TPU:0, one launch (start us, length us, event | category | flops | bytes accessed | tf_op | source)
XLA Modules:
  0.0 83.7 jit_solution(3261687649665152643)
XLA Ops:
  0.0 0.0 copy-start.3
  0.0 0.5 collective-permute-start.6
  0.5 1.4 %fusion = (bf16[512,128]{1,0:T(8,128)(2,1)S(1)}, bf16[512,128]{1,0:T(8,128)(2,1)S(1)}, bf16[512,128]{1,0:T(8,128)(2,1)S(1)}, bf16[512,128]{1,0:T(8,128)(2,1)S(1)...) fusion(bf16[512,512]{1,0:T(8,128)(2,1)} %param.6, ...), kind=kLoop, calls=%fused_computation.10 | loop fusion | bytes 2097152 | tf_op jit(solution)/shard_map/slice | solution.py:174
  1.8 0.0 copy-start.4
  1.9 0.0 copy-start.5
  1.9 0.0 copy-start.6
  1.9 0.0 copy-start.7
  1.9 5.3 %collective-permute-start.3 = (bf16[512,256]{1,0:T(8,128)(2,1)S(1)}, bf16[512,256]{1,0:T(8,128)(2,1)}, u32[]{:S(2)}, u32[]{:S(2)}) collective-permute-start(bf16[512,256]{1,0:T(8,128)(2,1)S(1)} %pad_maximum_fusion.1.own_ref), channel_id=1, source_target_pairs={{0,4},{2,6},{4,8},{6,10},{8,12},{10,14},{1,5},{3,7},{5,9},{7,11},{... | collective-permute-start | bytes 786440 | tf_op jit(solution)/shard_map/ppermute | solution.py:181
  7.2 4.1 %collective-permute-start.2 = (bf16[512,256]{1,0:T(8,128)(2,1)S(1)}, bf16[512,256]{1,0:T(8,128)(2,1)}, u32[]{:S(2)}, u32[]{:S(2)}) collective-permute-start(bf16[512,256]{1,0:T(8,128)(2,1)S(1)} %pad_maximum_fusion.1.own_ref), channel_id=1, source_target_pairs={{0,2},{2,4},{4,6},{6,8},{8,10},{10,12},{12,14},{1,3},{3,5},{5,7},{... | collective-permute-start | bytes 786440 | tf_op jit(solution)/shard_map/ppermute | solution.py:185
  11.3 2.1 %collective-permute-start.7 = (bf16[512,256]{1,0:T(8,128)(2,1)S(1)}, bf16[512,256]{1,0:T(8,128)(2,1)S(1)}, u32[]{:S(2)}, u32[]{:S(2)}) collective-permute-start(bf16[512,256]{1,0:T(8,128)(2,1)S(1)} %pad_maximum_fusion.2.own_ref), channel_id=1, source_target_pairs={{0,4},{2,6},{4,8},{6,10},{8,12},{10,14},{1,5},{3,7},{5,9},{7,11},{... | collective-permute-start | bytes 786440 | tf_op jit(solution)/shard_map/ppermute | solution.py:181
  13.5 0.0 copy-done.4
  13.5 0.0 copy-done.5
  13.5 3.5 %collective-permute-start.9 = (bf16[512,256]{1,0:T(8,128)(2,1)S(1)}, bf16[512,256]{1,0:T(8,128)(2,1)S(1)}, u32[]{:S(2)}, u32[]{:S(2)}) collective-permute-start(bf16[512,256]{1,0:T(8,128)(2,1)S(1)} %pad_maximum_fusion.3.own_ref), channel_id=1, source_target_pairs={{0,4},{2,6},{4,8},{6,10},{8,12},{10,14},{1,5},{3,7},{5,9},{7,11},{... | collective-permute-start | bytes 786440 | tf_op jit(solution)/shard_map/ppermute | solution.py:181
  17.0 0.0 copy-done.6
  17.0 0.0 copy-done.7
  17.1 0.8 pad_dynamic-slice_fusion
  17.8 0.3 select_convert_fusion.mark_ref
  18.2 2.0 %collective-permute-done.7.far_ref = bf16[512,256]{1,0:T(8,128)(2,1)S(1)} collective-permute-done((bf16[512,256]{1,0:T(8,128)(2,1)S(1)}, bf16[512,256]{1,0:T(8,128)(2,1)S(1)}, u32[]{:S(2)}, u32[]{:S(2)}) %collective-permute-start.7) | collective-permute-done | bytes 262176 | tf_op jit(solution)/shard_map/ppermute | solution.py:181
  20.2 4.4 %collective-permute-start = (bf16[512,256]{1,0:T(8,128)(2,1)S(1)}, bf16[512,256]{1,0:T(8,128)(2,1)S(1)}, u32[]{:S(2)}, u32[]{:S(2)}) collective-permute-start(bf16[512,256]{1,0:T(8,128)(2,1)S(1)} %pad_maximum_fusion.own_ref), channel_id=1, source_target_pairs={{0,4},{2,6},{4,8},{6,10},{8,12},{10,14},{1,5},{3,7},{5,9},{7,11},{... | collective-permute-start | bytes 786440 | tf_op jit(solution)/shard_map/ppermute | solution.py:181
  24.5 1.0 %broadcast_select_fusion.1 = bf16[512,256]{1,0:T(8,128)(2,1)S(1)} fusion(bf16[512,256]{1,0:T(8,128)(2,1)S(1)} %collective-permute-done.7.far_ref, pred[]{:T(512)S(6)} %eq.13, bf16[512,128]{1,0:T(8,128)(2,1)} %copy-done.7, bf16[512,128]{1,0:T(8,128)(2,1)} %copy-done.6), kind=kLoop, calls=%fused_computation.7 | loop fusion | flops 655360 | bytes 786433 | tf_op jit(solution)/shard_map/jit(_where)/select_n | solution.py:183
  25.6 0.2 collective-permute-done.9.far_ref
  25.8 5.7 %collective-permute-start.8 = (bf16[512,256]{1,0:T(8,128)(2,1)S(1)}, bf16[512,256]{1,0:T(8,128)(2,1)S(1)}, u32[]{:S(2)}, u32[]{:S(2)}) collective-permute-start(bf16[512,256]{1,0:T(8,128)(2,1)S(1)} %broadcast_select_fusion.1), channel_id=1, source_target_pairs={{0,2},{2,0},{4,6},{6,4},{8,10},{10,8},{12,14},{14,12},{1,3},{3,1},... | collective-permute-start | bytes 786440 | tf_op jit(solution)/shard_map/ppermute | solution.py:183
  31.5 1.0 %broadcast_select_fusion = bf16[512,256]{1,0:T(8,128)(2,1)S(1)} fusion(bf16[512,256]{1,0:T(8,128)(2,1)S(1)} %collective-permute-done.9.far_ref, pred[]{:T(512)S(6)} %eq.13, bf16[512,128]{1,0:T(8,128)(2,1)} %copy-done.5, bf16[512,128]{1,0:T(8,128)(2,1)} %copy-done.4), kind=kLoop, calls=%fused_computation.6 | loop fusion | flops 655360 | bytes 786433 | tf_op jit(solution)/shard_map/jit(_where)/select_n | solution.py:183
  32.5 0.0 collective-permute-done.far_ref
  32.5 4.1 %collective-permute-start.10 = (bf16[512,256]{1,0:T(8,128)(2,1)S(1)}, bf16[512,256]{1,0:T(8,128)(2,1)S(1)}, u32[]{:S(2)}, u32[]{:S(2)}) collective-permute-start(bf16[512,256]{1,0:T(8,128)(2,1)S(1)} %broadcast_select_fusion), channel_id=1, source_target_pairs={{0,2},{2,0},{4,6},{6,4},{8,10},{10,8},{12,14},{14,12},{1,3},{3,1},... | collective-permute-start | bytes 786440 | tf_op jit(solution)/shard_map/ppermute | solution.py:183
  36.6 0.8 broadcast_select_fusion.2
  37.4 0.0 collective-permute-done.8.near_ref
  37.4 1.5 %collective-permute-start.1 = (bf16[512,256]{1,0:T(8,128)(2,1)}, bf16[512,256]{1,0:T(8,128)(2,1)}, u32[]{:S(2)}, u32[]{:S(2)}) collective-permute-start(bf16[512,256]{1,0:T(8,128)(2,1)} %broadcast_select_fusion.2), channel_id=1, source_target_pairs={{0,2},{2,0},{4,6},{6,4},{8,10},{10,8},{12,14},{14,12},{1,3},{3,1},... | collective-permute-start | bytes 786440 | tf_op jit(solution)/shard_map/ppermute | solution.py:183
  38.9 0.0 copy-start.2
  38.9 1.2 %copy-done.2 = bf16[512,1024]{1,0:T(8,128)(2,1)S(1)} copy-done((bf16[512,1024]{1,0:T(8,128)(2,1)S(1)}, bf16[512,1024]{1,0:T(8,128)(2,1)}, u32[]{:S(2)}) %copy-start.2) | copy-done | bytes 1048600
  40.1 2.1 %shard_map.57.refs_1_ = bf16[512,256]{1,0:T(8,128)(2,1)S(1)} custom-call(bf16[512,1024]{1,0:T(8,128)(2,1)S(1)} %copy-done.2, bf16[512,256]{1,0:T(8,128)(2,1)S(1)} %pad_maximum_fusion.2.own_ref, bf16[512,256]{1,0:T(8,128)(2,1)S(1)} %collective-permute-done.8.near_ref, bf16[512,256]{1,0:T(8,128)(2,1)S(1)} %collective-permute-done.7.far_ref, ...), custom_call_target="tpu_custom_call" | custom-call | flops 1207959552 | bytes 2097152 | tf_op jit(solution)/shard_map/pallas_call | solution.py:90
  42.2 1.6 %collective-permute-done.10.near_ref = bf16[512,256]{1,0:T(8,128)(2,1)S(1)} collective-permute-done((bf16[512,256]{1,0:T(8,128)(2,1)S(1)}, bf16[512,256]{1,0:T(8,128)(2,1)S(1)}, u32[]{:S(2)}, u32[]{:S(2)}) %collective-permute-start.10) | collective-permute-done | bytes 262176 | tf_op jit(solution)/shard_map/ppermute | solution.py:183
  43.8 0.0 collective-permute-start.11
  43.8 2.1 %shard_map.58.refs_2_ = bf16[512,256]{1,0:T(8,128)(2,1)S(1)} custom-call(bf16[512,1024]{1,0:T(8,128)(2,1)S(1)} %copy-done.2, bf16[512,256]{1,0:T(8,128)(2,1)S(1)} %pad_maximum_fusion.3.own_ref, bf16[512,256]{1,0:T(8,128)(2,1)S(1)} %collective-permute-done.10.near_ref, bf16[512,256]{1,0:T(8,128)(2,1)S(1)} %collective-permute-done.9.far_ref, ...), custom_call_target="tpu_custom_call" | custom-call | flops 1207959552 | bytes 2097152 | tf_op jit(solution)/shard_map/pallas_call | solution.py:90
  45.9 0.0 collective-permute-done.3.far_ref
  45.9 0.6 collective-permute-start.12
  46.5 0.0 collective-permute-done.2.near_ref
  46.5 0.0 copy-done.3
  46.5 0.0 slice-start
  46.5 3.3 %shard_map.56.refs_2_ = bf16[512,256]{1,0:T(8,128)(2,1)S(1)} custom-call(bf16[512,1024]{1,0:T(8,128)(2,1)S(1)} %copy-done.3, bf16[512,256]{1,0:T(8,128)(2,1)S(1)} %pad_maximum_fusion.1.own_ref, bf16[512,256]{1,0:T(8,128)(2,1)} %collective-permute-done.2.near_ref, bf16[512,256]{1,0:T(8,128)(2,1)} %collective-permute-done.3.far_ref, ...), custom_call_target="tpu_custom_call" | custom-call | flops 1207959552 | bytes 2097152 | tf_op jit(solution)/shard_map/pallas_call | solution.py:90
  49.8 0.1 collective-permute-start.5
  49.9 0.0 collective-permute-done.1.near_ref
  49.9 3.0 %shard_map.55.refs_1_ = bf16[512,256]{1,0:T(8,128)(2,1)S(1)} custom-call(bf16[512,1024]{1,0:T(8,128)(2,1)S(1)} %copy-done.3, bf16[512,256]{1,0:T(8,128)(2,1)S(1)} %pad_maximum_fusion.own_ref, bf16[512,256]{1,0:T(8,128)(2,1)} %collective-permute-done.1.near_ref, bf16[512,256]{1,0:T(8,128)(2,1)S(1)} %collective-permute-done.far_ref, ...), custom_call_target="tpu_custom_call" | custom-call | flops 1207959552 | bytes 2097152 | tf_op jit(solution)/shard_map/pallas_call | solution.py:90
  52.9 0.5 collective-permute-start.4
  53.5 0.0 collective-permute-done.11.refs_3_
  53.5 0.0 collective-permute-done.12.refs_4_
  53.5 0.0 collective-permute-done.6.refs_6_
  53.5 0.0 copy-start
  53.5 4.1 %copy-done = bf16[1024,5376]{1,0:T(8,128)(2,1)S(1)} copy-done((bf16[1024,5376]{1,0:T(8,128)(2,1)S(1)}, bf16[1024,5376]{1,0:T(8,128)(2,1)}, u32[]{:S(2)}) %copy-start) | copy-done | bytes 11010072
  57.6 0.0 slice-start.1
  57.6 0.0 slice-start.2
  57.6 9.4 %shard_map.59.refs_7_ = f32[512,5376]{1,0:T(8,128)S(1)} custom-call(s32[1]{0:T(128)} %bitcast.refs_0_, bf16[512,256]{1,0:T(8,128)(2,1)S(1)} %shard_map.57.refs_1_, bf16[512,256]{1,0:T(8,128)(2,1)S(1)} %shard_map.58.refs_2_, bf16[512,256]{1,0:T(8,128)(2,1)S(1)} %collective-permute-done.11.refs_3_, bf16[512,256]{1,0:T(8,128)(2,1)S(1)} %collective-permute-done.12.refs_4_, ...), custom_call_target="tpu_custom_call" | custom-call | flops 5637144576 | bytes 16777216 | tf_op jit(solution)/shard_map/pallas_call | solution.py:146
  67.0 0.0 copy-start.1
  67.1 4.1 %copy-done.1 = f32[512,5376]{1,0:T(8,128)} copy-done((f32[512,5376]{1,0:T(8,128)}, f32[512,5376]{1,0:T(8,128)S(1)}, u32[]{:S(2)}) %copy-start.1) | copy-done | bytes 11010072
  71.1 0.0 collective-permute-done.5.refs_4_
  71.1 0.0 collective-permute-done.4.refs_3_
  71.1 0.0 slice-done
  71.1 0.0 slice-done.1
  71.1 0.0 slice-done.2
  71.2 12.6 %shard_map.60 = bf16[512,5376]{1,0:T(8,128)(2,1)} custom-call(s32[1]{0:T(128)} %bitcast.refs_0_, bf16[512,256]{1,0:T(8,128)(2,1)S(1)} %shard_map.55.refs_1_, bf16[512,256]{1,0:T(8,128)(2,1)S(1)} %shard_map.56.refs_2_, bf16[512,256]{1,0:T(8,128)(2,1)S(1)} %collective-permute-done.4.refs_3_, bf16[512,256]{1,0:T(8,128)(2,1)S(1)} %collective-permute-done.5.refs_4_, ...), custom_call_target="tpu_custom_call" | custom-call | flops 5637144576 | bytes 16777216 | tf_op jit(solution)/shard_map/pallas_call | solution.py:146
  (5 shorter events, 0.1 us)
Async XLA Ops:
  0.0 46.5 %copy-start.3 = (bf16[512,1024]{1,0:T(8,128)(2,1)S(1)}, bf16[512,1024]{1,0:T(8,128)(2,1)}, u32[]{:S(2)}) copy-start(bf16[512,1024]{1,0:T(8,128)(2,1)} %q_ref.7) | copy-start | bytes 3145732
  0.0 53.5 %collective-permute-start.6 = (bf16[1024,5376]{1,0:T(8,128)(2,1)}, bf16[1024,5376]{1,0:T(8,128)(2,1)}, u32[]{:S(2)}, u32[]{:S(2)}) collective-permute-start(bf16[1024,5376]{1,0:T(8,128)(2,1)} %refs_5_.3), channel_id=1, source_target_pairs={{0,1},{1,0},{2,3},{3,2},{4,5},{5,4},{6,7},{7,6},{8,9},{9,8},{10,11... | collective-permute-start | bytes 33030152 | tf_op jit(solution)/shard_map/ppermute | solution.py:186
  1.8 11.6 %copy-start.4 = (bf16[512,128]{1,0:T(8,128)(2,1)}, bf16[512,128]{1,0:T(8,128)(2,1)S(1)}, u32[]{:S(2)}) copy-start(bf16[512,128]{1,0:T(8,128)(2,1)S(1)} %get-tuple-element.5) | copy-start | bytes 393220
  1.9 11.7 %copy-start.5 = (bf16[512,128]{1,0:T(8,128)(2,1)}, bf16[512,128]{1,0:T(8,128)(2,1)S(1)}, u32[]{:S(2)}) copy-start(bf16[512,128]{1,0:T(8,128)(2,1)S(1)} %get-tuple-element.16) | copy-start | bytes 393220
  1.9 15.2 %copy-start.6 = (bf16[512,128]{1,0:T(8,128)(2,1)}, bf16[512,128]{1,0:T(8,128)(2,1)S(1)}, u32[]{:S(2)}) copy-start(bf16[512,128]{1,0:T(8,128)(2,1)S(1)} %get-tuple-element.8) | copy-start | bytes 393220
  1.9 15.2 %copy-start.7 = (bf16[512,128]{1,0:T(8,128)(2,1)}, bf16[512,128]{1,0:T(8,128)(2,1)S(1)}, u32[]{:S(2)}) copy-start(bf16[512,128]{1,0:T(8,128)(2,1)S(1)} %get-tuple-element.13) | copy-start | bytes 393220
  1.9 44.0 %collective-permute-start.3 = (bf16[512,256]{1,0:T(8,128)(2,1)S(1)}, bf16[512,256]{1,0:T(8,128)(2,1)}, u32[]{:S(2)}, u32[]{:S(2)}) collective-permute-start(bf16[512,256]{1,0:T(8,128)(2,1)S(1)} %pad_maximum_fusion.1.own_ref), channel_id=1, source_target_pairs={{0,4},{2,6},{4,8},{6,10},{8,12},{10,14},{1,5},{3,7},{5,9},{7,11},{... | collective-permute-start | bytes 786440 | tf_op jit(solution)/shard_map/ppermute | solution.py:181
  7.2 39.3 %collective-permute-start.2 = (bf16[512,256]{1,0:T(8,128)(2,1)S(1)}, bf16[512,256]{1,0:T(8,128)(2,1)}, u32[]{:S(2)}, u32[]{:S(2)}) collective-permute-start(bf16[512,256]{1,0:T(8,128)(2,1)S(1)} %pad_maximum_fusion.1.own_ref), channel_id=1, source_target_pairs={{0,2},{2,4},{4,6},{6,8},{8,10},{10,12},{12,14},{1,3},{3,5},{5,7},{... | collective-permute-start | bytes 786440 | tf_op jit(solution)/shard_map/ppermute | solution.py:185
  11.3 8.8 %collective-permute-start.7 = (bf16[512,256]{1,0:T(8,128)(2,1)S(1)}, bf16[512,256]{1,0:T(8,128)(2,1)S(1)}, u32[]{:S(2)}, u32[]{:S(2)}) collective-permute-start(bf16[512,256]{1,0:T(8,128)(2,1)S(1)} %pad_maximum_fusion.2.own_ref), channel_id=1, source_target_pairs={{0,4},{2,6},{4,8},{6,10},{8,12},{10,14},{1,5},{3,7},{5,9},{7,11},{... | collective-permute-start | bytes 786440 | tf_op jit(solution)/shard_map/ppermute | solution.py:181
  13.5 12.2 %collective-permute-start.9 = (bf16[512,256]{1,0:T(8,128)(2,1)S(1)}, bf16[512,256]{1,0:T(8,128)(2,1)S(1)}, u32[]{:S(2)}, u32[]{:S(2)}) collective-permute-start(bf16[512,256]{1,0:T(8,128)(2,1)S(1)} %pad_maximum_fusion.3.own_ref), channel_id=1, source_target_pairs={{0,4},{2,6},{4,8},{6,10},{8,12},{10,14},{1,5},{3,7},{5,9},{7,11},{... | collective-permute-start | bytes 786440 | tf_op jit(solution)/shard_map/ppermute | solution.py:181
  20.2 12.4 %collective-permute-start = (bf16[512,256]{1,0:T(8,128)(2,1)S(1)}, bf16[512,256]{1,0:T(8,128)(2,1)S(1)}, u32[]{:S(2)}, u32[]{:S(2)}) collective-permute-start(bf16[512,256]{1,0:T(8,128)(2,1)S(1)} %pad_maximum_fusion.own_ref), channel_id=1, source_target_pairs={{0,4},{2,6},{4,8},{6,10},{8,12},{10,14},{1,5},{3,7},{5,9},{7,11},{... | collective-permute-start | bytes 786440 | tf_op jit(solution)/shard_map/ppermute | solution.py:181
  25.8 11.6 %collective-permute-start.8 = (bf16[512,256]{1,0:T(8,128)(2,1)S(1)}, bf16[512,256]{1,0:T(8,128)(2,1)S(1)}, u32[]{:S(2)}, u32[]{:S(2)}) collective-permute-start(bf16[512,256]{1,0:T(8,128)(2,1)S(1)} %broadcast_select_fusion.1), channel_id=1, source_target_pairs={{0,2},{2,0},{4,6},{6,4},{8,10},{10,8},{12,14},{14,12},{1,3},{3,1},... | collective-permute-start | bytes 786440 | tf_op jit(solution)/shard_map/ppermute | solution.py:183
  32.5 11.3 %collective-permute-start.10 = (bf16[512,256]{1,0:T(8,128)(2,1)S(1)}, bf16[512,256]{1,0:T(8,128)(2,1)S(1)}, u32[]{:S(2)}, u32[]{:S(2)}) collective-permute-start(bf16[512,256]{1,0:T(8,128)(2,1)S(1)} %broadcast_select_fusion), channel_id=1, source_target_pairs={{0,2},{2,0},{4,6},{6,4},{8,10},{10,8},{12,14},{14,12},{1,3},{3,1},... | collective-permute-start | bytes 786440 | tf_op jit(solution)/shard_map/ppermute | solution.py:183
  37.4 12.5 %collective-permute-start.1 = (bf16[512,256]{1,0:T(8,128)(2,1)}, bf16[512,256]{1,0:T(8,128)(2,1)}, u32[]{:S(2)}, u32[]{:S(2)}) collective-permute-start(bf16[512,256]{1,0:T(8,128)(2,1)} %broadcast_select_fusion.2), channel_id=1, source_target_pairs={{0,2},{2,0},{4,6},{6,4},{8,10},{10,8},{12,14},{14,12},{1,3},{3,1},... | collective-permute-start | bytes 786440 | tf_op jit(solution)/shard_map/ppermute | solution.py:183
  38.9 1.2 %copy-start.2 = (bf16[512,1024]{1,0:T(8,128)(2,1)S(1)}, bf16[512,1024]{1,0:T(8,128)(2,1)}, u32[]{:S(2)}) copy-start(bf16[512,1024]{1,0:T(8,128)(2,1)} %q_ref.7) | copy-start | bytes 3145732
  43.8 9.7 %collective-permute-start.11 = (bf16[512,256]{1,0:T(8,128)(2,1)S(1)}, bf16[512,256]{1,0:T(8,128)(2,1)S(1)}, u32[]{:S(2)}, u32[]{:S(2)}) collective-permute-start(bf16[512,256]{1,0:T(8,128)(2,1)S(1)} %shard_map.57.refs_1_), channel_id=1, source_target_pairs={{0,1},{1,0},{2,3},{3,2},{4,5},{5,4},{6,7},{7,6},{8,9},{9,8},{10,11... | collective-permute-start | bytes 786440 | tf_op jit(solution)/shard_map/ppermute | solution.py:197
  45.9 7.6 %collective-permute-start.12 = (bf16[512,256]{1,0:T(8,128)(2,1)S(1)}, bf16[512,256]{1,0:T(8,128)(2,1)S(1)}, u32[]{:S(2)}, u32[]{:S(2)}) collective-permute-start(bf16[512,256]{1,0:T(8,128)(2,1)S(1)} %shard_map.58.refs_2_), channel_id=1, source_target_pairs={{0,1},{1,0},{2,3},{3,2},{4,5},{5,4},{6,7},{7,6},{8,9},{9,8},{10,11... | collective-permute-start | bytes 786440 | tf_op jit(solution)/shard_map/ppermute | solution.py:197
  46.5 24.6 %slice-start = ((s8[11010048]{0:T(1024)(128)(4,1)}), s8[4194304]{0:T(1024)(128)(4,1)S(1)}, s32[]{:S(2)}) async-start(s8[11010048]{0:T(1024)(128)(4,1)} %bitcast.1), calls=%async_computation | async-start | bytes 8388608
  49.8 21.3 %collective-permute-start.5 = (bf16[512,256]{1,0:T(8,128)(2,1)S(1)}, bf16[512,256]{1,0:T(8,128)(2,1)S(1)}, u32[]{:S(2)}, u32[]{:S(2)}) collective-permute-start(bf16[512,256]{1,0:T(8,128)(2,1)S(1)} %shard_map.56.refs_2_), channel_id=1, source_target_pairs={{0,1},{1,0},{2,3},{3,2},{4,5},{5,4},{6,7},{7,6},{8,9},{9,8},{10,11... | collective-permute-start | bytes 786440 | tf_op jit(solution)/shard_map/ppermute | solution.py:197
  52.9 18.2 %collective-permute-start.4 = (bf16[512,256]{1,0:T(8,128)(2,1)S(1)}, bf16[512,256]{1,0:T(8,128)(2,1)S(1)}, u32[]{:S(2)}, u32[]{:S(2)}) collective-permute-start(bf16[512,256]{1,0:T(8,128)(2,1)S(1)} %shard_map.55.refs_1_), channel_id=1, source_target_pairs={{0,1},{1,0},{2,3},{3,2},{4,5},{5,4},{6,7},{7,6},{8,9},{9,8},{10,11... | collective-permute-start | bytes 786440 | tf_op jit(solution)/shard_map/ppermute | solution.py:197
  53.5 4.1 %copy-start = (bf16[1024,5376]{1,0:T(8,128)(2,1)S(1)}, bf16[1024,5376]{1,0:T(8,128)(2,1)}, u32[]{:S(2)}) copy-start(bf16[1024,5376]{1,0:T(8,128)(2,1)} %refs_5_.3) | copy-start | bytes 33030148
  57.6 13.5 %slice-start.1 = ((s8[11010048]{0:T(1024)(128)(4,1)}), s8[4194304]{0:T(1024)(128)(4,1)S(1)}, s32[]{:S(2)}) async-start(s8[11010048]{0:T(1024)(128)(4,1)} %bitcast.1), calls=%async_computation.1 | async-start | bytes 8388608
  57.6 13.5 %slice-start.2 = ((s8[11010048]{0:T(1024)(128)(4,1)}), s8[2621440]{0:T(1024)(128)(4,1)S(1)}, s32[]{:S(2)}) async-start(s8[11010048]{0:T(1024)(128)(4,1)} %bitcast.1), calls=%async_computation.2 | async-start | bytes 5242880
  67.0 4.1 %copy-start.1 = (f32[512,5376]{1,0:T(8,128)}, f32[512,5376]{1,0:T(8,128)S(1)}, u32[]{:S(2)}) copy-start(f32[512,5376]{1,0:T(8,128)S(1)} %shard_map.59.refs_7_) | copy-start | bytes 33030148

commit v2 on v1

v2 whole, which is shorter than its diff:
```python
import jax
import jax.numpy as jnp
from jax import lax
from jax.experimental import pallas as pl
from jax.experimental.pallas import tpu as pltpu
from jax.sharding import PartitionSpec as P

HEAD_SIZE = 128
SCALAR = 168
ATTENTION_SPAN = 1024
TILE = 128
MARK = 128.0
LOG2E = 1.4426950408889634
MIB = 1 << 20


def joined(*parts):
    parts = [part for part in parts if part.shape[1]]
    return parts[0] if len(parts) == 1 else jnp.concatenate(parts, axis=1)


def attend_kernel(q_ref, own_ref, near_ref, far_ref, mark_ref, out_ref):
    rows = own_ref.shape[0]
    group = q_ref.shape[1] // HEAD_SIZE
    factor = LOG2E * SCALAR ** (-0.5)
    ones = jnp.ones((rows, HEAD_SIZE), jnp.bfloat16)

    def keys_of(ref, block):
        marks = mark_ref[block * rows : (block + 1) * rows, :]
        return jnp.concatenate([ref[:, :HEAD_SIZE], marks], axis=1)

    def values_of(ref):
        return jnp.concatenate([ref[:, HEAD_SIZE:], ones], axis=1)

    keys = [keys_of(far_ref, 0), keys_of(near_ref, 1), keys_of(own_ref, 2)]
    values = [values_of(far_ref), values_of(near_ref), values_of(own_ref)]
    row = lax.broadcasted_iota(jnp.int32, (TILE, TILE), 0)
    col = lax.broadcasted_iota(jnp.int32, (TILE, TILE), 1)
    inside = jnp.concatenate([col > row] * group, axis=0)
    causal = jnp.concatenate([col <= row] * group, axis=0)
    for t in range(rows // TILE):
        span = slice(t * TILE, (t + 1) * TILE)
        marks = mark_ref[2 * rows + t * TILE : 2 * rows + (t + 1) * TILE, :]
        query = jnp.concatenate(
            [
                jnp.concatenate([q_ref[span, g * HEAD_SIZE : (g + 1) * HEAD_SIZE], marks], axis=1)
                for g in range(group)
            ],
            axis=0,
        )
        parts = [
            (keys[0][t * TILE :], values[0][t * TILE :]),
            (keys[1], values[1]),
            (keys[2][: (t + 1) * TILE], values[2][: (t + 1) * TILE]),
        ]
        scores = [
            lax.dot_general(
                query, key, (((1,), (1,)), ((), ())), preferred_element_type=jnp.float32
            )
            for key, _ in parts
        ]
        first = jnp.where(inside, scores[0][:, :TILE], -1e30)
        scores[0] = joined(first, *([scores[0][:, TILE:]] if scores[0].shape[1] > TILE else []))
        last = jnp.where(causal, scores[2][:, t * TILE :], -1e30)
        scores[2] = joined(*([scores[2][:, : t * TILE]] if t else []), last)
        top = jnp.maximum(
            jnp.maximum(
                jnp.max(scores[0], axis=1, keepdims=True),
                jnp.max(scores[1], axis=1, keepdims=True),
            ),
            jnp.max(scores[2], axis=1, keepdims=True),
        )
        total = None
        for score, (_, value) in zip(scores, parts):
            weight = jnp.exp2((score - top) * factor).astype(jnp.bfloat16)
            term = jnp.dot(weight, value, preferred_element_type=jnp.float32)
            total = term if total is None else total + term
        result = (total[:, :HEAD_SIZE] / total[:, HEAD_SIZE:]).astype(jnp.bfloat16)
        for g in range(group):
            out_ref[span, g * HEAD_SIZE : (g + 1) * HEAD_SIZE] = result[
                g * TILE : (g + 1) * TILE
            ]


def in_vmem(x):
    return pltpu.with_memory_space_constraint(x, pltpu.VMEM)


def in_hbm(x):
    return pltpu.with_memory_space_constraint(x, pltpu.HBM)


def pack_kernel(keys_ref, values_ref, *refs):
    outs, sem = refs[:-1], refs[-1]
    copies = []
    for h, out in enumerate(outs):
        for side, ref in enumerate((keys_ref, values_ref)):
            copies.append(
                pltpu.make_async_copy(
                    ref.at[:, h * HEAD_SIZE : (h + 1) * HEAD_SIZE],
                    out.at[:, side * HEAD_SIZE : (side + 1) * HEAD_SIZE],
                    sem.at[h, side],
                )
            )
    for copy in copies:
        copy.start()
    for copy in copies:
        copy.wait()


def pack(keys, values):
    rows, heads = keys.shape[0], keys.shape[1] // HEAD_SIZE
    return pl.pallas_call(
        pack_kernel,
        in_specs=[pl.BlockSpec(memory_space=pltpu.HBM)] * 2,
        out_specs=[pl.BlockSpec(memory_space=pltpu.VMEM)] * heads,
        out_shape=[pltpu.VMEM((rows, 2 * HEAD_SIZE), jnp.bfloat16)] * heads,
        scratch_shapes=[pltpu.SemaphoreType.DMA((heads, 2))],
        compiler_params=pltpu.CompilerParams(vmem_limit_bytes=2 * MIB),
        cost_estimate=pl.CostEstimate(flops=0, bytes_accessed=2 * MIB, transcendentals=0),
    )(in_hbm(keys), in_hbm(values))


def attend(queries, marks, first, parts):
    rows = marks.shape[0] // 3
    count = len(parts)
    width = 2 * HEAD_SIZE

    def kernel(q_ref, mark_ref, *refs):
        out_ref = refs[-1]
        for i in range(count):
            left = (first + i) * width
            attend_kernel(
                q_ref.at[:, left : left + width],
                *refs[3 * i : 3 * i + 3],
                mark_ref,
                out_ref.at[:, i * width : (i + 1) * width],
            )

    flat = [in_vmem(x) for part in parts for x in part]
    return pl.pallas_call(
        kernel,
        in_specs=[pl.BlockSpec(memory_space=pltpu.VMEM)] * (2 + len(flat)),
        out_specs=pl.BlockSpec(memory_space=pltpu.VMEM),
        out_shape=pltpu.VMEM((rows, count * width), jnp.bfloat16),
        compiler_params=pltpu.CompilerParams(vmem_limit_bytes=8 * MIB),
        cost_estimate=pl.CostEstimate(
            flops=count * 4 * 1024 * 1152 * 256,
            bytes_accessed=2 * MIB,
            transcendentals=count * 1024 * 1152,
        ),
    )(queries, marks, *flat)


def project(core, own, other, own_w, other_w):
    count = len(own)
    rows = own[0].shape[0]
    depth, columns = own_w.shape
    tile = 768 if columns % 768 == 0 else 128
    tiles = columns // tile

    def kernel(core_ref, *refs):
        own_refs, other_refs = refs[:count], refs[count : 2 * count]
        own_w_ref, other_w_ref, out_ref, both, w_buf, w_sem, held, out_sem = refs[2 * count :]
        mine = pl.multiple_of(core_ref[0] * depth, depth)
        theirs = pl.multiple_of((1 - core_ref[0]) * depth, depth)

        def place(n):
            return pl.ds(pl.multiple_of(n * tile, tile), tile)

        def fetch(n):
            return [
                pltpu.make_async_copy(
                    ref.at[:, place(n)], w_buf.at[n, pl.ds(start, depth), :], w_sem.at[n, i]
                )
                for i, (ref, start) in enumerate(((own_w_ref, mine), (other_w_ref, theirs)))
            ]

        def give(n):
            return pltpu.make_async_copy(
                held.at[:, place(n)], out_ref.at[:, place(n)], out_sem.at[n]
            )

        for n in range(tiles):
            for copy in fetch(n):
                copy.start()
        for group, start in ((own_refs, mine), (other_refs, theirs)):
            at = 0
            for ref in group:
                width = ref.shape[1]
                both[:, pl.ds(pl.multiple_of(start + at, 128), width)] = ref[...]
                at += width

        @pl.loop(0, tiles)
        def _(n):
            for copy in fetch(n):
                copy.wait()
            total = jnp.dot(both[...], w_buf[n], preferred_element_type=jnp.float32)
            held[:, place(n)] = total.astype(held.dtype)
            give(n).start()

        @pl.loop(0, tiles)
        def _(n):
            give(n).wait()

    vmem = pl.BlockSpec(memory_space=pltpu.VMEM)
    hbm = pl.BlockSpec(memory_space=pltpu.HBM)
    return pl.pallas_call(
        kernel,
        in_specs=[pl.BlockSpec(memory_space=pltpu.SMEM)] + [vmem] * (2 * count) + [hbm] * 2,
        out_specs=pl.BlockSpec(memory_space=pl.ANY),
        out_shape=jax.ShapeDtypeStruct((rows, columns), jnp.bfloat16),
        scratch_shapes=[
            pltpu.VMEM((rows, 2 * depth), jnp.bfloat16),
            pltpu.VMEM((tiles, 2 * depth, tile), jnp.bfloat16),
            pltpu.SemaphoreType.DMA((tiles, 2)),
            pltpu.VMEM((rows, columns), jnp.bfloat16),
            pltpu.SemaphoreType.DMA((tiles,)),
        ],
        compiler_params=pltpu.CompilerParams(vmem_limit_bytes=40 * MIB),
        cost_estimate=pl.CostEstimate(
            flops=4 * rows * depth * columns, bytes_accessed=32 * MIB, transcendentals=0
        ),
    )(core, *[in_vmem(x) for x in own + other], in_hbm(own_w), in_hbm(other_w))


def shards(queries, keys, values, segments, out_weight):
    rows = queries.shape[0]
    heads_kv = keys.shape[1] // HEAD_SIZE
    peers = lax.axis_size("seq")
    seq_index = lax.axis_index("seq")
    core = lax.axis_index("head").astype(jnp.int32).reshape(1)
    swap = [(0, 1), (1, 0)]

    other_w = lax.ppermute(out_weight, "head", swap)
    own = pack(keys, values)
    two_on = [(i, i + 2) for i in range(peers - 2)]
    pair = [(i, i ^ 1) for i in range(peers)]
    odd = seq_index % 2 == 1
    far = [lax.ppermute(x, "seq", two_on) for x in own[:-1]]
    near = [lax.ppermute(jnp.where(odd, f, x), "seq", pair) for f, x in zip(far, own)]
    beside = lax.ppermute(own[-1], "seq", pair)
    last, far[0] = lax.optimization_barrier((jnp.concatenate([own[-1], beside]), far[0]))
    last = lax.ppermute(last, "seq", two_on)
    far.append(last[:rows])
    near.append(jnp.where(odd, beside, last[rows:]))

    halo = 2 * rows
    padded = jnp.concatenate([jnp.full((halo,), -1, jnp.int32), segments])
    seen = lax.dynamic_slice_in_dim(padded, seq_index * rows, halo + rows, 0)
    ids = lax.broadcasted_iota(jnp.int32, (halo + rows, HEAD_SIZE), 1)
    marks = in_vmem(jnp.where(seen[:, None] == ids, MARK, 0.0).astype(jnp.bfloat16))
    queries = in_vmem(queries)

    steps = [[h] for h in range(heads_kv - 2)] + [[heads_kv - 2, heads_kv - 1]]
    mine = [
        attend(queries, marks, step[0], [(own[h], near[h], far[h]) for h in step])
        for step in steps
    ]
    theirs = [lax.ppermute(x, "head", swap) for x in mine]
    return project(core, mine, theirs, out_weight, other_w)


def solution(mesh):
    placed = (
        P(("groups", "seq"), "head"),
        P(("groups", "seq"), "head"),
        P(("groups", "seq"), "head"),
        P("groups"),
        P("head", None),
    )
    return jax.shard_map(
        shards, mesh=mesh, in_specs=placed, out_specs=P(("groups", "seq"), None), check_vma=False
    )
```

time: 84.6 us -> 62.1 us (0.73)
  starting transfers between devices: 32.3 us -> 20.3 us
  waiting for transfers between devices: 3.78 us -> 14.3 us
  local copies, waits for them, and re-layouts: 11.6 us -> 2 us
  Pallas kernels: 32.5 us -> 24.6 us
  other arithmetic: 3.24 us -> 0.44 us
    ppermute x5, waiting for transfers between devices: 2.17 us -> 12.8 us  [the longest x1 8.63 us: shards(): last = lax.ppermute(last, 'seq', two_on)]
    unnamed x22 -> x2, local copies, waits for them, and re-layouts: 9.44 us -> 1.22 us
    pallas_call x6 -> x5, Pallas kernels: 32.5 us -> 24.6 us  [the longest x1 15.6 us: project(): pl.pallas_call(kernel, in_specs=[pl.BlockSpec(memory_space=pltpu.SMEM)] +...]
    ppermute x3, starting transfers between devices: 11.3 us -> 3.74 us  [shards(): lax.ppermute(jnp.where(odd, f, x), 'seq', pair)]
    ppermute x5, starting transfers between devices: 19.4 us -> 15.4 us  [the longest x3 11.5 us: shards(): far = [lax.ppermute(x, 'seq', two_on) for x in own[:-1]]]
    select_n x3, other arithmetic: 2.85 us -> 0.09 us  [shards(): jnp.where(odd, f, x)]
    ppermute x3, waiting for transfers between devices: 1.6 us -> 0.01 us  [shards(): lax.ppermute(jnp.where(odd, f, x), 'seq', pair)]
    ppermute x4 -> x3, waiting for transfers between devices: 0.01 us -> 1.51 us  [shards(): theirs = [lax.ppermute(x, 'head', swap) for x in mine]]
  transfers between devices with their start and end apart: 13 -> 12, of which waited for: 3 -> 3; matrix products, arithmetic and copies ran while one was open for 6% -> 2% of each run, Pallas kernels for 24% -> 15%
where the time goes in v2:
time: 62.1 us; the launch traced here: 61.8 us
  Pallas kernels  24.6 us (40%)
  starting transfers between devices  20.3 us (33%)
  waiting for transfers between devices  14.3 us (23%)
  local copies, waits for them, and re-layouts  2 us (3%)
    pallas_call x1, Pallas kernels, project(): pl.pallas_call(kernel, in_specs=[pl.BlockSpec(memory_space=pltpu.SMEM)] +...  15.6 us
    ppermute x3, starting transfers between devices, shards(): far = [lax.ppermute(x, 'seq', two_on) for x in own[:-1]]  11.5 us
    ppermute x1, waiting for transfers between devices, shards(): last = lax.ppermute(last, 'seq', two_on)  8.63 us
    pallas_call x3, Pallas kernels, attend(): pl.pallas_call(kernel, in_specs=[pl.BlockSpec(memory_space=pltpu.VMEM)] *...  7.7 us
    ppermute x3, waiting for transfers between devices, shards(): far = [lax.ppermute(x, 'seq', two_on) for x in own[:-1]]  4.14 us
    ppermute x3, starting transfers between devices, shards(): lax.ppermute(jnp.where(odd, f, x), 'seq', pair)  3.74 us
    ppermute x1, starting transfers between devices, shards(): last = lax.ppermute(last, 'seq', two_on)  2.36 us
    ppermute x1, starting transfers between devices, shards(): beside = lax.ppermute(own[-1], 'seq', pair)  1.58 us
  transfers between devices with their start and end apart: 12, of which 3 were waited for; matrix products, arithmetic and copies ran while one was open for 2% of the time, Pallas kernels for 15%

profile of v2, /device:TPU:0, one launch (start us, length us, event | category | flops | bytes accessed | tf_op | source)
XLA Modules:
  0.0 61.8 jit_solution(9256081503962992282)
XLA Ops:
  0.0 0.5 collective-permute-start.11
  0.5 1.4 %shard_map.55 = (bf16[512,256]{1,0:T(8,128)(2,1)S(1)}, bf16[512,256]{1,0:T(8,128)(2,1)S(1)}, bf16[512,256]{1,0:T(8,128)(2,1)S(1)}, bf16[512,256]{1,0:T(8,128)(2,1)S(1)}) custom-call(bf16[512,512]{1,0:T(8,128)(2,1)} %keys_ref.1, bf16[512,512]{1,0:T(8,128)(2,1)} %values_ref.1), custom_call_target="tpu_custom_call" | custom-call | bytes 2097152 | tf_op jit(solution)/shard_map/pallas_call | solution.py:113
  1.8 4.5 %collective-permute-start = (bf16[512,256]{1,0:T(8,128)(2,1)S(1)}, bf16[512,256]{1,0:T(8,128)(2,1)S(1)}, u32[]{:S(2)}, u32[]{:S(2)}) collective-permute-start(bf16[512,256]{1,0:T(8,128)(2,1)S(1)} %get-tuple-element.11.refs_0_), channel_id=1, source_target_pairs={{0,4},{2,6},{4,8},{6,10},{8,12},{10,14},{1,5},{3,7},{5,9},{7,11},{... | collective-permute-start | bytes 786440 | tf_op jit(solution)/shard_map/ppermute | solution.py:240
  6.3 1.6 %collective-permute-start.2 = (bf16[512,256]{1,0:T(8,128)(2,1)S(1)}, bf16[512,256]{1,0:T(8,128)(2,1)S(1)}, u32[]{:S(2)}, u32[]{:S(2)}) collective-permute-start(bf16[512,256]{1,0:T(8,128)(2,1)S(1)} %get-tuple-element.12.refs_3_), channel_id=1, source_target_pairs={{0,2},{2,0},{4,6},{6,4},{8,10},{10,8},{12,14},{14,12},{1,3},{3,1},... | collective-permute-start | bytes 786440 | tf_op jit(solution)/shard_map/ppermute | solution.py:242
  7.9 3.5 %collective-permute-start.3 = (bf16[512,256]{1,0:T(8,128)(2,1)S(1)}, bf16[512,256]{1,0:T(8,128)(2,1)S(1)}, u32[]{:S(2)}, u32[]{:S(2)}) collective-permute-start(bf16[512,256]{1,0:T(8,128)(2,1)S(1)} %get-tuple-element.14.refs_0_), channel_id=1, source_target_pairs={{0,4},{2,6},{4,8},{6,10},{8,12},{10,14},{1,5},{3,7},{5,9},{7,11},{... | collective-permute-start | bytes 786440 | tf_op jit(solution)/shard_map/ppermute | solution.py:240
  11.4 3.5 %collective-permute-start.5 = (bf16[512,256]{1,0:T(8,128)(2,1)S(1)}, bf16[512,256]{1,0:T(8,128)(2,1)S(1)}, u32[]{:S(2)}, u32[]{:S(2)}) collective-permute-start(bf16[512,256]{1,0:T(8,128)(2,1)S(1)} %get-tuple-element.15.refs_0_), channel_id=1, source_target_pairs={{0,4},{2,6},{4,8},{6,10},{8,12},{10,14},{1,5},{3,7},{5,9},{7,11},{... | collective-permute-start | bytes 786440 | tf_op jit(solution)/shard_map/ppermute | solution.py:240
  14.9 0.8 %pad_dynamic-slice_fusion = s32[1536]{0:T(1024)S(1)} fusion(s32[]{:T(128)S(6)} %select_n.36, s32[4096]{0:T(1024)} %param.8), kind=kLoop, calls=%fused_computation.7 | loop fusion | bytes 22532 | tf_op jit(solution)/shard_map/dynamic_slice | solution.py:250
  15.7 0.3 select_convert_fusion.mark_ref
  16.0 0.0 collective-permute-done.2
  16.0 0.0 collective-permute-done.refs_2_
  16.0 2.4 %collective-permute-start.7 = (bf16[1024,256]{1,0:T(8,128)(2,1)S(1)}, bf16[1024,256]{1,0:T(8,128)(2,1)S(1)}, u32[]{:S(2)}, u32[]{:S(2)}) collective-permute-start(bf16[1024,256]{1,0:T(8,128)(2,1)S(1)} %pad_maximum_fusion), channel_id=1, source_target_pairs={{0,4},{2,6},{4,8},{6,10},{8,12},{10,14},{1,5},{3,7},{5,9},{7,11},{... | collective-permute-start | bytes 1572872 | tf_op jit(solution)/shard_map/ppermute | solution.py:244
  18.4 1.6 %collective-permute-start.1 = (bf16[512,256]{1,0:T(8,128)(2,1)S(1)}, bf16[512,256]{1,0:T(8,128)(2,1)S(1)}, u32[]{:S(2)}, u32[]{:S(2)}) collective-permute-start(bf16[512,256]{1,0:T(8,128)(2,1)S(1)} %broadcast_select_fusion.2), channel_id=1, source_target_pairs={{0,2},{2,0},{4,6},{6,4},{8,10},{10,8},{12,14},{14,12},{1,3},{3,1},... | collective-permute-start | bytes 786440 | tf_op jit(solution)/shard_map/ppermute | solution.py:241
  20.0 4.1 %collective-permute-done.5.refs_2_ = bf16[512,256]{1,0:T(8,128)(2,1)S(1)} collective-permute-done((bf16[512,256]{1,0:T(8,128)(2,1)S(1)}, bf16[512,256]{1,0:T(8,128)(2,1)S(1)}, u32[]{:S(2)}, u32[]{:S(2)}) %collective-permute-start.5) | collective-permute-done | bytes 262176 | tf_op jit(solution)/shard_map/ppermute | solution.py:240
  24.2 1.6 %collective-permute-start.6 = (bf16[512,256]{1,0:T(8,128)(2,1)S(1)}, bf16[512,256]{1,0:T(8,128)(2,1)S(1)}, u32[]{:S(2)}, u32[]{:S(2)}) collective-permute-start(bf16[512,256]{1,0:T(8,128)(2,1)S(1)} %broadcast_select_fusion), channel_id=1, source_target_pairs={{0,2},{2,0},{4,6},{6,4},{8,10},{10,8},{12,14},{14,12},{1,3},{3,1},... | collective-permute-start | bytes 786440 | tf_op jit(solution)/shard_map/ppermute | solution.py:241
  25.8 0.0 collective-permute-done.3.refs_2_
  25.8 0.6 collective-permute-start.4
  26.4 8.6 %collective-permute-done.7 = bf16[1024,256]{1,0:T(8,128)(2,1)S(1)} collective-permute-done((bf16[1024,256]{1,0:T(8,128)(2,1)S(1)}, bf16[1024,256]{1,0:T(8,128)(2,1)S(1)}, u32[]{:S(2)}, u32[]{:S(2)}) %collective-permute-start.7) | collective-permute-done | bytes 524320 | tf_op jit(solution)/shard_map/ppermute | solution.py:244
  35.1 0.0 collective-permute-done.6.refs_1_
  35.1 0.0 copy-start
  35.1 1.2 %copy-done = bf16[512,1024]{1,0:T(8,128)(2,1)S(1)} copy-done((bf16[512,1024]{1,0:T(8,128)(2,1)S(1)}, bf16[512,1024]{1,0:T(8,128)(2,1)}, u32[]{:S(2)}) %copy-start) | copy-done | bytes 1048600
  36.3 3.5 %shard_map.58.refs_2_ = bf16[512,512]{1,0:T(8,128)(2,1)S(1)} custom-call(bf16[512,1024]{1,0:T(8,128)(2,1)S(1)} %copy-done, bf16[1536,128]{1,0:T(8,128)(2,1)S(1)} %select_convert_fusion.mark_ref, bf16[512,256]{1,0:T(8,128)(2,1)S(1)} %get-tuple-element.15.refs_0_, bf16[512,256]{1,0:T(8,128)(2,1)S(1)} %collective-permute-done.6.refs_1_, ...), custom_call_target="tpu_custom_call" | custom-call | flops 2415919104 | bytes 2097152 | tf_op jit(solution)/shard_map/pallas_call | solution.py:141
  39.9 0.1 collective-permute-start.10
  39.9 0.0 collective-permute-done.4.refs_1_
  39.9 2.1 %shard_map.57.refs_1_ = bf16[512,256]{1,0:T(8,128)(2,1)S(1)} custom-call(bf16[512,1024]{1,0:T(8,128)(2,1)S(1)} %copy-done, bf16[1536,128]{1,0:T(8,128)(2,1)S(1)} %select_convert_fusion.mark_ref, bf16[512,256]{1,0:T(8,128)(2,1)S(1)} %get-tuple-element.14.refs_0_, bf16[512,256]{1,0:T(8,128)(2,1)S(1)} %collective-permute-done.4.refs_1_, ...), custom_call_target="tpu_custom_call" | custom-call | flops 1207959552 | bytes 2097152 | tf_op jit(solution)/shard_map/pallas_call | solution.py:141
  42.0 0.6 collective-permute-start.9
  42.6 0.0 collective-permute-done.1.refs_1_
  42.6 2.1 %shard_map.56.refs_0_ = bf16[512,256]{1,0:T(8,128)(2,1)S(1)} custom-call(bf16[512,1024]{1,0:T(8,128)(2,1)S(1)} %copy-done, bf16[1536,128]{1,0:T(8,128)(2,1)S(1)} %select_convert_fusion.mark_ref, bf16[512,256]{1,0:T(8,128)(2,1)S(1)} %get-tuple-element.11.refs_0_, bf16[512,256]{1,0:T(8,128)(2,1)S(1)} %collective-permute-done.1.refs_1_, ...), custom_call_target="tpu_custom_call" | custom-call | flops 1207959552 | bytes 2097152 | tf_op jit(solution)/shard_map/pallas_call | solution.py:141
  44.7 0.1 collective-permute-start.8
  44.8 0.0 collective-permute-done.9.refs_4_
  44.8 1.5 %collective-permute-done.8.refs_3_ = bf16[512,256]{1,0:T(8,128)(2,1)S(1)} collective-permute-done((bf16[512,256]{1,0:T(8,128)(2,1)S(1)}, bf16[512,256]{1,0:T(8,128)(2,1)S(1)}, u32[]{:S(2)}, u32[]{:S(2)}) %collective-permute-start.8) | collective-permute-done | bytes 262176 | tf_op jit(solution)/shard_map/ppermute | solution.py:260
  46.3 0.0 collective-permute-done.10.refs_5_
  46.3 0.0 collective-permute-done.11.refs_7_
  46.3 15.6 %shard_map.59 = bf16[512,5376]{1,0:T(8,128)(2,1)} custom-call(s32[1]{0:T(128)} %bitcast.core_ref, bf16[512,256]{1,0:T(8,128)(2,1)S(1)} %shard_map.56.refs_0_, bf16[512,256]{1,0:T(8,128)(2,1)S(1)} %shard_map.57.refs_1_, bf16[512,512]{1,0:T(8,128)(2,1)S(1)} %shard_map.58.refs_2_, bf16[512,256]{1,0:T(8,128)(2,1)S(1)} %collective-permute-done.8.refs_3_, ...), custom_call_target="tpu_custom_call" | custom-call | flops 11274289152 | bytes 33554432 | tf_op jit(solution)/shard_map/pallas_call | solution.py:208
  (5 shorter events, 0.2 us)
Async XLA Ops:
  0.0 46.3 %collective-permute-start.11 = (bf16[1024,5376]{1,0:T(8,128)(2,1)}, bf16[1024,5376]{1,0:T(8,128)(2,1)}, u32[]{:S(2)}, u32[]{:S(2)}) collective-permute-start(bf16[1024,5376]{1,0:T(8,128)(2,1)} %refs_6_.1), channel_id=1, source_target_pairs={{0,1},{1,0},{2,3},{3,2},{4,5},{5,4},{6,7},{7,6},{8,9},{9,8},{10,11... | collective-permute-start | bytes 33030152 | tf_op jit(solution)/shard_map/ppermute | solution.py:235
  1.8 14.2 %collective-permute-start = (bf16[512,256]{1,0:T(8,128)(2,1)S(1)}, bf16[512,256]{1,0:T(8,128)(2,1)S(1)}, u32[]{:S(2)}, u32[]{:S(2)}) collective-permute-start(bf16[512,256]{1,0:T(8,128)(2,1)S(1)} %get-tuple-element.11.refs_0_), channel_id=1, source_target_pairs={{0,4},{2,6},{4,8},{6,10},{8,12},{10,14},{1,5},{3,7},{5,9},{7,11},{... | collective-permute-start | bytes 786440 | tf_op jit(solution)/shard_map/ppermute | solution.py:240
  6.3 9.6 %collective-permute-start.2 = (bf16[512,256]{1,0:T(8,128)(2,1)S(1)}, bf16[512,256]{1,0:T(8,128)(2,1)S(1)}, u32[]{:S(2)}, u32[]{:S(2)}) collective-permute-start(bf16[512,256]{1,0:T(8,128)(2,1)S(1)} %get-tuple-element.12.refs_3_), channel_id=1, source_target_pairs={{0,2},{2,0},{4,6},{6,4},{8,10},{10,8},{12,14},{14,12},{1,3},{3,1},... | collective-permute-start | bytes 786440 | tf_op jit(solution)/shard_map/ppermute | solution.py:242
  7.9 17.9 %collective-permute-start.3 = (bf16[512,256]{1,0:T(8,128)(2,1)S(1)}, bf16[512,256]{1,0:T(8,128)(2,1)S(1)}, u32[]{:S(2)}, u32[]{:S(2)}) collective-permute-start(bf16[512,256]{1,0:T(8,128)(2,1)S(1)} %get-tuple-element.14.refs_0_), channel_id=1, source_target_pairs={{0,4},{2,6},{4,8},{6,10},{8,12},{10,14},{1,5},{3,7},{5,9},{7,11},{... | collective-permute-start | bytes 786440 | tf_op jit(solution)/shard_map/ppermute | solution.py:240
  11.4 12.8 %collective-permute-start.5 = (bf16[512,256]{1,0:T(8,128)(2,1)S(1)}, bf16[512,256]{1,0:T(8,128)(2,1)S(1)}, u32[]{:S(2)}, u32[]{:S(2)}) collective-permute-start(bf16[512,256]{1,0:T(8,128)(2,1)S(1)} %get-tuple-element.15.refs_0_), channel_id=1, source_target_pairs={{0,4},{2,6},{4,8},{6,10},{8,12},{10,14},{1,5},{3,7},{5,9},{7,11},{... | collective-permute-start | bytes 786440 | tf_op jit(solution)/shard_map/ppermute | solution.py:240
  16.0 19.0 %collective-permute-start.7 = (bf16[1024,256]{1,0:T(8,128)(2,1)S(1)}, bf16[1024,256]{1,0:T(8,128)(2,1)S(1)}, u32[]{:S(2)}, u32[]{:S(2)}) collective-permute-start(bf16[1024,256]{1,0:T(8,128)(2,1)S(1)} %pad_maximum_fusion), channel_id=1, source_target_pairs={{0,4},{2,6},{4,8},{6,10},{8,12},{10,14},{1,5},{3,7},{5,9},{7,11},{... | collective-permute-start | bytes 1572872 | tf_op jit(solution)/shard_map/ppermute | solution.py:244
  18.4 24.1 %collective-permute-start.1 = (bf16[512,256]{1,0:T(8,128)(2,1)S(1)}, bf16[512,256]{1,0:T(8,128)(2,1)S(1)}, u32[]{:S(2)}, u32[]{:S(2)}) collective-permute-start(bf16[512,256]{1,0:T(8,128)(2,1)S(1)} %broadcast_select_fusion.2), channel_id=1, source_target_pairs={{0,2},{2,0},{4,6},{6,4},{8,10},{10,8},{12,14},{14,12},{1,3},{3,1},... | collective-permute-start | bytes 786440 | tf_op jit(solution)/shard_map/ppermute | solution.py:241
  24.2 10.9 %collective-permute-start.6 = (bf16[512,256]{1,0:T(8,128)(2,1)S(1)}, bf16[512,256]{1,0:T(8,128)(2,1)S(1)}, u32[]{:S(2)}, u32[]{:S(2)}) collective-permute-start(bf16[512,256]{1,0:T(8,128)(2,1)S(1)} %broadcast_select_fusion), channel_id=1, source_target_pairs={{0,2},{2,0},{4,6},{6,4},{8,10},{10,8},{12,14},{14,12},{1,3},{3,1},... | collective-permute-start | bytes 786440 | tf_op jit(solution)/shard_map/ppermute | solution.py:241
  25.8 14.1 %collective-permute-start.4 = (bf16[512,256]{1,0:T(8,128)(2,1)S(1)}, bf16[512,256]{1,0:T(8,128)(2,1)S(1)}, u32[]{:S(2)}, u32[]{:S(2)}) collective-permute-start(bf16[512,256]{1,0:T(8,128)(2,1)S(1)} %broadcast_select_fusion.1), channel_id=1, source_target_pairs={{0,2},{2,0},{4,6},{6,4},{8,10},{10,8},{12,14},{14,12},{1,3},{3,1},... | collective-permute-start | bytes 786440 | tf_op jit(solution)/shard_map/ppermute | solution.py:241
  35.1 1.2 %copy-start = (bf16[512,1024]{1,0:T(8,128)(2,1)S(1)}, bf16[512,1024]{1,0:T(8,128)(2,1)}, u32[]{:S(2)}) copy-start(bf16[512,1024]{1,0:T(8,128)(2,1)} %q_ref.5) | copy-start | bytes 3145732
  39.9 6.4 %collective-permute-start.10 = (bf16[512,512]{1,0:T(8,128)(2,1)S(1)}, bf16[512,512]{1,0:T(8,128)(2,1)S(1)}, u32[]{:S(2)}, u32[]{:S(2)}) collective-permute-start(bf16[512,512]{1,0:T(8,128)(2,1)S(1)} %shard_map.58.refs_2_), channel_id=1, source_target_pairs={{0,1},{1,0},{2,3},{3,2},{4,5},{5,4},{6,7},{7,6},{8,9},{9,8},{10,11... | collective-permute-start | bytes 1572872 | tf_op jit(solution)/shard_map/ppermute | solution.py:260
  42.0 2.7 %collective-permute-start.9 = (bf16[512,256]{1,0:T(8,128)(2,1)S(1)}, bf16[512,256]{1,0:T(8,128)(2,1)S(1)}, u32[]{:S(2)}, u32[]{:S(2)}) collective-permute-start(bf16[512,256]{1,0:T(8,128)(2,1)S(1)} %shard_map.57.refs_1_), channel_id=1, source_target_pairs={{0,1},{1,0},{2,3},{3,2},{4,5},{5,4},{6,7},{7,6},{8,9},{9,8},{10,11... | collective-permute-start | bytes 786440 | tf_op jit(solution)/shard_map/ppermute | solution.py:260
  44.7 1.6 %collective-permute-start.8 = (bf16[512,256]{1,0:T(8,128)(2,1)S(1)}, bf16[512,256]{1,0:T(8,128)(2,1)S(1)}, u32[]{:S(2)}, u32[]{:S(2)}) collective-permute-start(bf16[512,256]{1,0:T(8,128)(2,1)S(1)} %shard_map.56.refs_0_), channel_id=1, source_target_pairs={{0,1},{1,0},{2,3},{3,2},{4,5},{5,4},{6,7},{7,6},{8,9},{9,8},{10,11... | collective-permute-start | bytes 786440 | tf_op jit(solution)/shard_map/ppermute | solution.py:260

commit v3 on v2

--- a/solution.py
+++ b/solution.py
@@ -121,35 +121,26 @@
     )(in_hbm(keys), in_hbm(values))
 
 
-def attend(queries, marks, first, parts):
+def attend(queries, marks, head, part):
     rows = marks.shape[0] // 3
-    count = len(parts)
     width = 2 * HEAD_SIZE
 
-    def kernel(q_ref, mark_ref, *refs):
-        out_ref = refs[-1]
-        for i in range(count):
-            left = (first + i) * width
-            attend_kernel(
-                q_ref.at[:, left : left + width],
-                *refs[3 * i : 3 * i + 3],
-                mark_ref,
-                out_ref.at[:, i * width : (i + 1) * width],
-            )
-
-    flat = [in_vmem(x) for part in parts for x in part]
+    def kernel(q_ref, mark_ref, own_ref, near_ref, far_ref, out_ref):
+        left = head * width
+        attend_kernel(
+            q_ref.at[:, left : left + width], own_ref, near_ref, far_ref, mark_ref, out_ref
+        )
+
     return pl.pallas_call(
         kernel,
-        in_specs=[pl.BlockSpec(memory_space=pltpu.VMEM)] * (2 + len(flat)),
+        in_specs=[pl.BlockSpec(memory_space=pltpu.VMEM)] * 5,
         out_specs=pl.BlockSpec(memory_space=pltpu.VMEM),
-        out_shape=pltpu.VMEM((rows, count * width), jnp.bfloat16),
+        out_shape=pltpu.VMEM((rows, width), jnp.bfloat16),
         compiler_params=pltpu.CompilerParams(vmem_limit_bytes=8 * MIB),
         cost_estimate=pl.CostEstimate(
-            flops=count * 4 * 1024 * 1152 * 256,
-            bytes_accessed=2 * MIB,
-            transcendentals=count * 1024 * 1152,
+            flops=1024 * 1152, bytes_accessed=2 * MIB, transcendentals=0
         ),
-    )(queries, marks, *flat)
+    )(queries, marks, *[in_vmem(x) for x in part])
 
 
 def project(core, own, other, own_w, other_w):
@@ -252,11 +243,11 @@
     marks = in_vmem(jnp.where(seen[:, None] == ids, MARK, 0.0).astype(jnp.bfloat16))
     queries = in_vmem(queries)
 
-    steps = [[h] for h in range(heads_kv - 2)] + [[heads_kv - 2, heads_kv - 1]]
-    mine = [
-        attend(queries, marks, step[0], [(own[h], near[h], far[h]) for h in step])
-        for step in steps
-    ]
+    mine = []
+    for h in range(heads_kv):
+        if mine:
+            marks, mine[-1] = lax.optimization_barrier((marks, mine[-1]))
+        mine.append(attend(queries, marks, h, (own[h], near[h], far[h])))
     theirs = [lax.ppermute(x, "head", swap) for x in mine]
     return project(core, mine, theirs, out_weight, other_w)
 

time: 62.1 us -> 57.1 us (0.919)
  waiting for transfers between devices: 14.3 us -> 6.46 us
  starting transfers between devices: 20.3 us -> 22.4 us
  Pallas kernels: 24.6 us -> 25.4 us
    ppermute x1, waiting for transfers between devices: 8.63 us -> 0.01 us  [shards(): last = lax.ppermute(last, 'seq', two_on)]
    ppermute x3, waiting for transfers between devices: 0.01 us -> 3.03 us  [shards(): lax.ppermute(jnp.where(odd, f, x), 'seq', pair)]
    ppermute x1, starting transfers between devices: 2.36 us -> 4.42 us  [shards(): last = lax.ppermute(last, 'seq', two_on)]
    ppermute x3, waiting for transfers between devices: 4.14 us -> 2.26 us  [shards(): far = [lax.ppermute(x, 'seq', two_on) for x in own[:-1]]]
    pallas_call x3 -> x4, Pallas kernels: 7.7 us -> 8.46 us  [attend(): pl.pallas_call(kernel, in_specs=[pl.BlockSpec(memory_space=pltpu.VMEM)] *...]
    ppermute x3 -> x4, waiting for transfers between devices: 1.51 us -> 1.16 us  [shards(): theirs = [lax.ppermute(x, 'head', swap) for x in mine]]
  transfers between devices with their start and end apart: 12 -> 13, of which waited for: 3 -> 4; matrix products, arithmetic and copies ran while one was open for 2% -> 2% of each run, Pallas kernels for 15% -> 17%
where the time goes in v3:
time: 57.1 us; the launch traced here: 56.8 us
  Pallas kernels  25.4 us (44%)
  starting transfers between devices  22.4 us (39%)
  waiting for transfers between devices  6.46 us (11%)
  local copies, waits for them, and re-layouts  2 us (4%)
    pallas_call x1, Pallas kernels, project(): pl.pallas_call(kernel, in_specs=[pl.BlockSpec(memory_space=pltpu.SMEM)] +...  15.6 us
    ppermute x3, starting transfers between devices, shards(): far = [lax.ppermute(x, 'seq', two_on) for x in own[:-1]]  11.5 us
    pallas_call x4, Pallas kernels, attend(): pl.pallas_call(kernel, in_specs=[pl.BlockSpec(memory_space=pltpu.VMEM)] *...  8.46 us
    ppermute x1, starting transfers between devices, shards(): last = lax.ppermute(last, 'seq', two_on)  4.42 us
    ppermute x3, starting transfers between devices, shards(): lax.ppermute(jnp.where(odd, f, x), 'seq', pair)  3.26 us
    ppermute x3, waiting for transfers between devices, shards(): lax.ppermute(jnp.where(odd, f, x), 'seq', pair)  3.03 us
    ppermute x3, waiting for transfers between devices, shards(): far = [lax.ppermute(x, 'seq', two_on) for x in own[:-1]]  2.26 us
    ppermute x1, starting transfers between devices, shards(): beside = lax.ppermute(own[-1], 'seq', pair)  1.58 us
  transfers between devices with their start and end apart: 13, of which 4 were waited for; matrix products, arithmetic and copies ran while one was open for 2% of the time, Pallas kernels for 17%

profile of v3, /device:TPU:0, one launch (start us, length us, event | category | flops | bytes accessed | tf_op | source)
XLA Modules:
  0.0 56.8 jit_solution(16806407456983237289)
XLA Ops:
  0.0 0.0 copy-start.1
  0.0 0.5 collective-permute-start.12
  0.5 1.4 %shard_map.55 = (bf16[512,256]{1,0:T(8,128)(2,1)S(1)}, bf16[512,256]{1,0:T(8,128)(2,1)S(1)}, bf16[512,256]{1,0:T(8,128)(2,1)S(1)}, bf16[512,256]{1,0:T(8,128)(2,1)S(1)}) custom-call(bf16[512,512]{1,0:T(8,128)(2,1)} %keys_ref.1, bf16[512,512]{1,0:T(8,128)(2,1)} %values_ref.1), custom_call_target="tpu_custom_call" | custom-call | bytes 2097152 | tf_op jit(solution)/shard_map/pallas_call | solution.py:113
  1.8 4.6 %collective-permute-start = (bf16[512,256]{1,0:T(8,128)(2,1)S(1)}, bf16[512,256]{1,0:T(8,128)(2,1)S(1)}, u32[]{:S(2)}, u32[]{:S(2)}) collective-permute-start(bf16[512,256]{1,0:T(8,128)(2,1)S(1)} %get-tuple-element.17.own_ref), channel_id=1, source_target_pairs={{0,4},{2,6},{4,8},{6,10},{8,12},{10,14},{1,5},{3,7},{5,9},{7,11},{... | collective-permute-start | bytes 786440 | tf_op jit(solution)/shard_map/ppermute | solution.py:231
  6.4 1.6 %collective-permute-start.2 = (bf16[512,256]{1,0:T(8,128)(2,1)S(1)}, bf16[512,256]{1,0:T(8,128)(2,1)S(1)}, u32[]{:S(2)}, u32[]{:S(2)}) collective-permute-start(bf16[512,256]{1,0:T(8,128)(2,1)S(1)} %get-tuple-element.18.own_ref), channel_id=1, source_target_pairs={{0,2},{2,0},{4,6},{6,4},{8,10},{10,8},{12,14},{14,12},{1,3},{3,1},... | collective-permute-start | bytes 786440 | tf_op jit(solution)/shard_map/ppermute | solution.py:233
  8.0 3.5 %collective-permute-start.3 = (bf16[512,256]{1,0:T(8,128)(2,1)S(1)}, bf16[512,256]{1,0:T(8,128)(2,1)S(1)}, u32[]{:S(2)}, u32[]{:S(2)}) collective-permute-start(bf16[512,256]{1,0:T(8,128)(2,1)S(1)} %get-tuple-element.22.own_ref), channel_id=1, source_target_pairs={{0,4},{2,6},{4,8},{6,10},{8,12},{10,14},{1,5},{3,7},{5,9},{7,11},{... | collective-permute-start | bytes 786440 | tf_op jit(solution)/shard_map/ppermute | solution.py:231
  11.5 3.5 %collective-permute-start.5 = (bf16[512,256]{1,0:T(8,128)(2,1)S(1)}, bf16[512,256]{1,0:T(8,128)(2,1)S(1)}, u32[]{:S(2)}, u32[]{:S(2)}) collective-permute-start(bf16[512,256]{1,0:T(8,128)(2,1)S(1)} %get-tuple-element.25.own_ref), channel_id=1, source_target_pairs={{0,4},{2,6},{4,8},{6,10},{8,12},{10,14},{1,5},{3,7},{5,9},{7,11},{... | collective-permute-start | bytes 786440 | tf_op jit(solution)/shard_map/ppermute | solution.py:231
  15.0 0.8 %pad_dynamic-slice_fusion = s32[1536]{0:T(1024)S(1)} fusion(s32[]{:T(128)S(6)} %select_n.36, s32[4096]{0:T(1024)} %param.8), kind=kLoop, calls=%fused_computation.7 | loop fusion | bytes 22532 | tf_op jit(solution)/shard_map/dynamic_slice | solution.py:241
  15.8 0.0 collective-permute-done.far_ref
  15.8 0.6 %collective-permute-start.1 = (bf16[512,256]{1,0:T(8,128)(2,1)S(1)}, bf16[512,256]{1,0:T(8,128)(2,1)S(1)}, u32[]{:S(2)}, u32[]{:S(2)}) collective-permute-start(bf16[512,256]{1,0:T(8,128)(2,1)S(1)} %broadcast_select_fusion.2), channel_id=1, source_target_pairs={{0,2},{2,0},{4,6},{6,4},{8,10},{10,8},{12,14},{14,12},{1,3},{3,1},... | collective-permute-start | bytes 786440 | tf_op jit(solution)/shard_map/ppermute | solution.py:232
  16.4 2.3 %collective-permute-done.3.far_ref = bf16[512,256]{1,0:T(8,128)(2,1)S(1)} collective-permute-done((bf16[512,256]{1,0:T(8,128)(2,1)S(1)}, bf16[512,256]{1,0:T(8,128)(2,1)S(1)}, u32[]{:S(2)}, u32[]{:S(2)}) %collective-permute-start.3) | collective-permute-done | bytes 262176 | tf_op jit(solution)/shard_map/ppermute | solution.py:231
  18.7 1.6 %collective-permute-start.4 = (bf16[512,256]{1,0:T(8,128)(2,1)S(1)}, bf16[512,256]{1,0:T(8,128)(2,1)S(1)}, u32[]{:S(2)}, u32[]{:S(2)}) collective-permute-start(bf16[512,256]{1,0:T(8,128)(2,1)S(1)} %broadcast_select_fusion.1), channel_id=1, source_target_pairs={{0,2},{2,0},{4,6},{6,4},{8,10},{10,8},{12,14},{14,12},{1,3},{3,1},... | collective-permute-start | bytes 786440 | tf_op jit(solution)/shard_map/ppermute | solution.py:232
  20.3 0.0 collective-permute-done.2
  20.3 4.4 %collective-permute-start.7 = (bf16[1024,256]{1,0:T(8,128)(2,1)S(1)}, bf16[1024,256]{1,0:T(8,128)(2,1)S(1)}, u32[]{:S(2)}, u32[]{:S(2)}) collective-permute-start(bf16[1024,256]{1,0:T(8,128)(2,1)S(1)} %pad_maximum_fusion), channel_id=1, source_target_pairs={{0,4},{2,6},{4,8},{6,10},{8,12},{10,14},{1,5},{3,7},{5,9},{7,11},{... | collective-permute-start | bytes 1572872 | tf_op jit(solution)/shard_map/ppermute | solution.py:235
  24.7 0.0 collective-permute-done.5.far_ref
  24.8 1.1 %collective-permute-start.6 = (bf16[512,256]{1,0:T(8,128)(2,1)S(1)}, bf16[512,256]{1,0:T(8,128)(2,1)S(1)}, u32[]{:S(2)}, u32[]{:S(2)}) collective-permute-start(bf16[512,256]{1,0:T(8,128)(2,1)S(1)} %broadcast_select_fusion), channel_id=1, source_target_pairs={{0,2},{2,0},{4,6},{6,4},{8,10},{10,8},{12,14},{14,12},{1,3},{3,1},... | collective-permute-start | bytes 786440 | tf_op jit(solution)/shard_map/ppermute | solution.py:232
  25.9 0.3 select_convert_fusion.mark_ref
  26.1 0.0 collective-permute-done.1.near_ref
  26.2 0.0 copy-start
  26.2 1.2 %copy-done = bf16[512,1024]{1,0:T(8,128)(2,1)S(1)} copy-done((bf16[512,1024]{1,0:T(8,128)(2,1)S(1)}, bf16[512,1024]{1,0:T(8,128)(2,1)}, u32[]{:S(2)}) %copy-start) | copy-done | bytes 1048600
  27.4 2.1 %shard_map.56.refs_0_ = bf16[512,256]{1,0:T(8,128)(2,1)S(1)} custom-call(bf16[512,1024]{1,0:T(8,128)(2,1)S(1)} %copy-done, bf16[1536,128]{1,0:T(8,128)(2,1)S(1)} %select_convert_fusion.mark_ref, bf16[512,256]{1,0:T(8,128)(2,1)S(1)} %get-tuple-element.17.own_ref, bf16[512,256]{1,0:T(8,128)(2,1)S(1)} %collective-permute-done.1.near_ref, ...), custom_call_target="tpu_custom_call" | custom-call | flops 1179648 | bytes 2097152 | tf_op jit(solution)/shard_map/pallas_call | solution.py:134
  29.5 1.2 %collective-permute-done.4.near_ref = bf16[512,256]{1,0:T(8,128)(2,1)S(1)} collective-permute-done((bf16[512,256]{1,0:T(8,128)(2,1)S(1)}, bf16[512,256]{1,0:T(8,128)(2,1)S(1)}, u32[]{:S(2)}, u32[]{:S(2)}) %collective-permute-start.4) | collective-permute-done | bytes 262176 | tf_op jit(solution)/shard_map/ppermute | solution.py:232
  30.7 2.1 %shard_map.57.refs_1_ = bf16[512,256]{1,0:T(8,128)(2,1)S(1)} custom-call(bf16[512,1024]{1,0:T(8,128)(2,1)S(1)} %copy-done, bf16[1536,128]{1,0:T(8,128)(2,1)S(1)} %select_convert_fusion.mark_ref, bf16[512,256]{1,0:T(8,128)(2,1)S(1)} %get-tuple-element.22.own_ref, bf16[512,256]{1,0:T(8,128)(2,1)S(1)} %collective-permute-done.4.near_ref, ...), custom_call_target="tpu_custom_call" | custom-call | flops 1179648 | bytes 2097152 | tf_op jit(solution)/shard_map/pallas_call | solution.py:134
  32.9 1.8 %collective-permute-done.6.near_ref = bf16[512,256]{1,0:T(8,128)(2,1)S(1)} collective-permute-done((bf16[512,256]{1,0:T(8,128)(2,1)S(1)}, bf16[512,256]{1,0:T(8,128)(2,1)S(1)}, u32[]{:S(2)}, u32[]{:S(2)}) %collective-permute-start.6) | collective-permute-done | bytes 262176 | tf_op jit(solution)/shard_map/ppermute | solution.py:232
  34.6 2.1 %shard_map.58.refs_2_ = bf16[512,256]{1,0:T(8,128)(2,1)S(1)} custom-call(bf16[512,1024]{1,0:T(8,128)(2,1)S(1)} %copy-done, bf16[1536,128]{1,0:T(8,128)(2,1)S(1)} %select_convert_fusion.mark_ref, bf16[512,256]{1,0:T(8,128)(2,1)S(1)} %get-tuple-element.25.own_ref, bf16[512,256]{1,0:T(8,128)(2,1)S(1)} %collective-permute-done.6.near_ref, ...), custom_call_target="tpu_custom_call" | custom-call | flops 1179648 | bytes 2097152 | tf_op jit(solution)/shard_map/pallas_call | solution.py:134
  36.8 0.1 collective-permute-start.10
  36.8 0.5 collective-permute-start.9
  37.3 0.1 collective-permute-start.8
  37.4 0.0 collective-permute-done.7
  37.5 0.0 copy-done.1
  37.5 2.1 %shard_map.59.refs_3_ = bf16[512,256]{1,0:T(8,128)(2,1)S(1)} custom-call(bf16[512,1024]{1,0:T(8,128)(2,1)S(1)} %copy-done.1, bf16[1536,128]{1,0:T(8,128)(2,1)S(1)} %select_convert_fusion.mark_ref, bf16[512,256]{1,0:T(8,128)(2,1)S(1)} %get-tuple-element.18.own_ref, bf16[512,256]{1,0:T(8,128)(2,1)S(1)} %get-tuple-element.30.near_ref, ...), custom_call_target="tpu_custom_call" | custom-call | flops 1179648 | bytes 2097152 | tf_op jit(solution)/shard_map/pallas_call | solution.py:134
  39.6 0.5 collective-permute-start.11
  40.1 0.0 collective-permute-done.10.refs_6_
  40.1 0.0 collective-permute-done.9.refs_5_
  40.1 0.0 collective-permute-done.8.refs_4_
  40.1 1.1 %collective-permute-done.11.refs_7_ = bf16[512,256]{1,0:T(8,128)(2,1)S(1)} collective-permute-done((bf16[512,256]{1,0:T(8,128)(2,1)S(1)}, bf16[512,256]{1,0:T(8,128)(2,1)S(1)}, u32[]{:S(2)}, u32[]{:S(2)}) %collective-permute-start.11) | collective-permute-done | bytes 262176 | tf_op jit(solution)/shard_map/ppermute | solution.py:251
  41.3 0.0 collective-permute-done.12.refs_9_
  41.3 15.6 %shard_map.60 = bf16[512,5376]{1,0:T(8,128)(2,1)} custom-call(s32[1]{0:T(128)} %bitcast.core_ref, bf16[512,256]{1,0:T(8,128)(2,1)S(1)} %shard_map.56.refs_0_, bf16[512,256]{1,0:T(8,128)(2,1)S(1)} %shard_map.57.refs_1_, bf16[512,256]{1,0:T(8,128)(2,1)S(1)} %shard_map.58.refs_2_, bf16[512,256]{1,0:T(8,128)(2,1)S(1)} %shard_map.59.refs_3_, ...), custom_call_target="tpu_custom_call" | custom-call | flops 11274289152 | bytes 33554432 | tf_op jit(solution)/shard_map/pallas_call | solution.py:199
  (5 shorter events, 0.2 us)
Async XLA Ops:
  0.0 37.5 %copy-start.1 = (bf16[512,1024]{1,0:T(8,128)(2,1)S(1)}, bf16[512,1024]{1,0:T(8,128)(2,1)}, u32[]{:S(2)}) copy-start(bf16[512,1024]{1,0:T(8,128)(2,1)} %q_ref.7) | copy-start | bytes 3145732
  0.0 41.3 %collective-permute-start.12 = (bf16[1024,5376]{1,0:T(8,128)(2,1)}, bf16[1024,5376]{1,0:T(8,128)(2,1)}, u32[]{:S(2)}, u32[]{:S(2)}) collective-permute-start(bf16[1024,5376]{1,0:T(8,128)(2,1)} %refs_8_.1), channel_id=1, source_target_pairs={{0,1},{1,0},{2,3},{3,2},{4,5},{5,4},{6,7},{7,6},{8,9},{9,8},{10,11... | collective-permute-start | bytes 33030152 | tf_op jit(solution)/shard_map/ppermute | solution.py:226
  1.8 13.9 %collective-permute-start = (bf16[512,256]{1,0:T(8,128)(2,1)S(1)}, bf16[512,256]{1,0:T(8,128)(2,1)S(1)}, u32[]{:S(2)}, u32[]{:S(2)}) collective-permute-start(bf16[512,256]{1,0:T(8,128)(2,1)S(1)} %get-tuple-element.17.own_ref), channel_id=1, source_target_pairs={{0,4},{2,6},{4,8},{6,10},{8,12},{10,14},{1,5},{3,7},{5,9},{7,11},{... | collective-permute-start | bytes 786440 | tf_op jit(solution)/shard_map/ppermute | solution.py:231
  6.4 13.8 %collective-permute-start.2 = (bf16[512,256]{1,0:T(8,128)(2,1)S(1)}, bf16[512,256]{1,0:T(8,128)(2,1)S(1)}, u32[]{:S(2)}, u32[]{:S(2)}) collective-permute-start(bf16[512,256]{1,0:T(8,128)(2,1)S(1)} %get-tuple-element.18.own_ref), channel_id=1, source_target_pairs={{0,2},{2,0},{4,6},{6,4},{8,10},{10,8},{12,14},{14,12},{1,3},{3,1},... | collective-permute-start | bytes 786440 | tf_op jit(solution)/shard_map/ppermute | solution.py:233
  8.0 10.6 %collective-permute-start.3 = (bf16[512,256]{1,0:T(8,128)(2,1)S(1)}, bf16[512,256]{1,0:T(8,128)(2,1)S(1)}, u32[]{:S(2)}, u32[]{:S(2)}) collective-permute-start(bf16[512,256]{1,0:T(8,128)(2,1)S(1)} %get-tuple-element.22.own_ref), channel_id=1, source_target_pairs={{0,4},{2,6},{4,8},{6,10},{8,12},{10,14},{1,5},{3,7},{5,9},{7,11},{... | collective-permute-start | bytes 786440 | tf_op jit(solution)/shard_map/ppermute | solution.py:231
  11.5 13.2 %collective-permute-start.5 = (bf16[512,256]{1,0:T(8,128)(2,1)S(1)}, bf16[512,256]{1,0:T(8,128)(2,1)S(1)}, u32[]{:S(2)}, u32[]{:S(2)}) collective-permute-start(bf16[512,256]{1,0:T(8,128)(2,1)S(1)} %get-tuple-element.25.own_ref), channel_id=1, source_target_pairs={{0,4},{2,6},{4,8},{6,10},{8,12},{10,14},{1,5},{3,7},{5,9},{7,11},{... | collective-permute-start | bytes 786440 | tf_op jit(solution)/shard_map/ppermute | solution.py:231
  15.8 10.3 %collective-permute-start.1 = (bf16[512,256]{1,0:T(8,128)(2,1)S(1)}, bf16[512,256]{1,0:T(8,128)(2,1)S(1)}, u32[]{:S(2)}, u32[]{:S(2)}) collective-permute-start(bf16[512,256]{1,0:T(8,128)(2,1)S(1)} %broadcast_select_fusion.2), channel_id=1, source_target_pairs={{0,2},{2,0},{4,6},{6,4},{8,10},{10,8},{12,14},{14,12},{1,3},{3,1},... | collective-permute-start | bytes 786440 | tf_op jit(solution)/shard_map/ppermute | solution.py:232
  18.7 12.1 %collective-permute-start.4 = (bf16[512,256]{1,0:T(8,128)(2,1)S(1)}, bf16[512,256]{1,0:T(8,128)(2,1)S(1)}, u32[]{:S(2)}, u32[]{:S(2)}) collective-permute-start(bf16[512,256]{1,0:T(8,128)(2,1)S(1)} %broadcast_select_fusion.1), channel_id=1, source_target_pairs={{0,2},{2,0},{4,6},{6,4},{8,10},{10,8},{12,14},{14,12},{1,3},{3,1},... | collective-permute-start | bytes 786440 | tf_op jit(solution)/shard_map/ppermute | solution.py:232
  20.3 17.1 %collective-permute-start.7 = (bf16[1024,256]{1,0:T(8,128)(2,1)S(1)}, bf16[1024,256]{1,0:T(8,128)(2,1)S(1)}, u32[]{:S(2)}, u32[]{:S(2)}) collective-permute-start(bf16[1024,256]{1,0:T(8,128)(2,1)S(1)} %pad_maximum_fusion), channel_id=1, source_target_pairs={{0,4},{2,6},{4,8},{6,10},{8,12},{10,14},{1,5},{3,7},{5,9},{7,11},{... | collective-permute-start | bytes 1572872 | tf_op jit(solution)/shard_map/ppermute | solution.py:235
  24.8 9.9 %collective-permute-start.6 = (bf16[512,256]{1,0:T(8,128)(2,1)S(1)}, bf16[512,256]{1,0:T(8,128)(2,1)S(1)}, u32[]{:S(2)}, u32[]{:S(2)}) collective-permute-start(bf16[512,256]{1,0:T(8,128)(2,1)S(1)} %broadcast_select_fusion), channel_id=1, source_target_pairs={{0,2},{2,0},{4,6},{6,4},{8,10},{10,8},{12,14},{14,12},{1,3},{3,1},... | collective-permute-start | bytes 786440 | tf_op jit(solution)/shard_map/ppermute | solution.py:232
  26.2 1.2 %copy-start = (bf16[512,1024]{1,0:T(8,128)(2,1)S(1)}, bf16[512,1024]{1,0:T(8,128)(2,1)}, u32[]{:S(2)}) copy-start(bf16[512,1024]{1,0:T(8,128)(2,1)} %q_ref.7) | copy-start | bytes 3145732
  36.8 3.4 %collective-permute-start.10 = (bf16[512,256]{1,0:T(8,128)(2,1)S(1)}, bf16[512,256]{1,0:T(8,128)(2,1)S(1)}, u32[]{:S(2)}, u32[]{:S(2)}) collective-permute-start(bf16[512,256]{1,0:T(8,128)(2,1)S(1)} %shard_map.58.refs_2_), channel_id=1, source_target_pairs={{0,1},{1,0},{2,3},{3,2},{4,5},{5,4},{6,7},{7,6},{8,9},{9,8},{10,11... | collective-permute-start | bytes 786440 | tf_op jit(solution)/shard_map/ppermute | solution.py:251
  36.8 3.3 %collective-permute-start.9 = (bf16[512,256]{1,0:T(8,128)(2,1)S(1)}, bf16[512,256]{1,0:T(8,128)(2,1)S(1)}, u32[]{:S(2)}, u32[]{:S(2)}) collective-permute-start(bf16[512,256]{1,0:T(8,128)(2,1)S(1)} %shard_map.57.refs_1_), channel_id=1, source_target_pairs={{0,1},{1,0},{2,3},{3,2},{4,5},{5,4},{6,7},{7,6},{8,9},{9,8},{10,11... | collective-permute-start | bytes 786440 | tf_op jit(solution)/shard_map/ppermute | solution.py:251
  37.3 2.8 %collective-permute-start.8 = (bf16[512,256]{1,0:T(8,128)(2,1)S(1)}, bf16[512,256]{1,0:T(8,128)(2,1)S(1)}, u32[]{:S(2)}, u32[]{:S(2)}) collective-permute-start(bf16[512,256]{1,0:T(8,128)(2,1)S(1)} %shard_map.56.refs_0_), channel_id=1, source_target_pairs={{0,1},{1,0},{2,3},{3,2},{4,5},{5,4},{6,7},{7,6},{8,9},{9,8},{10,11... | collective-permute-start | bytes 786440 | tf_op jit(solution)/shard_map/ppermute | solution.py:251
  39.6 1.7 %collective-permute-start.11 = (bf16[512,256]{1,0:T(8,128)(2,1)S(1)}, bf16[512,256]{1,0:T(8,128)(2,1)S(1)}, u32[]{:S(2)}, u32[]{:S(2)}) collective-permute-start(bf16[512,256]{1,0:T(8,128)(2,1)S(1)} %shard_map.59.refs_3_), channel_id=1, source_target_pairs={{0,1},{1,0},{2,3},{3,2},{4,5},{5,4},{6,7},{7,6},{8,9},{9,8},{10,11... | collective-permute-start | bytes 786440 | tf_op jit(solution)/shard_map/ppermute | solution.py:251

commit v4 on v3

--- a/solution.py
+++ b/solution.py
@@ -12,6 +12,7 @@
 MARK = 128.0
 LOG2E = 1.4426950408889634
 MIB = 1 << 20
+EARLY = 2
 
 
 def joined(*parts):
@@ -121,74 +122,139 @@
     )(in_hbm(keys), in_hbm(values))
 
 
-def attend(queries, marks, head, part):
+def prepare(seq_index, segments, queries):
+    rows = queries.shape[0]
+    slab = segments.shape[0]
+    blocks = 3
+
+    def kernel(index_ref, seg_ref, q_ref, mark_ref, q_out, sem):
+        copy = pltpu.make_async_copy(q_ref, q_out, sem)
+        copy.start()
+        ids = lax.broadcasted_iota(jnp.int32, (HEAD_SIZE, rows), 0)
+        for b in range(blocks):
+            block = index_ref[0] + b - (blocks - 1)
+            seen = seg_ref[pl.ds(jnp.maximum(block, 0), 1), :]
+            hit = (seen == ids) & (block >= 0)
+            mark = jnp.where(hit, MARK, 0.0)
+            mark_ref[b * rows : (b + 1) * rows, :] = mark.T.astype(jnp.bfloat16)
+        copy.wait()
+
+    vmem = pl.BlockSpec(memory_space=pltpu.VMEM)
+    return pl.pallas_call(
+        kernel,
+        in_specs=[
+            pl.BlockSpec(memory_space=pltpu.SMEM),
+            vmem,
+            pl.BlockSpec(memory_space=pltpu.HBM),
+        ],
+        out_specs=[vmem, vmem],
+        out_shape=[
+            pltpu.VMEM((blocks * rows, HEAD_SIZE), jnp.bfloat16),
+            pltpu.VMEM(queries.shape, queries.dtype),
+        ],
+        scratch_shapes=[pltpu.SemaphoreType.DMA],
+        compiler_params=pltpu.CompilerParams(vmem_limit_bytes=4 * MIB),
+        cost_estimate=pl.CostEstimate(flops=1024, bytes_accessed=1024, transcendentals=0),
+    )(seq_index, segments.reshape(slab // rows, rows), in_hbm(queries))
+
+
+def column_tile(columns):
+    return 768 if columns % 768 == 0 else 128
+
+
+def tile_copy(weights, n, into, sem):
+    tile = into.shape[1]
+    place = pl.ds(pl.multiple_of(n * tile, tile), tile)
+    return pltpu.make_async_copy(weights.at[:, place], into, sem)
+
+
+def attend(queries, marks, head, part, weights=None):
     rows = marks.shape[0] // 3
     width = 2 * HEAD_SIZE
 
-    def kernel(q_ref, mark_ref, own_ref, near_ref, far_ref, out_ref):
+    def kernel(q_ref, mark_ref, own_ref, near_ref, far_ref, *refs):
+        if weights is None:
+            (out_ref,) = refs
+        else:
+            w_ref, out_ref, *tile_refs, sem = refs
+            copies = [tile_copy(w_ref, n, ref, sem.at[n]) for n, ref in enumerate(tile_refs)]
+            for copy in copies:
+                copy.start()
         left = head * width
         attend_kernel(
             q_ref.at[:, left : left + width], own_ref, near_ref, far_ref, mark_ref, out_ref
         )
-
+        if weights is not None:
+            for copy in copies:
+                copy.wait()
+
+    vmem = pl.BlockSpec(memory_space=pltpu.VMEM)
+    specs, outs = [vmem] * 5, [pltpu.VMEM((rows, width), jnp.bfloat16)]
+    flat, scratch = [], []
+    if weights is not None:
+        depth, columns = weights.shape
+        specs.append(pl.BlockSpec(memory_space=pltpu.HBM))
+        flat.append(in_hbm(weights))
+        outs += [pltpu.VMEM((depth, column_tile(columns)), jnp.bfloat16)] * EARLY
+        scratch.append(pltpu.SemaphoreType.DMA((EARLY,)))
     return pl.pallas_call(
         kernel,
-        in_specs=[pl.BlockSpec(memory_space=pltpu.VMEM)] * 5,
-        out_specs=pl.BlockSpec(memory_space=pltpu.VMEM),
-        out_shape=pltpu.VMEM((rows, width), jnp.bfloat16),
+        in_specs=specs,
+        out_specs=[vmem] * len(outs),
+        out_shape=outs,
+        scratch_shapes=scratch,
         compiler_params=pltpu.CompilerParams(vmem_limit_bytes=8 * MIB),
-        cost_estimate=pl.CostEstimate(
-            flops=1024 * 1152, bytes_accessed=2 * MIB, transcendentals=0
-        ),
-    )(queries, marks, *[in_vmem(x) for x in part])
-
-
-def project(core, own, other, own_w, other_w):
+        cost_estimate=pl.CostEstimate(flops=1024, bytes_accessed=1024, transcendentals=0),
+    )(queries, marks, *[in_vmem(x) for x in part], *flat)
+
+
+def project(own, other, own_w, other_w, ready):
     count = len(own)
     rows = own[0].shape[0]
     depth, columns = own_w.shape
-    tile = 768 if columns % 768 == 0 else 128
+    tile = column_tile(columns)
     tiles = columns // tile
-
-    def kernel(core_ref, *refs):
+    late = tiles - len(ready)
+
+    def kernel(*refs):
         own_refs, other_refs = refs[:count], refs[count : 2 * count]
-        own_w_ref, other_w_ref, out_ref, both, w_buf, w_sem, held, out_sem = refs[2 * count :]
-        mine = pl.multiple_of(core_ref[0] * depth, depth)
-        theirs = pl.multiple_of((1 - core_ref[0]) * depth, depth)
+        own_w_ref, other_w_ref, *refs = refs[2 * count :]
+        ready_refs, refs = refs[: len(ready)], refs[len(ready) :]
+        out_ref, row, other_row, held, out_sem, w_buf, w_sem = refs
 
         def place(n):
             return pl.ds(pl.multiple_of(n * tile, tile), tile)
-
-        def fetch(n):
-            return [
-                pltpu.make_async_copy(
-                    ref.at[:, place(n)], w_buf.at[n, pl.ds(start, depth), :], w_sem.at[n, i]
-                )
-                for i, (ref, start) in enumerate(((own_w_ref, mine), (other_w_ref, theirs)))
-            ]
 
         def give(n):
             return pltpu.make_async_copy(
                 held.at[:, place(n)], out_ref.at[:, place(n)], out_sem.at[n]
             )
 
-        for n in range(tiles):
-            for copy in fetch(n):
-                copy.start()
-        for group, start in ((own_refs, mine), (other_refs, theirs)):
-            at = 0
-            for ref in group:
+        def coming(n):
+            slot = n - len(ready)
+            return tile_copy(other_w_ref, n, w_buf.at[slot], w_sem.at[slot])
+
+        def multiply(n, weight):
+            term = jnp.dot(row[...], own_w_ref[:, place(n)], preferred_element_type=jnp.float32)
+            other_term = jnp.dot(
+                other_row[...], weight[...], preferred_element_type=jnp.float32
+            )
+            held[:, place(n)] = (term + other_term).astype(held.dtype)
+            give(n).start()
+
+        for n in range(len(ready), tiles):
+            coming(n).start()
+        for into, group in ((row, own_refs), (other_row, other_refs)):
+            for i, ref in enumerate(group):
                 width = ref.shape[1]
-                both[:, pl.ds(pl.multiple_of(start + at, 128), width)] = ref[...]
-                at += width
-
-        @pl.loop(0, tiles)
+                into[:, i * width : (i + 1) * width] = ref[...]
+        for n, ref in enumerate(ready_refs):
+            multiply(n, ref)
+
+        @pl.loop(len(ready), tiles)
         def _(n):
-            for copy in fetch(n):
-                copy.wait()
-            total = jnp.dot(both[...], w_buf[n], preferred_element_type=jnp.float32)
-            held[:, place(n)] = total.astype(held.dtype)
-            give(n).start()
+            coming(n).wait()
+            multiply(n, w_buf.at[n - len(ready)])
 
         @pl.loop(0, tiles)
         def _(n):
@@ -198,21 +264,22 @@
     hbm = pl.BlockSpec(memory_space=pltpu.HBM)
     return pl.pallas_call(
         kernel,
-        in_specs=[pl.BlockSpec(memory_space=pltpu.SMEM)] + [vmem] * (2 * count) + [hbm] * 2,
+        in_specs=[vmem] * (2 * count + 1) + [hbm] + [vmem] * len(ready),
         out_specs=pl.BlockSpec(memory_space=pl.ANY),
         out_shape=jax.ShapeDtypeStruct((rows, columns), jnp.bfloat16),
         scratch_shapes=[
-            pltpu.VMEM((rows, 2 * depth), jnp.bfloat16),
-            pltpu.VMEM((tiles, 2 * depth, tile), jnp.bfloat16),
-            pltpu.SemaphoreType.DMA((tiles, 2)),
+            pltpu.VMEM((rows, depth), jnp.bfloat16),
+            pltpu.VMEM((rows, depth), jnp.bfloat16),
             pltpu.VMEM((rows, columns), jnp.bfloat16),
             pltpu.SemaphoreType.DMA((tiles,)),
+            pltpu.VMEM((late, depth, tile), jnp.bfloat16),
+            pltpu.SemaphoreType.DMA((late,)),
         ],
-        compiler_params=pltpu.CompilerParams(vmem_limit_bytes=40 * MIB),
+        compiler_params=pltpu.CompilerParams(vmem_limit_bytes=24 * MIB),
         cost_estimate=pl.CostEstimate(
             flops=4 * rows * depth * columns, bytes_accessed=32 * MIB, transcendentals=0
         ),
-    )(core, *[in_vmem(x) for x in own + other], in_hbm(own_w), in_hbm(other_w))
+    )(*[in_vmem(x) for x in own + other], in_vmem(own_w), in_hbm(other_w), *ready)
 
 
 def shards(queries, keys, values, segments, out_weight):
@@ -220,15 +287,18 @@
     heads_kv = keys.shape[1] // HEAD_SIZE
     peers = lax.axis_size("seq")
     seq_index = lax.axis_index("seq")
-    core = lax.axis_index("head").astype(jnp.int32).reshape(1)
     swap = [(0, 1), (1, 0)]
 
+    own = list(pack(keys, values))
+    out_weight, own[0] = lax.optimization_barrier((out_weight, own[0]))
     other_w = lax.ppermute(out_weight, "head", swap)
-    own = pack(keys, values)
     two_on = [(i, i + 2) for i in range(peers - 2)]
     pair = [(i, i ^ 1) for i in range(peers)]
     odd = seq_index % 2 == 1
     far = [lax.ppermute(x, "seq", two_on) for x in own[:-1]]
+    queries, far[0] = lax.optimization_barrier((queries, far[0]))
+    marks, queries = prepare(seq_index.astype(jnp.int32).reshape(1), segments, queries)
+    far[1], marks = lax.optimization_barrier((far[1], marks))
     near = [lax.ppermute(jnp.where(odd, f, x), "seq", pair) for f, x in zip(far, own)]
     beside = lax.ppermute(own[-1], "seq", pair)
     last, far[0] = lax.optimization_barrier((jnp.concatenate([own[-1], beside]), far[0]))
@@ -236,20 +306,16 @@
     far.append(last[:rows])
     near.append(jnp.where(odd, beside, last[rows:]))
 
-    halo = 2 * rows
-    padded = jnp.concatenate([jnp.full((halo,), -1, jnp.int32), segments])
-    seen = lax.dynamic_slice_in_dim(padded, seq_index * rows, halo + rows, 0)
-    ids = lax.broadcasted_iota(jnp.int32, (halo + rows, HEAD_SIZE), 1)
-    marks = in_vmem(jnp.where(seen[:, None] == ids, MARK, 0.0).astype(jnp.bfloat16))
-    queries = in_vmem(queries)
-
-    mine = []
+    mine, ready = [], []
     for h in range(heads_kv):
         if mine:
             marks, mine[-1] = lax.optimization_barrier((marks, mine[-1]))
-        mine.append(attend(queries, marks, h, (own[h], near[h], far[h])))
+        weights = other_w if h == heads_kv - 1 else None
+        result, *tile = attend(queries, marks, h, (own[h], near[h], far[h]), weights)
+        mine.append(result)
+        ready += tile
     theirs = [lax.ppermute(x, "head", swap) for x in mine]
-    return project(core, mine, theirs, out_weight, other_w)
+    return project(mine, theirs, out_weight, other_w, ready)
 
 
 def solution(mesh):

time: 57.1 us -> 55 us (0.963)
  waiting for transfers between devices: 6.46 us -> 8.68 us
  starting transfers between devices: 22.4 us -> 20.5 us
  local copies, waits for them, and re-layouts: 2 us -> 0.74 us
  Pallas kernels: 25.4 us -> 24.4 us
    ppermute x1, starting transfers between devices: 4.42 us -> 2.73 us  [shards(): last = lax.ppermute(last, 'seq', two_on)]
    ppermute x3, waiting for transfers between devices: 3.03 us -> 4.59 us  [shards(): lax.ppermute(jnp.where(odd, f, x), 'seq', pair)]
    unnamed x4 -> x6, local copies, waits for them, and re-layouts: 1.22 us -> 0.02 us
    pallas_call x5 -> x6, Pallas kernels: 24 us -> 23 us  [the longest x1 13.5 us: project(): pl.pallas_call(kernel, in_specs=[vmem] * (2 * count + 1) + [hbm] + [vmem]...]
    dynamic_slice x1 -> x0, local copies, waits for them, and re-layouts: 0.78 us -> none  [shards(): seen = lax.dynamic_slice_in_dim(padded, seq_index * rows, halo + rows, 0)]
    reshape x0 -> x1, local copies, waits for them, and re-layouts: none -> 0.72 us  [prepare(): segments.reshape(slab // rows, rows)]
    ppermute x3, waiting for transfers between devices: 2.26 us -> 2.92 us  [shards(): far = [lax.ppermute(x, 'seq', two_on) for x in own[:-1]]]
where the time goes in v4:
time: 55 us; the launch traced here: 54.7 us
  Pallas kernels  24.4 us (44%)
  starting transfers between devices  20.5 us (37%)
  waiting for transfers between devices  8.68 us (16%)
  local copies, waits for them, and re-layouts  0.74 us (1%)
    pallas_call x1, Pallas kernels, project(): pl.pallas_call(kernel, in_specs=[vmem] * (2 * count + 1) + [hbm] + [vmem]...  13.5 us
    ppermute x3, starting transfers between devices, shards(): far = [lax.ppermute(x, 'seq', two_on) for x in own[:-1]]  11.5 us
    pallas_call x4, Pallas kernels, attend(): pl.pallas_call(kernel, in_specs=specs, out_specs=[vmem] * len(outs), out_...  8.3 us
    ppermute x3, waiting for transfers between devices, shards(): lax.ppermute(jnp.where(odd, f, x), 'seq', pair)  4.59 us
    ppermute x3, starting transfers between devices, shards(): lax.ppermute(jnp.where(odd, f, x), 'seq', pair)  3.09 us
    ppermute x3, waiting for transfers between devices, shards(): far = [lax.ppermute(x, 'seq', two_on) for x in own[:-1]]  2.92 us
    ppermute x1, starting transfers between devices, shards(): last = lax.ppermute(last, 'seq', two_on)  2.73 us
    ppermute x1, starting transfers between devices, shards(): beside = lax.ppermute(own[-1], 'seq', pair)  1.58 us
  transfers between devices with their start and end apart: 13, of which 4 were waited for; matrix products, arithmetic and copies ran while one was open for 2% of the time, Pallas kernels for 17%

profile of v4, /device:TPU:0, one launch (start us, length us, event | category | flops | bytes accessed | tf_op | source)
XLA Modules:
  0.0 54.7 jit_solution(14516243029992694901)
XLA Ops:
  0.0 1.4 %shard_map.55 = (bf16[512,256]{1,0:T(8,128)(2,1)S(1)}, bf16[512,256]{1,0:T(8,128)(2,1)S(1)}, bf16[512,256]{1,0:T(8,128)(2,1)S(1)}, bf16[512,256]{1,0:T(8,128)(2,1)S(1)}) custom-call(bf16[512,512]{1,0:T(8,128)(2,1)} %keys_ref.1, bf16[512,512]{1,0:T(8,128)(2,1)} %values_ref.1), custom_call_target="tpu_custom_call" | custom-call | bytes 2097152 | tf_op jit(solution)/shard_map/pallas_call | solution.py:114
  1.4 0.5 collective-permute-start.8
  1.9 4.5 %collective-permute-start.1 = (bf16[512,256]{1,0:T(8,128)(2,1)S(1)}, bf16[512,256]{1,0:T(8,128)(2,1)S(1)}, u32[]{:S(2)}, u32[]{:S(2)}) collective-permute-start(bf16[512,256]{1,0:T(8,128)(2,1)S(1)} %get-tuple-element.30.own_ref), channel_id=1, source_target_pairs={{0,4},{2,6},{4,8},{6,10},{8,12},{10,14},{1,5},{3,7},{5,9},{7,11},{... | collective-permute-start | bytes 786440 | tf_op jit(solution)/shard_map/ppermute | solution.py:298
  6.4 1.6 %collective-permute-start.3 = (bf16[512,256]{1,0:T(8,128)(2,1)S(1)}, bf16[512,256]{1,0:T(8,128)(2,1)S(1)}, u32[]{:S(2)}, u32[]{:S(2)}) collective-permute-start(bf16[512,256]{1,0:T(8,128)(2,1)S(1)} %get-tuple-element.36.own_ref), channel_id=1, source_target_pairs={{0,2},{2,0},{4,6},{6,4},{8,10},{10,8},{12,14},{14,12},{1,3},{3,1},... | collective-permute-start | bytes 786440 | tf_op jit(solution)/shard_map/ppermute | solution.py:303
  8.0 3.5 %collective-permute-start = (bf16[512,256]{1,0:T(8,128)(2,1)S(1)}, bf16[512,256]{1,0:T(8,128)(2,1)S(1)}, u32[]{:S(2)}, u32[]{:S(2)}) collective-permute-start(bf16[512,256]{1,0:T(8,128)(2,1)S(1)} %get-tuple-element.28.own_ref), channel_id=1, source_target_pairs={{0,4},{2,6},{4,8},{6,10},{8,12},{10,14},{1,5},{3,7},{5,9},{7,11},{... | collective-permute-start | bytes 786440 | tf_op jit(solution)/shard_map/ppermute | solution.py:298
  11.5 3.5 %collective-permute-start.5 = (bf16[512,256]{1,0:T(8,128)(2,1)S(1)}, bf16[512,256]{1,0:T(8,128)(2,1)S(1)}, u32[]{:S(2)}, u32[]{:S(2)}) collective-permute-start(bf16[512,256]{1,0:T(8,128)(2,1)S(1)} %get-tuple-element.43.own_ref), channel_id=1, source_target_pairs={{0,4},{2,6},{4,8},{6,10},{8,12},{10,14},{1,5},{3,7},{5,9},{7,11},{... | collective-permute-start | bytes 786440 | tf_op jit(solution)/shard_map/ppermute | solution.py:298
  15.0 0.7 %reshape.7.seg_ref = s32[8,512]{1,0:T(8,128)S(1)} reshape(s32[4096]{0:T(1024)} %param.8) | data formatting | bytes 32768 | tf_op jit(solution)/shard_map/reshape | solution.py:158
  15.7 0.0 collective-permute-done.1.far_ref
  15.8 0.6 %collective-permute-start.2 = (bf16[512,256]{1,0:T(8,128)(2,1)S(1)}, bf16[512,256]{1,0:T(8,128)(2,1)S(1)}, u32[]{:S(2)}, u32[]{:S(2)}) collective-permute-start(bf16[512,256]{1,0:T(8,128)(2,1)S(1)} %broadcast_select_fusion.2), channel_id=1, source_target_pairs={{0,2},{2,0},{4,6},{6,4},{8,10},{10,8},{12,14},{14,12},{1,3},{3,1},... | collective-permute-start | bytes 786440 | tf_op jit(solution)/shard_map/ppermute | solution.py:302
  16.3 0.0 collective-permute-done.3
  16.4 2.7 %collective-permute-start.7 = (bf16[1024,256]{1,0:T(8,128)(2,1)S(1)}, bf16[1024,256]{1,0:T(8,128)(2,1)S(1)}, u32[]{:S(2)}, u32[]{:S(2)}) collective-permute-start(bf16[1024,256]{1,0:T(8,128)(2,1)S(1)} %pad_maximum_fusion), channel_id=1, source_target_pairs={{0,4},{2,6},{4,8},{6,10},{8,12},{10,14},{1,5},{3,7},{5,9},{7,11},{... | collective-permute-start | bytes 1572872 | tf_op jit(solution)/shard_map/ppermute | solution.py:305
  19.1 1.2 %shard_map.56 = (bf16[1536,128]{1,0:T(8,128)(2,1)S(1)}, bf16[512,1024]{1,0:T(8,128)(2,1)S(1)}) custom-call(s32[1]{0:T(128)} %bitcast.index_ref, s32[8,512]{1,0:T(8,128)S(1)} %reshape.7.seg_ref, bf16[512,1024]{1,0:T(8,128)(2,1)} %q_ref), custom_call_target="tpu_custom_call" | custom-call | flops 1024 | bytes 1024 | tf_op jit(solution)/shard_map/pallas_call | solution.py:143
  20.4 0.0 collective-permute-done.far_ref
  20.4 0.9 %collective-permute-start.4 = (bf16[512,256]{1,0:T(8,128)(2,1)S(1)}, bf16[512,256]{1,0:T(8,128)(2,1)S(1)}, u32[]{:S(2)}, u32[]{:S(2)}) collective-permute-start(bf16[512,256]{1,0:T(8,128)(2,1)S(1)} %broadcast_select_fusion.1), channel_id=1, source_target_pairs={{0,2},{2,0},{4,6},{6,4},{8,10},{10,8},{12,14},{14,12},{1,3},{3,1},... | collective-permute-start | bytes 786440 | tf_op jit(solution)/shard_map/ppermute | solution.py:302
  21.3 2.9 %collective-permute-done.5.far_ref = bf16[512,256]{1,0:T(8,128)(2,1)S(1)} collective-permute-done((bf16[512,256]{1,0:T(8,128)(2,1)S(1)}, bf16[512,256]{1,0:T(8,128)(2,1)S(1)}, u32[]{:S(2)}, u32[]{:S(2)}) %collective-permute-start.5) | collective-permute-done | bytes 262176 | tf_op jit(solution)/shard_map/ppermute | solution.py:298
  24.3 1.6 %collective-permute-start.6 = (bf16[512,256]{1,0:T(8,128)(2,1)S(1)}, bf16[512,256]{1,0:T(8,128)(2,1)S(1)}, u32[]{:S(2)}, u32[]{:S(2)}) collective-permute-start(bf16[512,256]{1,0:T(8,128)(2,1)S(1)} %broadcast_select_fusion), channel_id=1, source_target_pairs={{0,2},{2,0},{4,6},{6,4},{8,10},{10,8},{12,14},{14,12},{1,3},{3,1},... | collective-permute-start | bytes 786440 | tf_op jit(solution)/shard_map/ppermute | solution.py:302
  25.9 0.0 collective-permute-done.2.near_ref
  25.9 0.0 slice-start
  25.9 2.1 %shard_map.57.refs_0_ = bf16[512,256]{1,0:T(8,128)(2,1)S(1)} custom-call(bf16[512,1024]{1,0:T(8,128)(2,1)S(1)} %get-tuple-element.34.q_ref, bf16[1536,128]{1,0:T(8,128)(2,1)S(1)} %get-tuple-element.45.mark_ref, bf16[512,256]{1,0:T(8,128)(2,1)S(1)} %get-tuple-element.30.own_ref, bf16[512,256]{1,0:T(8,128)(2,1)S(1)} %collective-permute-done.2.near_ref, ...), custom_call_target="tpu_custom_call" | custom-call | flops 1024 | bytes 1024 | tf_op jit(solution)/shard_map/pallas_call | solution.py:200
  27.9 2.6 %collective-permute-done.4.near_ref = bf16[512,256]{1,0:T(8,128)(2,1)S(1)} collective-permute-done((bf16[512,256]{1,0:T(8,128)(2,1)S(1)}, bf16[512,256]{1,0:T(8,128)(2,1)S(1)}, u32[]{:S(2)}, u32[]{:S(2)}) %collective-permute-start.4) | collective-permute-done | bytes 262176 | tf_op jit(solution)/shard_map/ppermute | solution.py:302
  30.5 2.1 %shard_map.58.refs_1_ = bf16[512,256]{1,0:T(8,128)(2,1)S(1)} custom-call(bf16[512,1024]{1,0:T(8,128)(2,1)S(1)} %get-tuple-element.34.q_ref, bf16[1536,128]{1,0:T(8,128)(2,1)S(1)} %get-tuple-element.45.mark_ref, bf16[512,256]{1,0:T(8,128)(2,1)S(1)} %get-tuple-element.28.own_ref, bf16[512,256]{1,0:T(8,128)(2,1)S(1)} %collective-permute-done.4.near_ref, ...), custom_call_target="tpu_custom_call" | custom-call | flops 1024 | bytes 1024 | tf_op jit(solution)/shard_map/pallas_call | solution.py:200
  32.6 0.0 slice-start.1
  32.6 2.0 %collective-permute-done.6.near_ref = bf16[512,256]{1,0:T(8,128)(2,1)S(1)} collective-permute-done((bf16[512,256]{1,0:T(8,128)(2,1)S(1)}, bf16[512,256]{1,0:T(8,128)(2,1)S(1)}, u32[]{:S(2)}, u32[]{:S(2)}) %collective-permute-start.6) | collective-permute-done | bytes 262176 | tf_op jit(solution)/shard_map/ppermute | solution.py:302
  34.6 2.1 %shard_map.59.refs_2_ = bf16[512,256]{1,0:T(8,128)(2,1)S(1)} custom-call(bf16[512,1024]{1,0:T(8,128)(2,1)S(1)} %get-tuple-element.34.q_ref, bf16[1536,128]{1,0:T(8,128)(2,1)S(1)} %get-tuple-element.45.mark_ref, bf16[512,256]{1,0:T(8,128)(2,1)S(1)} %get-tuple-element.43.own_ref, bf16[512,256]{1,0:T(8,128)(2,1)S(1)} %collective-permute-done.6.near_ref, ...), custom_call_target="tpu_custom_call" | custom-call | flops 1024 | bytes 1024 | tf_op jit(solution)/shard_map/pallas_call | solution.py:200
  36.7 0.1 collective-permute-start.11
  36.8 0.5 collective-permute-start.10
  37.3 0.1 collective-permute-start.9
  37.4 0.0 collective-permute-done.7
  37.4 0.0 collective-permute-done.8.refs_0_.refs_9_
  37.4 0.0 slice-start.2
  37.4 2.1 %shard_map.60 = (bf16[512,256]{1,0:T(8,128)(2,1)S(1)}, bf16[1024,768]{1,0:T(8,128)(2,1)S(1)}, bf16[1024,768]{1,0:T(8,128)(2,1)S(1)}) custom-call(bf16[512,1024]{1,0:T(8,128)(2,1)S(1)} %get-tuple-element.34.q_ref, bf16[1536,128]{1,0:T(8,128)(2,1)S(1)} %get-tuple-element.45.mark_ref, bf16[512,256]{1,0:T(8,128)(2,1)S(1)} %get-tuple-element.36.own_ref, ...), custom_call_target="tpu_custom_call" | custom-call | flops 1024 | bytes 1024 | tf_op jit(solution)/shard_map/pallas_call | solution.py:200
  39.5 0.5 collective-permute-start.12
  40.0 0.0 collective-permute-done.11.refs_6_
  40.0 0.0 collective-permute-done.10.refs_5_
  40.0 0.0 collective-permute-done.9.refs_4_
  40.0 1.1 %collective-permute-done.12.refs_7_ = bf16[512,256]{1,0:T(8,128)(2,1)S(1)} collective-permute-done((bf16[512,256]{1,0:T(8,128)(2,1)S(1)}, bf16[512,256]{1,0:T(8,128)(2,1)S(1)}, u32[]{:S(2)}, u32[]{:S(2)}) %collective-permute-start.12) | collective-permute-done | bytes 262176 | tf_op jit(solution)/shard_map/ppermute | solution.py:317
  41.2 0.0 slice-done
  41.2 0.0 slice-done.1
  41.2 0.0 slice-done.2
  41.2 13.5 %shard_map.61 = bf16[512,5376]{1,0:T(8,128)(2,1)} custom-call(bf16[512,256]{1,0:T(8,128)(2,1)S(1)} %shard_map.57.refs_0_, bf16[512,256]{1,0:T(8,128)(2,1)S(1)} %shard_map.58.refs_1_, bf16[512,256]{1,0:T(8,128)(2,1)S(1)} %shard_map.59.refs_2_, bf16[512,256]{1,0:T(8,128)(2,1)S(1)} %get-tuple-element.48.refs_3_, ...), custom_call_target="tpu_custom_call" | custom-call | flops 11274289152 | bytes 33554432 | tf_op jit(solution)/shard_map/pallas_call | solution.py:265
  (6 shorter events, 0.2 us)
Async XLA Ops:
  1.4 36.0 %collective-permute-start.8 = (bf16[1024,5376]{1,0:T(8,128)(2,1)}, bf16[1024,5376]{1,0:T(8,128)(2,1)}, u32[]{:S(2)}, u32[]{:S(2)}) collective-permute-start(bf16[1024,5376]{1,0:T(8,128)(2,1)} %refs_8_), channel_id=1, source_target_pairs={{0,1},{1,0},{2,3},{3,2},{4,5},{5,4},{6,7},{7,6},{8,9},{9,8},{10,11... | collective-permute-start | bytes 33030152 | tf_op jit(solution)/shard_map/ppermute | solution.py:294
  1.9 13.8 %collective-permute-start.1 = (bf16[512,256]{1,0:T(8,128)(2,1)S(1)}, bf16[512,256]{1,0:T(8,128)(2,1)S(1)}, u32[]{:S(2)}, u32[]{:S(2)}) collective-permute-start(bf16[512,256]{1,0:T(8,128)(2,1)S(1)} %get-tuple-element.30.own_ref), channel_id=1, source_target_pairs={{0,4},{2,6},{4,8},{6,10},{8,12},{10,14},{1,5},{3,7},{5,9},{7,11},{... | collective-permute-start | bytes 786440 | tf_op jit(solution)/shard_map/ppermute | solution.py:298
  6.4 9.9 %collective-permute-start.3 = (bf16[512,256]{1,0:T(8,128)(2,1)S(1)}, bf16[512,256]{1,0:T(8,128)(2,1)S(1)}, u32[]{:S(2)}, u32[]{:S(2)}) collective-permute-start(bf16[512,256]{1,0:T(8,128)(2,1)S(1)} %get-tuple-element.36.own_ref), channel_id=1, source_target_pairs={{0,2},{2,0},{4,6},{6,4},{8,10},{10,8},{12,14},{14,12},{1,3},{3,1},... | collective-permute-start | bytes 786440 | tf_op jit(solution)/shard_map/ppermute | solution.py:303
  8.0 12.4 %collective-permute-start = (bf16[512,256]{1,0:T(8,128)(2,1)S(1)}, bf16[512,256]{1,0:T(8,128)(2,1)S(1)}, u32[]{:S(2)}, u32[]{:S(2)}) collective-permute-start(bf16[512,256]{1,0:T(8,128)(2,1)S(1)} %get-tuple-element.28.own_ref), channel_id=1, source_target_pairs={{0,4},{2,6},{4,8},{6,10},{8,12},{10,14},{1,5},{3,7},{5,9},{7,11},{... | collective-permute-start | bytes 786440 | tf_op jit(solution)/shard_map/ppermute | solution.py:298
  11.5 12.8 %collective-permute-start.5 = (bf16[512,256]{1,0:T(8,128)(2,1)S(1)}, bf16[512,256]{1,0:T(8,128)(2,1)S(1)}, u32[]{:S(2)}, u32[]{:S(2)}) collective-permute-start(bf16[512,256]{1,0:T(8,128)(2,1)S(1)} %get-tuple-element.43.own_ref), channel_id=1, source_target_pairs={{0,4},{2,6},{4,8},{6,10},{8,12},{10,14},{1,5},{3,7},{5,9},{7,11},{... | collective-permute-start | bytes 786440 | tf_op jit(solution)/shard_map/ppermute | solution.py:298
  15.8 10.1 %collective-permute-start.2 = (bf16[512,256]{1,0:T(8,128)(2,1)S(1)}, bf16[512,256]{1,0:T(8,128)(2,1)S(1)}, u32[]{:S(2)}, u32[]{:S(2)}) collective-permute-start(bf16[512,256]{1,0:T(8,128)(2,1)S(1)} %broadcast_select_fusion.2), channel_id=1, source_target_pairs={{0,2},{2,0},{4,6},{6,4},{8,10},{10,8},{12,14},{14,12},{1,3},{3,1},... | collective-permute-start | bytes 786440 | tf_op jit(solution)/shard_map/ppermute | solution.py:302
  16.4 21.0 %collective-permute-start.7 = (bf16[1024,256]{1,0:T(8,128)(2,1)S(1)}, bf16[1024,256]{1,0:T(8,128)(2,1)S(1)}, u32[]{:S(2)}, u32[]{:S(2)}) collective-permute-start(bf16[1024,256]{1,0:T(8,128)(2,1)S(1)} %pad_maximum_fusion), channel_id=1, source_target_pairs={{0,4},{2,6},{4,8},{6,10},{8,12},{10,14},{1,5},{3,7},{5,9},{7,11},{... | collective-permute-start | bytes 1572872 | tf_op jit(solution)/shard_map/ppermute | solution.py:305
  20.4 10.1 %collective-permute-start.4 = (bf16[512,256]{1,0:T(8,128)(2,1)S(1)}, bf16[512,256]{1,0:T(8,128)(2,1)S(1)}, u32[]{:S(2)}, u32[]{:S(2)}) collective-permute-start(bf16[512,256]{1,0:T(8,128)(2,1)S(1)} %broadcast_select_fusion.1), channel_id=1, source_target_pairs={{0,2},{2,0},{4,6},{6,4},{8,10},{10,8},{12,14},{14,12},{1,3},{3,1},... | collective-permute-start | bytes 786440 | tf_op jit(solution)/shard_map/ppermute | solution.py:302
  24.3 10.3 %collective-permute-start.6 = (bf16[512,256]{1,0:T(8,128)(2,1)S(1)}, bf16[512,256]{1,0:T(8,128)(2,1)S(1)}, u32[]{:S(2)}, u32[]{:S(2)}) collective-permute-start(bf16[512,256]{1,0:T(8,128)(2,1)S(1)} %broadcast_select_fusion), channel_id=1, source_target_pairs={{0,2},{2,0},{4,6},{6,4},{8,10},{10,8},{12,14},{14,12},{1,3},{3,1},... | collective-permute-start | bytes 786440 | tf_op jit(solution)/shard_map/ppermute | solution.py:302
  25.9 15.3 %slice-start = ((s8[11010048]{0:T(1024)(128)(4,1)}), s8[4194304]{0:T(1024)(128)(4,1)S(1)}, s32[]{:S(2)}) async-start(s8[11010048]{0:T(1024)(128)(4,1)} %bitcast.1), calls=%async_computation | async-start | bytes 8388608
  32.6 8.6 %slice-start.1 = ((s8[11010048]{0:T(1024)(128)(4,1)}), s8[4194304]{0:T(1024)(128)(4,1)S(1)}, s32[]{:S(2)}) async-start(s8[11010048]{0:T(1024)(128)(4,1)} %bitcast.1), calls=%async_computation.1 | async-start | bytes 8388608
  36.7 3.3 %collective-permute-start.11 = (bf16[512,256]{1,0:T(8,128)(2,1)S(1)}, bf16[512,256]{1,0:T(8,128)(2,1)S(1)}, u32[]{:S(2)}, u32[]{:S(2)}) collective-permute-start(bf16[512,256]{1,0:T(8,128)(2,1)S(1)} %shard_map.59.refs_2_), channel_id=1, source_target_pairs={{0,1},{1,0},{2,3},{3,2},{4,5},{5,4},{6,7},{7,6},{8,9},{9,8},{10,11... | collective-permute-start | bytes 786440 | tf_op jit(solution)/shard_map/ppermute | solution.py:317
  36.8 3.2 %collective-permute-start.10 = (bf16[512,256]{1,0:T(8,128)(2,1)S(1)}, bf16[512,256]{1,0:T(8,128)(2,1)S(1)}, u32[]{:S(2)}, u32[]{:S(2)}) collective-permute-start(bf16[512,256]{1,0:T(8,128)(2,1)S(1)} %shard_map.58.refs_1_), channel_id=1, source_target_pairs={{0,1},{1,0},{2,3},{3,2},{4,5},{5,4},{6,7},{7,6},{8,9},{9,8},{10,11... | collective-permute-start | bytes 786440 | tf_op jit(solution)/shard_map/ppermute | solution.py:317
  37.3 2.8 %collective-permute-start.9 = (bf16[512,256]{1,0:T(8,128)(2,1)S(1)}, bf16[512,256]{1,0:T(8,128)(2,1)S(1)}, u32[]{:S(2)}, u32[]{:S(2)}) collective-permute-start(bf16[512,256]{1,0:T(8,128)(2,1)S(1)} %shard_map.57.refs_0_), channel_id=1, source_target_pairs={{0,1},{1,0},{2,3},{3,2},{4,5},{5,4},{6,7},{7,6},{8,9},{9,8},{10,11... | collective-permute-start | bytes 786440 | tf_op jit(solution)/shard_map/ppermute | solution.py:317
  37.4 3.8 %slice-start.2 = ((s8[11010048]{0:T(1024)(128)(4,1)}), s8[2621440]{0:T(1024)(128)(4,1)S(1)}, s32[]{:S(2)}) async-start(s8[11010048]{0:T(1024)(128)(4,1)} %bitcast.1), calls=%async_computation.2 | async-start | bytes 5242880
  39.5 1.7 %collective-permute-start.12 = (bf16[512,256]{1,0:T(8,128)(2,1)S(1)}, bf16[512,256]{1,0:T(8,128)(2,1)S(1)}, u32[]{:S(2)}, u32[]{:S(2)}) collective-permute-start(bf16[512,256]{1,0:T(8,128)(2,1)S(1)} %get-tuple-element.48.refs_3_), channel_id=1, source_target_pairs={{0,1},{1,0},{2,3},{3,2},{4,5},{5,4},{6,7},{7,6},{8,9},{9,8},{10,11... | collective-permute-start | bytes 786440 | tf_op jit(solution)/shard_map/ppermute | solution.py:317

commit v5 on v4

--- a/solution.py
+++ b/solution.py
@@ -208,7 +208,39 @@
     )(queries, marks, *[in_vmem(x) for x in part], *flat)
 
 
-def project(own, other, own_w, other_w, ready):
+def project_early(own, other, own_w, ready):
+    count = len(own)
+    rows, width = own[0].shape
+    tile = ready.shape[1]
+    depth = count * width
+
+    def kernel(*refs):
+        own_refs, other_refs = refs[:count], refs[count : 2 * count]
+        own_w_ref, ready_ref, out_ref, row, other_row = refs[2 * count :]
+        for into, group in ((row, own_refs), (other_row, other_refs)):
+            for i, ref in enumerate(group):
+                into[:, i * width : (i + 1) * width] = ref[...]
+        term = jnp.dot(row[...], own_w_ref[:depth, :tile], preferred_element_type=jnp.float32)
+        other_term = jnp.dot(
+            other_row[...], ready_ref[:depth, :], preferred_element_type=jnp.float32
+        )
+        out_ref[...] = term + other_term
+
+    vmem = pl.BlockSpec(memory_space=pltpu.VMEM)
+    return pl.pallas_call(
+        kernel,
+        in_specs=[vmem] * (2 * count + 2),
+        out_specs=vmem,
+        out_shape=pltpu.VMEM((rows, tile), jnp.float32),
+        scratch_shapes=[pltpu.VMEM((rows, depth), jnp.bfloat16)] * 2,
+        compiler_params=pltpu.CompilerParams(vmem_limit_bytes=8 * MIB),
+        cost_estimate=pl.CostEstimate(
+            flops=4 * rows * depth * tile, bytes_accessed=4 * MIB, transcendentals=0
+        ),
+    )(*[in_vmem(x) for x in own + other], in_vmem(own_w), ready)
+
+
+def project(own, other, own_w, other_w, ready, base):
     count = len(own)
     rows = own[0].shape[0]
     depth, columns = own_w.shape
@@ -219,6 +251,7 @@
     def kernel(*refs):
         own_refs, other_refs = refs[:count], refs[count : 2 * count]
         own_w_ref, other_w_ref, *refs = refs[2 * count :]
+        base_ref, *refs = refs
         ready_refs, refs = refs[: len(ready)], refs[len(ready) :]
         out_ref, row, other_row, held, out_sem, w_buf, w_sem = refs
 
@@ -234,12 +267,18 @@
             slot = n - len(ready)
             return tile_copy(other_w_ref, n, w_buf.at[slot], w_sem.at[slot])
 
-        def multiply(n, weight):
-            term = jnp.dot(row[...], own_w_ref[:, place(n)], preferred_element_type=jnp.float32)
+        def multiply(n, weight, base=None):
+            down = slice(0 if base is None else depth - own_refs[-1].shape[1], depth)
+            term = jnp.dot(
+                row[:, down], own_w_ref[down, place(n)], preferred_element_type=jnp.float32
+            )
             other_term = jnp.dot(
-                other_row[...], weight[...], preferred_element_type=jnp.float32
-            )
-            held[:, place(n)] = (term + other_term).astype(held.dtype)
+                other_row[:, down], weight[down, :], preferred_element_type=jnp.float32
+            )
+            total = term + other_term
+            if base is not None:
+                total = total + base[...]
+            held[:, place(n)] = total.astype(held.dtype)
             give(n).start()
 
         for n in range(len(ready), tiles):
@@ -249,7 +288,7 @@
                 width = ref.shape[1]
                 into[:, i * width : (i + 1) * width] = ref[...]
         for n, ref in enumerate(ready_refs):
-            multiply(n, ref)
+            multiply(n, ref, base_ref if n == 0 else None)
 
         @pl.loop(len(ready), tiles)
         def _(n):
@@ -264,7 +303,7 @@
     hbm = pl.BlockSpec(memory_space=pltpu.HBM)
     return pl.pallas_call(
         kernel,
-        in_specs=[vmem] * (2 * count + 1) + [hbm] + [vmem] * len(ready),
+        in_specs=[vmem] * (2 * count + 1) + [hbm] + [vmem] * (1 + len(ready)),
         out_specs=pl.BlockSpec(memory_space=pl.ANY),
         out_shape=jax.ShapeDtypeStruct((rows, columns), jnp.bfloat16),
         scratch_shapes=[
@@ -279,7 +318,7 @@
         cost_estimate=pl.CostEstimate(
             flops=4 * rows * depth * columns, bytes_accessed=32 * MIB, transcendentals=0
         ),
-    )(*[in_vmem(x) for x in own + other], in_vmem(own_w), in_hbm(other_w), *ready)
+    )(*[in_vmem(x) for x in own + other], in_vmem(own_w), in_hbm(other_w), base, *ready)
 
 
 def shards(queries, keys, values, segments, out_weight):
@@ -315,7 +354,8 @@
         mine.append(result)
         ready += tile
     theirs = [lax.ppermute(x, "head", swap) for x in mine]
-    return project(mine, theirs, out_weight, other_w, ready)
+    base = project_early(mine[:-1], theirs[:-1], out_weight, ready[0])
+    return project(mine, theirs, out_weight, other_w, ready, base)
 
 
 def solution(mesh):

time: 55 us -> 54.1 us (0.984)
  waiting for transfers between devices: 8.68 us -> 7.53 us
    pallas_call x0 -> x1, Pallas kernels: none -> 1.38 us  [project_early(): pl.pallas_call(kernel, in_specs=[vmem] * (2 * count + 2), out_specs=vmem,...]
    pallas_call x1, Pallas kernels: 13.5 us -> 12.2 us  [project(): pl.pallas_call(kernel, in_specs=[vmem] * (2 * count + 1) + [hbm] + [vmem]...]
    ppermute x4, waiting for transfers between devices: 1.16 us -> 0.01 us  [shards(): theirs = [lax.ppermute(x, 'head', swap) for x in mine]]
  transfers between devices with their start and end apart: 13 -> 13, of which waited for: 4 -> 3; matrix products, arithmetic and copies ran while one was open for 2% -> 2% of each run, Pallas kernels for 17% -> 20%
where the time goes in v5:
time: 54.1 us; the launch traced here: 53.8 us
  Pallas kernels  24.5 us (45%)
  starting transfers between devices  20.5 us (38%)
  waiting for transfers between devices  7.53 us (14%)
  local copies, waits for them, and re-layouts  0.81 us (1%)
    pallas_call x1, Pallas kernels, project(): pl.pallas_call(kernel, in_specs=[vmem] * (2 * count + 1) + [hbm] + [vmem]...  12.2 us
    ppermute x3, starting transfers between devices, shards(): far = [lax.ppermute(x, 'seq', two_on) for x in own[:-1]]  11.5 us
    pallas_call x4, Pallas kernels, attend(): pl.pallas_call(kernel, in_specs=specs, out_specs=[vmem] * len(outs), out_...  8.3 us
    ppermute x3, waiting for transfers between devices, shards(): lax.ppermute(jnp.where(odd, f, x), 'seq', pair)  4.59 us
    ppermute x3, starting transfers between devices, shards(): lax.ppermute(jnp.where(odd, f, x), 'seq', pair)  3.09 us
    ppermute x3, waiting for transfers between devices, shards(): far = [lax.ppermute(x, 'seq', two_on) for x in own[:-1]]  2.92 us
    ppermute x1, starting transfers between devices, shards(): last = lax.ppermute(last, 'seq', two_on)  2.73 us
    ppermute x1, starting transfers between devices, shards(): beside = lax.ppermute(own[-1], 'seq', pair)  1.58 us
  transfers between devices with their start and end apart: 13, of which 3 were waited for; matrix products, arithmetic and copies ran while one was open for 2% of the time, Pallas kernels for 20%

profile of v5, /device:TPU:0, one launch (start us, length us, event | category | flops | bytes accessed | tf_op | source)
XLA Modules:
  0.0 53.8 jit_solution(8190969368973669804)
XLA Ops:
  0.0 1.4 %shard_map.55 = (bf16[512,256]{1,0:T(8,128)(2,1)S(1)}, bf16[512,256]{1,0:T(8,128)(2,1)S(1)}, bf16[512,256]{1,0:T(8,128)(2,1)S(1)}, bf16[512,256]{1,0:T(8,128)(2,1)S(1)}) custom-call(bf16[512,512]{1,0:T(8,128)(2,1)} %keys_ref.1, bf16[512,512]{1,0:T(8,128)(2,1)} %values_ref.1), custom_call_target="tpu_custom_call" | custom-call | bytes 2097152 | tf_op jit(solution)/shard_map/pallas_call | solution.py:114
  1.4 0.5 collective-permute-start.8
  1.9 4.5 %collective-permute-start.1 = (bf16[512,256]{1,0:T(8,128)(2,1)S(1)}, bf16[512,256]{1,0:T(8,128)(2,1)S(1)}, u32[]{:S(2)}, u32[]{:S(2)}) collective-permute-start(bf16[512,256]{1,0:T(8,128)(2,1)S(1)} %get-tuple-element.30.own_ref), channel_id=1, source_target_pairs={{0,4},{2,6},{4,8},{6,10},{8,12},{10,14},{1,5},{3,7},{5,9},{7,11},{... | collective-permute-start | bytes 786440 | tf_op jit(solution)/shard_map/ppermute | solution.py:337
  6.4 1.6 %collective-permute-start.3 = (bf16[512,256]{1,0:T(8,128)(2,1)S(1)}, bf16[512,256]{1,0:T(8,128)(2,1)S(1)}, u32[]{:S(2)}, u32[]{:S(2)}) collective-permute-start(bf16[512,256]{1,0:T(8,128)(2,1)S(1)} %get-tuple-element.36.own_ref), channel_id=1, source_target_pairs={{0,2},{2,0},{4,6},{6,4},{8,10},{10,8},{12,14},{14,12},{1,3},{3,1},... | collective-permute-start | bytes 786440 | tf_op jit(solution)/shard_map/ppermute | solution.py:342
  8.0 3.5 %collective-permute-start = (bf16[512,256]{1,0:T(8,128)(2,1)S(1)}, bf16[512,256]{1,0:T(8,128)(2,1)S(1)}, u32[]{:S(2)}, u32[]{:S(2)}) collective-permute-start(bf16[512,256]{1,0:T(8,128)(2,1)S(1)} %get-tuple-element.28.own_ref), channel_id=1, source_target_pairs={{0,4},{2,6},{4,8},{6,10},{8,12},{10,14},{1,5},{3,7},{5,9},{7,11},{... | collective-permute-start | bytes 786440 | tf_op jit(solution)/shard_map/ppermute | solution.py:337
  11.5 3.5 %collective-permute-start.5 = (bf16[512,256]{1,0:T(8,128)(2,1)S(1)}, bf16[512,256]{1,0:T(8,128)(2,1)S(1)}, u32[]{:S(2)}, u32[]{:S(2)}) collective-permute-start(bf16[512,256]{1,0:T(8,128)(2,1)S(1)} %get-tuple-element.43.own_ref), channel_id=1, source_target_pairs={{0,4},{2,6},{4,8},{6,10},{8,12},{10,14},{1,5},{3,7},{5,9},{7,11},{... | collective-permute-start | bytes 786440 | tf_op jit(solution)/shard_map/ppermute | solution.py:337
  15.0 0.7 %reshape.7.seg_ref = s32[8,512]{1,0:T(8,128)S(1)} reshape(s32[4096]{0:T(1024)} %param.8) | data formatting | bytes 32768 | tf_op jit(solution)/shard_map/reshape | solution.py:158
  15.7 0.0 collective-permute-done.1.far_ref
  15.8 0.6 %collective-permute-start.2 = (bf16[512,256]{1,0:T(8,128)(2,1)S(1)}, bf16[512,256]{1,0:T(8,128)(2,1)S(1)}, u32[]{:S(2)}, u32[]{:S(2)}) collective-permute-start(bf16[512,256]{1,0:T(8,128)(2,1)S(1)} %broadcast_select_fusion.2), channel_id=1, source_target_pairs={{0,2},{2,0},{4,6},{6,4},{8,10},{10,8},{12,14},{14,12},{1,3},{3,1},... | collective-permute-start | bytes 786440 | tf_op jit(solution)/shard_map/ppermute | solution.py:341
  16.3 0.0 collective-permute-done.3
  16.4 2.7 %collective-permute-start.7 = (bf16[1024,256]{1,0:T(8,128)(2,1)S(1)}, bf16[1024,256]{1,0:T(8,128)(2,1)S(1)}, u32[]{:S(2)}, u32[]{:S(2)}) collective-permute-start(bf16[1024,256]{1,0:T(8,128)(2,1)S(1)} %pad_maximum_fusion), channel_id=1, source_target_pairs={{0,4},{2,6},{4,8},{6,10},{8,12},{10,14},{1,5},{3,7},{5,9},{7,11},{... | collective-permute-start | bytes 1572872 | tf_op jit(solution)/shard_map/ppermute | solution.py:344
  19.1 1.2 %shard_map.56 = (bf16[1536,128]{1,0:T(8,128)(2,1)S(1)}, bf16[512,1024]{1,0:T(8,128)(2,1)S(1)}) custom-call(s32[1]{0:T(128)} %bitcast.index_ref, s32[8,512]{1,0:T(8,128)S(1)} %reshape.7.seg_ref, bf16[512,1024]{1,0:T(8,128)(2,1)} %q_ref), custom_call_target="tpu_custom_call" | custom-call | flops 1024 | bytes 1024 | tf_op jit(solution)/shard_map/pallas_call | solution.py:143
  20.4 0.0 collective-permute-done.far_ref
  20.4 0.9 %collective-permute-start.4 = (bf16[512,256]{1,0:T(8,128)(2,1)S(1)}, bf16[512,256]{1,0:T(8,128)(2,1)S(1)}, u32[]{:S(2)}, u32[]{:S(2)}) collective-permute-start(bf16[512,256]{1,0:T(8,128)(2,1)S(1)} %broadcast_select_fusion.1), channel_id=1, source_target_pairs={{0,2},{2,0},{4,6},{6,4},{8,10},{10,8},{12,14},{14,12},{1,3},{3,1},... | collective-permute-start | bytes 786440 | tf_op jit(solution)/shard_map/ppermute | solution.py:341
  21.3 2.9 %collective-permute-done.5.far_ref = bf16[512,256]{1,0:T(8,128)(2,1)S(1)} collective-permute-done((bf16[512,256]{1,0:T(8,128)(2,1)S(1)}, bf16[512,256]{1,0:T(8,128)(2,1)S(1)}, u32[]{:S(2)}, u32[]{:S(2)}) %collective-permute-start.5) | collective-permute-done | bytes 262176 | tf_op jit(solution)/shard_map/ppermute | solution.py:337
  24.3 1.6 %collective-permute-start.6 = (bf16[512,256]{1,0:T(8,128)(2,1)S(1)}, bf16[512,256]{1,0:T(8,128)(2,1)S(1)}, u32[]{:S(2)}, u32[]{:S(2)}) collective-permute-start(bf16[512,256]{1,0:T(8,128)(2,1)S(1)} %broadcast_select_fusion), channel_id=1, source_target_pairs={{0,2},{2,0},{4,6},{6,4},{8,10},{10,8},{12,14},{14,12},{1,3},{3,1},... | collective-permute-start | bytes 786440 | tf_op jit(solution)/shard_map/ppermute | solution.py:341
  25.9 0.0 collective-permute-done.2.near_ref
  25.9 0.0 slice-start
  25.9 2.1 %shard_map.57.refs_0_ = bf16[512,256]{1,0:T(8,128)(2,1)S(1)} custom-call(bf16[512,1024]{1,0:T(8,128)(2,1)S(1)} %get-tuple-element.34.q_ref, bf16[1536,128]{1,0:T(8,128)(2,1)S(1)} %get-tuple-element.45.mark_ref, bf16[512,256]{1,0:T(8,128)(2,1)S(1)} %get-tuple-element.30.own_ref, bf16[512,256]{1,0:T(8,128)(2,1)S(1)} %collective-permute-done.2.near_ref, ...), custom_call_target="tpu_custom_call" | custom-call | flops 1024 | bytes 1024 | tf_op jit(solution)/shard_map/pallas_call | solution.py:200
  27.9 2.6 %collective-permute-done.4.near_ref = bf16[512,256]{1,0:T(8,128)(2,1)S(1)} collective-permute-done((bf16[512,256]{1,0:T(8,128)(2,1)S(1)}, bf16[512,256]{1,0:T(8,128)(2,1)S(1)}, u32[]{:S(2)}, u32[]{:S(2)}) %collective-permute-start.4) | collective-permute-done | bytes 262176 | tf_op jit(solution)/shard_map/ppermute | solution.py:341
  30.5 2.1 %shard_map.58.refs_1_ = bf16[512,256]{1,0:T(8,128)(2,1)S(1)} custom-call(bf16[512,1024]{1,0:T(8,128)(2,1)S(1)} %get-tuple-element.34.q_ref, bf16[1536,128]{1,0:T(8,128)(2,1)S(1)} %get-tuple-element.45.mark_ref, bf16[512,256]{1,0:T(8,128)(2,1)S(1)} %get-tuple-element.28.own_ref, bf16[512,256]{1,0:T(8,128)(2,1)S(1)} %collective-permute-done.4.near_ref, ...), custom_call_target="tpu_custom_call" | custom-call | flops 1024 | bytes 1024 | tf_op jit(solution)/shard_map/pallas_call | solution.py:200
  32.6 0.0 slice-start.1
  32.6 2.0 %collective-permute-done.6.near_ref = bf16[512,256]{1,0:T(8,128)(2,1)S(1)} collective-permute-done((bf16[512,256]{1,0:T(8,128)(2,1)S(1)}, bf16[512,256]{1,0:T(8,128)(2,1)S(1)}, u32[]{:S(2)}, u32[]{:S(2)}) %collective-permute-start.6) | collective-permute-done | bytes 262176 | tf_op jit(solution)/shard_map/ppermute | solution.py:341
  34.6 2.1 %shard_map.59.refs_2_ = bf16[512,256]{1,0:T(8,128)(2,1)S(1)} custom-call(bf16[512,1024]{1,0:T(8,128)(2,1)S(1)} %get-tuple-element.34.q_ref, bf16[1536,128]{1,0:T(8,128)(2,1)S(1)} %get-tuple-element.45.mark_ref, bf16[512,256]{1,0:T(8,128)(2,1)S(1)} %get-tuple-element.43.own_ref, bf16[512,256]{1,0:T(8,128)(2,1)S(1)} %collective-permute-done.6.near_ref, ...), custom_call_target="tpu_custom_call" | custom-call | flops 1024 | bytes 1024 | tf_op jit(solution)/shard_map/pallas_call | solution.py:200
  36.7 0.1 collective-permute-start.11
  36.8 0.5 collective-permute-start.10
  37.3 0.1 collective-permute-start.9
  37.4 0.0 collective-permute-done.7
  37.4 0.0 collective-permute-done.8.refs_0_.refs_9_
  37.4 0.0 slice-start.2
  37.4 2.1 %shard_map.60 = (bf16[512,256]{1,0:T(8,128)(2,1)S(1)}, bf16[1024,768]{1,0:T(8,128)(2,1)S(1)}, bf16[1024,768]{1,0:T(8,128)(2,1)S(1)}) custom-call(bf16[512,1024]{1,0:T(8,128)(2,1)S(1)} %get-tuple-element.34.q_ref, bf16[1536,128]{1,0:T(8,128)(2,1)S(1)} %get-tuple-element.45.mark_ref, bf16[512,256]{1,0:T(8,128)(2,1)S(1)} %get-tuple-element.36.own_ref, ...), custom_call_target="tpu_custom_call" | custom-call | flops 1024 | bytes 1024 | tf_op jit(solution)/shard_map/pallas_call | solution.py:200
  39.5 0.5 collective-permute-start.12
  40.0 0.0 collective-permute-done.11.refs_5_.refs_6_
  40.0 0.0 collective-permute-done.10.refs_4_.refs_5_
  40.0 0.0 collective-permute-done.9.refs_3_.refs_4_
  40.0 0.0 slice-done
  40.1 0.0 slice-done.1
  40.1 0.1 slice-done.2
  40.1 1.4 %shard_map.61.refs_10_ = f32[512,768]{1,0:T(8,128)S(1)} custom-call(bf16[512,256]{1,0:T(8,128)(2,1)S(1)} %shard_map.57.refs_0_, bf16[512,256]{1,0:T(8,128)(2,1)S(1)} %shard_map.58.refs_1_, bf16[512,256]{1,0:T(8,128)(2,1)S(1)} %shard_map.59.refs_2_, bf16[512,256]{1,0:T(8,128)(2,1)S(1)} %collective-permute-done.9.refs_3_.refs_4_, ...), custom_call_target="tpu_custom_call" | custom-call | flops 1207959552 | bytes 4194304 | tf_op jit(solution)/shard_map/pallas_call | solution.py:230
  41.5 0.0 collective-permute-done.12.refs_7_
  41.5 12.2 %shard_map.62 = bf16[512,5376]{1,0:T(8,128)(2,1)} custom-call(bf16[512,256]{1,0:T(8,128)(2,1)S(1)} %shard_map.57.refs_0_, bf16[512,256]{1,0:T(8,128)(2,1)S(1)} %shard_map.58.refs_1_, bf16[512,256]{1,0:T(8,128)(2,1)S(1)} %shard_map.59.refs_2_, bf16[512,256]{1,0:T(8,128)(2,1)S(1)} %get-tuple-element.48.refs_3_, ...), custom_call_target="tpu_custom_call" | custom-call | flops 11274289152 | bytes 33554432 | tf_op jit(solution)/shard_map/pallas_call | solution.py:304
  (6 shorter events, 0.2 us)
Async XLA Ops:
  1.4 36.0 %collective-permute-start.8 = (bf16[1024,5376]{1,0:T(8,128)(2,1)}, bf16[1024,5376]{1,0:T(8,128)(2,1)}, u32[]{:S(2)}, u32[]{:S(2)}) collective-permute-start(bf16[1024,5376]{1,0:T(8,128)(2,1)} %refs_8_), channel_id=1, source_target_pairs={{0,1},{1,0},{2,3},{3,2},{4,5},{5,4},{6,7},{7,6},{8,9},{9,8},{10,11... | collective-permute-start | bytes 33030152 | tf_op jit(solution)/shard_map/ppermute | solution.py:333
  1.9 13.8 %collective-permute-start.1 = (bf16[512,256]{1,0:T(8,128)(2,1)S(1)}, bf16[512,256]{1,0:T(8,128)(2,1)S(1)}, u32[]{:S(2)}, u32[]{:S(2)}) collective-permute-start(bf16[512,256]{1,0:T(8,128)(2,1)S(1)} %get-tuple-element.30.own_ref), channel_id=1, source_target_pairs={{0,4},{2,6},{4,8},{6,10},{8,12},{10,14},{1,5},{3,7},{5,9},{7,11},{... | collective-permute-start | bytes 786440 | tf_op jit(solution)/shard_map/ppermute | solution.py:337
  6.4 9.9 %collective-permute-start.3 = (bf16[512,256]{1,0:T(8,128)(2,1)S(1)}, bf16[512,256]{1,0:T(8,128)(2,1)S(1)}, u32[]{:S(2)}, u32[]{:S(2)}) collective-permute-start(bf16[512,256]{1,0:T(8,128)(2,1)S(1)} %get-tuple-element.36.own_ref), channel_id=1, source_target_pairs={{0,2},{2,0},{4,6},{6,4},{8,10},{10,8},{12,14},{14,12},{1,3},{3,1},... | collective-permute-start | bytes 786440 | tf_op jit(solution)/shard_map/ppermute | solution.py:342
  8.0 12.4 %collective-permute-start = (bf16[512,256]{1,0:T(8,128)(2,1)S(1)}, bf16[512,256]{1,0:T(8,128)(2,1)S(1)}, u32[]{:S(2)}, u32[]{:S(2)}) collective-permute-start(bf16[512,256]{1,0:T(8,128)(2,1)S(1)} %get-tuple-element.28.own_ref), channel_id=1, source_target_pairs={{0,4},{2,6},{4,8},{6,10},{8,12},{10,14},{1,5},{3,7},{5,9},{7,11},{... | collective-permute-start | bytes 786440 | tf_op jit(solution)/shard_map/ppermute | solution.py:337
  11.5 12.8 %collective-permute-start.5 = (bf16[512,256]{1,0:T(8,128)(2,1)S(1)}, bf16[512,256]{1,0:T(8,128)(2,1)S(1)}, u32[]{:S(2)}, u32[]{:S(2)}) collective-permute-start(bf16[512,256]{1,0:T(8,128)(2,1)S(1)} %get-tuple-element.43.own_ref), channel_id=1, source_target_pairs={{0,4},{2,6},{4,8},{6,10},{8,12},{10,14},{1,5},{3,7},{5,9},{7,11},{... | collective-permute-start | bytes 786440 | tf_op jit(solution)/shard_map/ppermute | solution.py:337
  15.8 10.1 %collective-permute-start.2 = (bf16[512,256]{1,0:T(8,128)(2,1)S(1)}, bf16[512,256]{1,0:T(8,128)(2,1)S(1)}, u32[]{:S(2)}, u32[]{:S(2)}) collective-permute-start(bf16[512,256]{1,0:T(8,128)(2,1)S(1)} %broadcast_select_fusion.2), channel_id=1, source_target_pairs={{0,2},{2,0},{4,6},{6,4},{8,10},{10,8},{12,14},{14,12},{1,3},{3,1},... | collective-permute-start | bytes 786440 | tf_op jit(solution)/shard_map/ppermute | solution.py:341
  16.4 21.0 %collective-permute-start.7 = (bf16[1024,256]{1,0:T(8,128)(2,1)S(1)}, bf16[1024,256]{1,0:T(8,128)(2,1)S(1)}, u32[]{:S(2)}, u32[]{:S(2)}) collective-permute-start(bf16[1024,256]{1,0:T(8,128)(2,1)S(1)} %pad_maximum_fusion), channel_id=1, source_target_pairs={{0,4},{2,6},{4,8},{6,10},{8,12},{10,14},{1,5},{3,7},{5,9},{7,11},{... | collective-permute-start | bytes 1572872 | tf_op jit(solution)/shard_map/ppermute | solution.py:344
  20.4 10.1 %collective-permute-start.4 = (bf16[512,256]{1,0:T(8,128)(2,1)S(1)}, bf16[512,256]{1,0:T(8,128)(2,1)S(1)}, u32[]{:S(2)}, u32[]{:S(2)}) collective-permute-start(bf16[512,256]{1,0:T(8,128)(2,1)S(1)} %broadcast_select_fusion.1), channel_id=1, source_target_pairs={{0,2},{2,0},{4,6},{6,4},{8,10},{10,8},{12,14},{14,12},{1,3},{3,1},... | collective-permute-start | bytes 786440 | tf_op jit(solution)/shard_map/ppermute | solution.py:341
  24.3 10.3 %collective-permute-start.6 = (bf16[512,256]{1,0:T(8,128)(2,1)S(1)}, bf16[512,256]{1,0:T(8,128)(2,1)S(1)}, u32[]{:S(2)}, u32[]{:S(2)}) collective-permute-start(bf16[512,256]{1,0:T(8,128)(2,1)S(1)} %broadcast_select_fusion), channel_id=1, source_target_pairs={{0,2},{2,0},{4,6},{6,4},{8,10},{10,8},{12,14},{14,12},{1,3},{3,1},... | collective-permute-start | bytes 786440 | tf_op jit(solution)/shard_map/ppermute | solution.py:341
  25.9 14.2 %slice-start = ((s8[11010048]{0:T(1024)(128)(4,1)}), s8[4194304]{0:T(1024)(128)(4,1)S(1)}, s32[]{:S(2)}) async-start(s8[11010048]{0:T(1024)(128)(4,1)} %bitcast.1), calls=%async_computation | async-start | bytes 8388608
  32.6 7.4 %slice-start.1 = ((s8[11010048]{0:T(1024)(128)(4,1)}), s8[4194304]{0:T(1024)(128)(4,1)S(1)}, s32[]{:S(2)}) async-start(s8[11010048]{0:T(1024)(128)(4,1)} %bitcast.1), calls=%async_computation.1 | async-start | bytes 8388608
  36.7 3.3 %collective-permute-start.11 = (bf16[512,256]{1,0:T(8,128)(2,1)S(1)}, bf16[512,256]{1,0:T(8,128)(2,1)S(1)}, u32[]{:S(2)}, u32[]{:S(2)}) collective-permute-start(bf16[512,256]{1,0:T(8,128)(2,1)S(1)} %shard_map.59.refs_2_), channel_id=1, source_target_pairs={{0,1},{1,0},{2,3},{3,2},{4,5},{5,4},{6,7},{7,6},{8,9},{9,8},{10,11... | collective-permute-start | bytes 786440 | tf_op jit(solution)/shard_map/ppermute | solution.py:356
  36.8 3.2 %collective-permute-start.10 = (bf16[512,256]{1,0:T(8,128)(2,1)S(1)}, bf16[512,256]{1,0:T(8,128)(2,1)S(1)}, u32[]{:S(2)}, u32[]{:S(2)}) collective-permute-start(bf16[512,256]{1,0:T(8,128)(2,1)S(1)} %shard_map.58.refs_1_), channel_id=1, source_target_pairs={{0,1},{1,0},{2,3},{3,2},{4,5},{5,4},{6,7},{7,6},{8,9},{9,8},{10,11... | collective-permute-start | bytes 786440 | tf_op jit(solution)/shard_map/ppermute | solution.py:356
  37.3 2.8 %collective-permute-start.9 = (bf16[512,256]{1,0:T(8,128)(2,1)S(1)}, bf16[512,256]{1,0:T(8,128)(2,1)S(1)}, u32[]{:S(2)}, u32[]{:S(2)}) collective-permute-start(bf16[512,256]{1,0:T(8,128)(2,1)S(1)} %shard_map.57.refs_0_), channel_id=1, source_target_pairs={{0,1},{1,0},{2,3},{3,2},{4,5},{5,4},{6,7},{7,6},{8,9},{9,8},{10,11... | collective-permute-start | bytes 786440 | tf_op jit(solution)/shard_map/ppermute | solution.py:356
  37.4 2.7 %slice-start.2 = ((s8[11010048]{0:T(1024)(128)(4,1)}), s8[2621440]{0:T(1024)(128)(4,1)S(1)}, s32[]{:S(2)}) async-start(s8[11010048]{0:T(1024)(128)(4,1)} %bitcast.1), calls=%async_computation.2 | async-start | bytes 5242880
  39.5 2.0 %collective-permute-start.12 = (bf16[512,256]{1,0:T(8,128)(2,1)S(1)}, bf16[512,256]{1,0:T(8,128)(2,1)S(1)}, u32[]{:S(2)}, u32[]{:S(2)}) collective-permute-start(bf16[512,256]{1,0:T(8,128)(2,1)S(1)} %get-tuple-element.48.refs_3_), channel_id=1, source_target_pairs={{0,1},{1,0},{2,3},{3,2},{4,5},{5,4},{6,7},{7,6},{8,9},{9,8},{10,11... | collective-permute-start | bytes 786440 | tf_op jit(solution)/shard_map/ppermute | solution.py:356

commit v6 on v5

--- a/solution.py
+++ b/solution.py
@@ -1,3 +1,5 @@
+import functools
+
 import jax
 import jax.numpy as jnp
 from jax import lax
@@ -39,7 +41,8 @@
     col = lax.broadcasted_iota(jnp.int32, (TILE, TILE), 1)
     inside = jnp.concatenate([col > row] * group, axis=0)
     causal = jnp.concatenate([col <= row] * group, axis=0)
-    for t in range(rows // TILE):
+
+    def score_tile(t):
         span = slice(t * TILE, (t + 1) * TILE)
         marks = mark_ref[2 * rows + t * TILE : 2 * rows + (t + 1) * TILE, :]
         query = jnp.concatenate(
@@ -49,31 +52,33 @@
             ],
             axis=0,
         )
-        parts = [
-            (keys[0][t * TILE :], values[0][t * TILE :]),
-            (keys[1], values[1]),
-            (keys[2][: (t + 1) * TILE], values[2][: (t + 1) * TILE]),
-        ]
+        parts = [keys[0][t * TILE :], keys[1], keys[2][: (t + 1) * TILE]]
         scores = [
             lax.dot_general(
                 query, key, (((1,), (1,)), ((), ())), preferred_element_type=jnp.float32
             )
-            for key, _ in parts
+            for key in parts
         ]
         first = jnp.where(inside, scores[0][:, :TILE], -1e30)
         scores[0] = joined(first, *([scores[0][:, TILE:]] if scores[0].shape[1] > TILE else []))
         last = jnp.where(causal, scores[2][:, t * TILE :], -1e30)
         scores[2] = joined(*([scores[2][:, : t * TILE]] if t else []), last)
-        top = jnp.maximum(
-            jnp.maximum(
-                jnp.max(scores[0], axis=1, keepdims=True),
-                jnp.max(scores[1], axis=1, keepdims=True),
-            ),
-            jnp.max(scores[2], axis=1, keepdims=True),
-        )
+        return scores
+
+    def weigh_tile(t, scores):
+        columns = [
+            score[:, c : c + HEAD_SIZE]
+            for score in scores
+            for c in range(0, score.shape[1], HEAD_SIZE)
+        ]
+        top = jnp.max(functools.reduce(jnp.maximum, columns), axis=1, keepdims=True)
+        return [jnp.exp2((score - top) * factor).astype(jnp.bfloat16) for score in scores]
+
+    def give_tile(t, weights):
+        span = slice(t * TILE, (t + 1) * TILE)
+        parts = [values[0][t * TILE :], values[1], values[2][: (t + 1) * TILE]]
         total = None
-        for score, (_, value) in zip(scores, parts):
-            weight = jnp.exp2((score - top) * factor).astype(jnp.bfloat16)
+        for weight, value in zip(weights, parts):
             term = jnp.dot(weight, value, preferred_element_type=jnp.float32)
             total = term if total is None else total + term
         result = (total[:, :HEAD_SIZE] / total[:, HEAD_SIZE:]).astype(jnp.bfloat16)
@@ -81,6 +86,12 @@
             out_ref[span, g * HEAD_SIZE : (g + 1) * HEAD_SIZE] = result[
                 g * TILE : (g + 1) * TILE
             ]
+
+    tiles = rows // TILE
+    scores = [score_tile(t) for t in range(tiles)]
+    weights = [weigh_tile(t, scores[t]) for t in range(tiles)]
+    for t in range(tiles):
+        give_tile(t, weights[t])
 
 
 def in_vmem(x):
@@ -208,6 +219,57 @@
     )(queries, marks, *[in_vmem(x) for x in part], *flat)
 
 
+def stage_kernel(in_ref, out_ref, sem, *, skip):
+    rows, columns = out_ref.shape
+    copy = pltpu.make_async_copy(in_ref.at[:rows, skip : skip + columns], out_ref, sem)
+    copy.start()
+    copy.wait()
+
+
+def stage(own_w):
+    depth, columns = own_w.shape
+    skip = column_tile(columns)
+    return pl.pallas_call(
+        functools.partial(stage_kernel, skip=skip),
+        in_specs=[pl.BlockSpec(memory_space=pltpu.HBM)],
+        out_specs=pl.BlockSpec(memory_space=pltpu.VMEM),
+        out_shape=pltpu.VMEM((depth // 2, columns - skip), own_w.dtype),
+        scratch_shapes=[pltpu.SemaphoreType.DMA],
+        compiler_params=pltpu.CompilerParams(vmem_limit_bytes=MIB),
+        cost_estimate=pl.CostEstimate(flops=1024, bytes_accessed=1024, transcendentals=0),
+    )(in_hbm(own_w))
+
+
+def project_own(own, upper_w, tile):
+    count = len(own)
+    rows, width = own[0].shape
+    columns = upper_w.shape[1]
+    depth = count * width
+
+    def kernel(*refs):
+        own_refs, (upper_w_ref, out_ref, row) = refs[:count], refs[count:]
+        for i, ref in enumerate(own_refs):
+            row[:, i * width : (i + 1) * width] = ref[...]
+
+        @pl.loop(0, columns // tile)
+        def _(n):
+            place = pl.ds(pl.multiple_of(n * tile, tile), tile)
+            out_ref[:, place] = jnp.dot(
+                row[...], upper_w_ref[:, place], preferred_element_type=jnp.float32
+            )
+
+    vmem = pl.BlockSpec(memory_space=pltpu.VMEM)
+    return pl.pallas_call(
+        kernel,
+        in_specs=[vmem] * (count + 1),
+        out_specs=vmem,
+        out_shape=pltpu.VMEM((rows, columns), jnp.float32),
+        scratch_shapes=[pltpu.VMEM((rows, depth), jnp.bfloat16)],
+        compiler_params=pltpu.CompilerParams(vmem_limit_bytes=6 * MIB),
+        cost_estimate=pl.CostEstimate(flops=1024, bytes_accessed=1024, transcendentals=0),
+    )(*[in_vmem(x) for x in own], upper_w)
+
+
 def project_early(own, other, own_w, ready):
     count = len(own)
     rows, width = own[0].shape
@@ -240,7 +302,7 @@
     )(*[in_vmem(x) for x in own + other], in_vmem(own_w), ready)
 
 
-def project(own, other, own_w, other_w, ready, base):
+def project(own, other, own_w, other_w, ready, base, own_base):
     count = len(own)
     rows = own[0].shape[0]
     depth, columns = own_w.shape
@@ -251,9 +313,9 @@
     def kernel(*refs):
         own_refs, other_refs = refs[:count], refs[count : 2 * count]
         own_w_ref, other_w_ref, *refs = refs[2 * count :]
-        base_ref, *refs = refs
+        base_ref, own_base_ref, *refs = refs
         ready_refs, refs = refs[: len(ready)], refs[len(ready) :]
-        out_ref, row, other_row, held, out_sem, w_buf, w_sem = refs
+        out_ref, row, other_row, other_base, held, out_sem, w_buf, w_sem = refs
 
         def place(n):
             return pl.ds(pl.multiple_of(n * tile, tile), tile)
@@ -267,19 +329,26 @@
             slot = n - len(ready)
             return tile_copy(other_w_ref, n, w_buf.at[slot], w_sem.at[slot])
 
-        def multiply(n, weight, base=None):
-            down = slice(0 if base is None else depth - own_refs[-1].shape[1], depth)
-            term = jnp.dot(
-                row[:, down], own_w_ref[down, place(n)], preferred_element_type=jnp.float32
+        def dot(array, weight, down, place=slice(None)):
+            return jnp.dot(
+                array[:, down], weight[down, place], preferred_element_type=jnp.float32
             )
-            other_term = jnp.dot(
-                other_row[:, down], weight[down, :], preferred_element_type=jnp.float32
-            )
-            total = term + other_term
-            if base is not None:
-                total = total + base[...]
+
+        def finish(n, total):
             held[:, place(n)] = total.astype(held.dtype)
             give(n).start()
+
+        def multiply_first(weight):
+            down = slice(depth - own_refs[-1].shape[1], depth)
+            total = dot(row, own_w_ref, down, place(0)) + dot(other_row, weight, down)
+            finish(0, total + base_ref[...])
+
+        def multiply(n, weight):
+            half, rest = slice(0, depth // 2), slice(depth // 2, depth)
+            other_base[...] = dot(other_row, weight, half)
+            term = own_base_ref[:, place(n - 1)] + dot(row, own_w_ref, rest, place(n))
+            other_term = other_base[...] + dot(other_row, weight, rest)
+            finish(n, term + other_term)
 
         for n in range(len(ready), tiles):
             coming(n).start()
@@ -288,7 +357,10 @@
                 width = ref.shape[1]
                 into[:, i * width : (i + 1) * width] = ref[...]
         for n, ref in enumerate(ready_refs):
-            multiply(n, ref, base_ref if n == 0 else None)
+            if n:
+                multiply(n, ref)
+            else:
+                multiply_first(ref)
 
         @pl.loop(len(ready), tiles)
         def _(n):
@@ -303,12 +375,13 @@
     hbm = pl.BlockSpec(memory_space=pltpu.HBM)
     return pl.pallas_call(
         kernel,
-        in_specs=[vmem] * (2 * count + 1) + [hbm] + [vmem] * (1 + len(ready)),
+        in_specs=[vmem] * (2 * count + 1) + [hbm] + [vmem] * (2 + len(ready)),
         out_specs=pl.BlockSpec(memory_space=pl.ANY),
         out_shape=jax.ShapeDtypeStruct((rows, columns), jnp.bfloat16),
         scratch_shapes=[
             pltpu.VMEM((rows, depth), jnp.bfloat16),
             pltpu.VMEM((rows, depth), jnp.bfloat16),
+            pltpu.VMEM((rows, tile), jnp.float32),
             pltpu.VMEM((rows, columns), jnp.bfloat16),
             pltpu.SemaphoreType.DMA((tiles,)),
             pltpu.VMEM((late, depth, tile), jnp.bfloat16),
@@ -318,7 +391,7 @@
         cost_estimate=pl.CostEstimate(
             flops=4 * rows * depth * columns, bytes_accessed=32 * MIB, transcendentals=0
         ),
-    )(*[in_vmem(x) for x in own + other], in_vmem(own_w), in_hbm(other_w), base, *ready)
+    )(*[in_vmem(x) for x in own + other], in_vmem(own_w), in_hbm(other_w), base, own_base, *ready)
 
 
 def shards(queries, keys, values, segments, out_weight):
@@ -338,6 +411,10 @@
     queries, far[0] = lax.optimization_barrier((queries, far[0]))
     marks, queries = prepare(seq_index.astype(jnp.int32).reshape(1), segments, queries)
     far[1], marks = lax.optimization_barrier((far[1], marks))
+    upper_w = out_weight
+    upper_w, marks = lax.optimization_barrier((upper_w, marks))
+    upper_w = stage(upper_w)
+    far[2], upper_w = lax.optimization_barrier((far[2], upper_w))
     near = [lax.ppermute(jnp.where(odd, f, x), "seq", pair) for f, x in zip(far, own)]
     beside = lax.ppermute(own[-1], "seq", pair)
     last, far[0] = lax.optimization_barrier((jnp.concatenate([own[-1], beside]), far[0]))
@@ -353,9 +430,12 @@
         result, *tile = attend(queries, marks, h, (own[h], near[h], far[h]), weights)
         mine.append(result)
         ready += tile
+        if h == heads_kv // 2 - 1:
+            own_base = project_own(mine, upper_w, column_tile(out_weight.shape[1]))
+            marks, own_base = lax.optimization_barrier((marks, own_base))
     theirs = [lax.ppermute(x, "head", swap) for x in mine]
     base = project_early(mine[:-1], theirs[:-1], out_weight, ready[0])
-    return project(mine, theirs, out_weight, other_w, ready, base)
+    return project(mine, theirs, out_weight, other_w, ready, base, own_base)
 
 
 def solution(mesh):

time: 54.1 us -> 52.8 us (0.976)
  waiting for transfers between devices: 7.53 us -> 3.34 us
  Pallas kernels: 24.5 us -> 27.4 us
    pallas_call x0 -> x2, Pallas kernels: none -> 5.85 us  [the longest x1 3.51 us: project_own(): pl.pallas_call(kernel, in_specs=[vmem] * (count + 1), out_specs=vmem, out...]
    ppermute x3, waiting for transfers between devices: 2.92 us -> 0.57 us  [shards(): far = [lax.ppermute(x, 'seq', two_on) for x in own[:-1]]]
    pallas_call x1, Pallas kernels: 12.2 us -> 9.95 us  [project(): pl.pallas_call(kernel, in_specs=[vmem] * (2 * count + 1) + [hbm] + [vmem]...]
    ppermute x3, waiting for transfers between devices: 4.59 us -> 2.75 us  [shards(): lax.ppermute(jnp.where(odd, f, x), 'seq', pair)]
    pallas_call x4, Pallas kernels: 8.3 us -> 7.58 us  [attend(): pl.pallas_call(kernel, in_specs=specs, out_specs=[vmem] * len(outs), out_...]
  transfers between devices with their start and end apart: 13 -> 13, of which waited for: 3 -> 2; matrix products, arithmetic and copies ran while one was open for 2% -> 2% of each run, Pallas kernels for 20% -> 31%
where the time goes in v6:
time: 52.8 us; the launch traced here: 52.5 us
  Pallas kernels  27.4 us (52%)
  starting transfers between devices  20.2 us (38%)
  waiting for transfers between devices  3.34 us (6%)
  local copies, waits for them, and re-layouts  1.17 us (2%)
    ppermute x3, starting transfers between devices, shards(): far = [lax.ppermute(x, 'seq', two_on) for x in own[:-1]]  11.5 us
    pallas_call x1, Pallas kernels, project(): pl.pallas_call(kernel, in_specs=[vmem] * (2 * count + 1) + [hbm] + [vmem]...  9.95 us
    pallas_call x4, Pallas kernels, attend(): pl.pallas_call(kernel, in_specs=specs, out_specs=[vmem] * len(outs), out_...  7.58 us
    pallas_call x1, Pallas kernels, project_own(): pl.pallas_call(kernel, in_specs=[vmem] * (count + 1), out_specs=vmem, out...  3.51 us
    ppermute x3, starting transfers between devices, shards(): lax.ppermute(jnp.where(odd, f, x), 'seq', pair)  3.09 us
    ppermute x3, waiting for transfers between devices, shards(): lax.ppermute(jnp.where(odd, f, x), 'seq', pair)  2.75 us
    ppermute x1, starting transfers between devices, shards(): last = lax.ppermute(last, 'seq', two_on)  2.73 us
    pallas_call x1, Pallas kernels, stage(): pl.pallas_call(functools.partial(stage_kernel, skip=skip), in_specs=[pl.B...  2.34 us
  transfers between devices with their start and end apart: 13, of which 2 were waited for; matrix products, arithmetic and copies ran while one was open for 2% of the time, Pallas kernels for 31%

profile of v6, /device:TPU:0, one launch (start us, length us, event | category | flops | bytes accessed | tf_op | source)
XLA Modules:
  0.0 52.5 jit_solution(125009309515356833)
XLA Ops:
  0.0 1.4 %shard_map.55 = (bf16[512,256]{1,0:T(8,128)(2,1)S(1)}, bf16[512,256]{1,0:T(8,128)(2,1)S(1)}, bf16[512,256]{1,0:T(8,128)(2,1)S(1)}, bf16[512,256]{1,0:T(8,128)(2,1)S(1)}) custom-call(bf16[512,512]{1,0:T(8,128)(2,1)} %keys_ref.1, bf16[512,512]{1,0:T(8,128)(2,1)} %values_ref.1), custom_call_target="tpu_custom_call" | custom-call | bytes 2097152 | tf_op jit(solution)/shard_map/pallas_call | solution.py:125
  1.4 0.5 collective-permute-start.8
  1.9 4.5 %collective-permute-start.1 = (bf16[512,256]{1,0:T(8,128)(2,1)S(1)}, bf16[512,256]{1,0:T(8,128)(2,1)S(1)}, u32[]{:S(2)}, u32[]{:S(2)}) collective-permute-start(bf16[512,256]{1,0:T(8,128)(2,1)S(1)} %get-tuple-element.37.own_ref), channel_id=1, source_target_pairs={{0,4},{2,6},{4,8},{6,10},{8,12},{10,14},{1,5},{3,7},{5,9},{7,11},{... | collective-permute-start | bytes 786440 | tf_op jit(solution)/shard_map/ppermute | solution.py:410
  6.4 1.6 %collective-permute-start.3 = (bf16[512,256]{1,0:T(8,128)(2,1)S(1)}, bf16[512,256]{1,0:T(8,128)(2,1)S(1)}, u32[]{:S(2)}, u32[]{:S(2)}) collective-permute-start(bf16[512,256]{1,0:T(8,128)(2,1)S(1)} %get-tuple-element.44.own_ref), channel_id=1, source_target_pairs={{0,2},{2,0},{4,6},{6,4},{8,10},{10,8},{12,14},{14,12},{1,3},{3,1},... | collective-permute-start | bytes 786440 | tf_op jit(solution)/shard_map/ppermute | solution.py:419
  8.0 3.5 %collective-permute-start = (bf16[512,256]{1,0:T(8,128)(2,1)S(1)}, bf16[512,256]{1,0:T(8,128)(2,1)S(1)}, u32[]{:S(2)}, u32[]{:S(2)}) collective-permute-start(bf16[512,256]{1,0:T(8,128)(2,1)S(1)} %get-tuple-element.36.own_ref), channel_id=1, source_target_pairs={{0,4},{2,6},{4,8},{6,10},{8,12},{10,14},{1,5},{3,7},{5,9},{7,11},{... | collective-permute-start | bytes 786440 | tf_op jit(solution)/shard_map/ppermute | solution.py:410
  11.5 3.5 %collective-permute-start.5 = (bf16[512,256]{1,0:T(8,128)(2,1)S(1)}, bf16[512,256]{1,0:T(8,128)(2,1)S(1)}, u32[]{:S(2)}, u32[]{:S(2)}) collective-permute-start(bf16[512,256]{1,0:T(8,128)(2,1)S(1)} %get-tuple-element.49.own_ref), channel_id=1, source_target_pairs={{0,4},{2,6},{4,8},{6,10},{8,12},{10,14},{1,5},{3,7},{5,9},{7,11},{... | collective-permute-start | bytes 786440 | tf_op jit(solution)/shard_map/ppermute | solution.py:410
  15.0 0.7 %reshape.7.seg_ref = s32[8,512]{1,0:T(8,128)S(1)} reshape(s32[4096]{0:T(1024)} %param.8) | data formatting | bytes 32768 | tf_op jit(solution)/shard_map/reshape | solution.py:169
  15.7 0.0 collective-permute-done.1.far_ref
  15.8 0.6 %collective-permute-start.2 = (bf16[512,256]{1,0:T(8,128)(2,1)S(1)}, bf16[512,256]{1,0:T(8,128)(2,1)S(1)}, u32[]{:S(2)}, u32[]{:S(2)}) collective-permute-start(bf16[512,256]{1,0:T(8,128)(2,1)S(1)} %broadcast_select_fusion.2), channel_id=1, source_target_pairs={{0,2},{2,0},{4,6},{6,4},{8,10},{10,8},{12,14},{14,12},{1,3},{3,1},... | collective-permute-start | bytes 786440 | tf_op jit(solution)/shard_map/ppermute | solution.py:418
  16.3 0.0 collective-permute-done.3
  16.4 2.7 %collective-permute-start.7 = (bf16[1024,256]{1,0:T(8,128)(2,1)S(1)}, bf16[1024,256]{1,0:T(8,128)(2,1)S(1)}, u32[]{:S(2)}, u32[]{:S(2)}) collective-permute-start(bf16[1024,256]{1,0:T(8,128)(2,1)S(1)} %pad_maximum_fusion), channel_id=1, source_target_pairs={{0,4},{2,6},{4,8},{6,10},{8,12},{10,14},{1,5},{3,7},{5,9},{7,11},{... | collective-permute-start | bytes 1572872 | tf_op jit(solution)/shard_map/ppermute | solution.py:421
  19.1 1.2 %shard_map.56 = (bf16[1536,128]{1,0:T(8,128)(2,1)S(1)}, bf16[512,1024]{1,0:T(8,128)(2,1)S(1)}) custom-call(s32[1]{0:T(128)} %bitcast.index_ref, s32[8,512]{1,0:T(8,128)S(1)} %reshape.7.seg_ref, bf16[512,1024]{1,0:T(8,128)(2,1)} %q_ref), custom_call_target="tpu_custom_call" | custom-call | flops 1024 | bytes 1024 | tf_op jit(solution)/shard_map/pallas_call | solution.py:154
  20.4 0.0 collective-permute-done.far_ref
  20.4 0.9 %collective-permute-start.4 = (bf16[512,256]{1,0:T(8,128)(2,1)S(1)}, bf16[512,256]{1,0:T(8,128)(2,1)S(1)}, u32[]{:S(2)}, u32[]{:S(2)}) collective-permute-start(bf16[512,256]{1,0:T(8,128)(2,1)S(1)} %broadcast_select_fusion.1), channel_id=1, source_target_pairs={{0,2},{2,0},{4,6},{6,4},{8,10},{10,8},{12,14},{14,12},{1,3},{3,1},... | collective-permute-start | bytes 786440 | tf_op jit(solution)/shard_map/ppermute | solution.py:418
  21.3 2.3 %shard_map.59.refs_2_ = bf16[512,4608]{1,0:T(8,128)(2,1)S(1)} custom-call(bf16[1024,5376]{1,0:T(8,128)(2,1)} %refs_8_), custom_call_target="tpu_custom_call" | custom-call | flops 1024 | bytes 1024 | tf_op jit(solution)/shard_map/pallas_call | solution.py:232
  23.7 0.6 %collective-permute-done.5.far_ref = bf16[512,256]{1,0:T(8,128)(2,1)S(1)} collective-permute-done((bf16[512,256]{1,0:T(8,128)(2,1)S(1)}, bf16[512,256]{1,0:T(8,128)(2,1)S(1)}, u32[]{:S(2)}, u32[]{:S(2)}) %collective-permute-start.5) | collective-permute-done | bytes 262176 | tf_op jit(solution)/shard_map/ppermute | solution.py:410
  24.3 1.6 %collective-permute-start.6 = (bf16[512,256]{1,0:T(8,128)(2,1)S(1)}, bf16[512,256]{1,0:T(8,128)(2,1)S(1)}, u32[]{:S(2)}, u32[]{:S(2)}) collective-permute-start(bf16[512,256]{1,0:T(8,128)(2,1)S(1)} %broadcast_select_fusion), channel_id=1, source_target_pairs={{0,2},{2,0},{4,6},{6,4},{8,10},{10,8},{12,14},{14,12},{1,3},{3,1},... | collective-permute-start | bytes 786440 | tf_op jit(solution)/shard_map/ppermute | solution.py:418
  25.9 0.0 collective-permute-done.2.near_ref
  25.9 1.8 %shard_map.57.refs_0_ = bf16[512,256]{1,0:T(8,128)(2,1)S(1)} custom-call(bf16[512,1024]{1,0:T(8,128)(2,1)S(1)} %get-tuple-element.42.q_ref, bf16[1536,128]{1,0:T(8,128)(2,1)S(1)} %get-tuple-element.57.mark_ref, bf16[512,256]{1,0:T(8,128)(2,1)S(1)} %get-tuple-element.37.own_ref, bf16[512,256]{1,0:T(8,128)(2,1)S(1)} %collective-permute-done.2.near_ref, ...), custom_call_target="tpu_custom_call" | custom-call | flops 1024 | bytes 1024 | tf_op jit(solution)/shard_map/pallas_call | solution.py:211
  27.7 0.1 collective-permute-start.9
  27.8 2.7 %collective-permute-done.4.near_ref = bf16[512,256]{1,0:T(8,128)(2,1)S(1)} collective-permute-done((bf16[512,256]{1,0:T(8,128)(2,1)S(1)}, bf16[512,256]{1,0:T(8,128)(2,1)S(1)}, u32[]{:S(2)}, u32[]{:S(2)}) %collective-permute-start.4) | collective-permute-done | bytes 262176 | tf_op jit(solution)/shard_map/ppermute | solution.py:418
  30.5 1.8 %shard_map.58.refs_1_ = bf16[512,256]{1,0:T(8,128)(2,1)S(1)} custom-call(bf16[512,1024]{1,0:T(8,128)(2,1)S(1)} %get-tuple-element.42.q_ref, bf16[1536,128]{1,0:T(8,128)(2,1)S(1)} %get-tuple-element.57.mark_ref, bf16[512,256]{1,0:T(8,128)(2,1)S(1)} %get-tuple-element.36.own_ref, bf16[512,256]{1,0:T(8,128)(2,1)S(1)} %collective-permute-done.4.near_ref, ...), custom_call_target="tpu_custom_call" | custom-call | flops 1024 | bytes 1024 | tf_op jit(solution)/shard_map/pallas_call | solution.py:211
  32.4 0.0 slice-start
  32.4 0.0 slice-start.1
  32.4 3.5 %shard_map.60.refs_11_ = f32[512,4608]{1,0:T(8,128)S(1)} custom-call(bf16[512,256]{1,0:T(8,128)(2,1)S(1)} %shard_map.57.refs_0_, bf16[512,256]{1,0:T(8,128)(2,1)S(1)} %shard_map.58.refs_1_, bf16[512,4608]{1,0:T(8,128)(2,1)S(1)} %shard_map.59.refs_2_), custom_call_target="tpu_custom_call" | custom-call | flops 1024 | bytes 1024 | tf_op jit(solution)/shard_map/pallas_call | solution.py:262
  35.9 0.0 collective-permute-done.6.near_ref
  35.9 1.8 %shard_map.61.refs_2_ = bf16[512,256]{1,0:T(8,128)(2,1)S(1)} custom-call(bf16[512,1024]{1,0:T(8,128)(2,1)S(1)} %get-tuple-element.42.q_ref, bf16[1536,128]{1,0:T(8,128)(2,1)S(1)} %get-tuple-element.57.mark_ref, bf16[512,256]{1,0:T(8,128)(2,1)S(1)} %get-tuple-element.49.own_ref, bf16[512,256]{1,0:T(8,128)(2,1)S(1)} %collective-permute-done.6.near_ref, ...), custom_call_target="tpu_custom_call" | custom-call | flops 1024 | bytes 1024 | tf_op jit(solution)/shard_map/pallas_call | solution.py:211
  37.8 0.1 collective-permute-start.11
  37.8 0.5 collective-permute-start.10
  38.3 0.0 collective-permute-done.7
  38.4 0.0 collective-permute-done.8.refs_0_.refs_9_
  38.4 0.0 slice-start.2
  38.4 2.1 %shard_map.62 = (bf16[512,256]{1,0:T(8,128)(2,1)S(1)}, bf16[1024,768]{1,0:T(8,128)(2,1)S(1)}, bf16[1024,768]{1,0:T(8,128)(2,1)S(1)}) custom-call(bf16[512,1024]{1,0:T(8,128)(2,1)S(1)} %get-tuple-element.42.q_ref, bf16[1536,128]{1,0:T(8,128)(2,1)S(1)} %get-tuple-element.57.mark_ref, bf16[512,256]{1,0:T(8,128)(2,1)S(1)} %get-tuple-element.44.own_ref, ...), custom_call_target="tpu_custom_call" | custom-call | flops 1024 | bytes 1024 | tf_op jit(solution)/shard_map/pallas_call | solution.py:211
  40.5 0.1 collective-permute-start.12
  40.6 0.0 collective-permute-done.9.refs_3_.refs_4_
  40.7 0.0 collective-permute-done.11.refs_5_.refs_6_
  40.7 0.0 collective-permute-done.10.refs_4_.refs_5_
  40.7 0.0 slice-done
  40.7 0.0 slice-done.1
  40.7 0.4 slice-done.2
  41.1 1.4 %shard_map.63.refs_10_ = f32[512,768]{1,0:T(8,128)S(1)} custom-call(bf16[512,256]{1,0:T(8,128)(2,1)S(1)} %shard_map.57.refs_0_, bf16[512,256]{1,0:T(8,128)(2,1)S(1)} %shard_map.58.refs_1_, bf16[512,256]{1,0:T(8,128)(2,1)S(1)} %shard_map.61.refs_2_, bf16[512,256]{1,0:T(8,128)(2,1)S(1)} %collective-permute-done.9.refs_3_.refs_4_, ...), custom_call_target="tpu_custom_call" | custom-call | flops 1207959552 | bytes 4194304 | tf_op jit(solution)/shard_map/pallas_call | solution.py:292
  42.5 0.0 collective-permute-done.12.refs_7_
  42.5 9.9 %shard_map.64 = bf16[512,5376]{1,0:T(8,128)(2,1)} custom-call(bf16[512,256]{1,0:T(8,128)(2,1)S(1)} %shard_map.57.refs_0_, bf16[512,256]{1,0:T(8,128)(2,1)S(1)} %shard_map.58.refs_1_, bf16[512,256]{1,0:T(8,128)(2,1)S(1)} %shard_map.61.refs_2_, bf16[512,256]{1,0:T(8,128)(2,1)S(1)} %get-tuple-element.59.refs_3_, ...), custom_call_target="tpu_custom_call" | custom-call | flops 11274289152 | bytes 33554432 | tf_op jit(solution)/shard_map/pallas_call | solution.py:376
  (6 shorter events, 0.2 us)
Async XLA Ops:
  1.4 37.0 %collective-permute-start.8 = (bf16[1024,5376]{1,0:T(8,128)(2,1)}, bf16[1024,5376]{1,0:T(8,128)(2,1)}, u32[]{:S(2)}, u32[]{:S(2)}) collective-permute-start(bf16[1024,5376]{1,0:T(8,128)(2,1)} %refs_8_), channel_id=1, source_target_pairs={{0,1},{1,0},{2,3},{3,2},{4,5},{5,4},{6,7},{7,6},{8,9},{9,8},{10,11... | collective-permute-start | bytes 33030152 | tf_op jit(solution)/shard_map/ppermute | solution.py:406
  1.9 13.8 %collective-permute-start.1 = (bf16[512,256]{1,0:T(8,128)(2,1)S(1)}, bf16[512,256]{1,0:T(8,128)(2,1)S(1)}, u32[]{:S(2)}, u32[]{:S(2)}) collective-permute-start(bf16[512,256]{1,0:T(8,128)(2,1)S(1)} %get-tuple-element.37.own_ref), channel_id=1, source_target_pairs={{0,4},{2,6},{4,8},{6,10},{8,12},{10,14},{1,5},{3,7},{5,9},{7,11},{... | collective-permute-start | bytes 786440 | tf_op jit(solution)/shard_map/ppermute | solution.py:410
  6.4 9.9 %collective-permute-start.3 = (bf16[512,256]{1,0:T(8,128)(2,1)S(1)}, bf16[512,256]{1,0:T(8,128)(2,1)S(1)}, u32[]{:S(2)}, u32[]{:S(2)}) collective-permute-start(bf16[512,256]{1,0:T(8,128)(2,1)S(1)} %get-tuple-element.44.own_ref), channel_id=1, source_target_pairs={{0,2},{2,0},{4,6},{6,4},{8,10},{10,8},{12,14},{14,12},{1,3},{3,1},... | collective-permute-start | bytes 786440 | tf_op jit(solution)/shard_map/ppermute | solution.py:419
  8.0 12.4 %collective-permute-start = (bf16[512,256]{1,0:T(8,128)(2,1)S(1)}, bf16[512,256]{1,0:T(8,128)(2,1)S(1)}, u32[]{:S(2)}, u32[]{:S(2)}) collective-permute-start(bf16[512,256]{1,0:T(8,128)(2,1)S(1)} %get-tuple-element.36.own_ref), channel_id=1, source_target_pairs={{0,4},{2,6},{4,8},{6,10},{8,12},{10,14},{1,5},{3,7},{5,9},{7,11},{... | collective-permute-start | bytes 786440 | tf_op jit(solution)/shard_map/ppermute | solution.py:410
  11.5 12.8 %collective-permute-start.5 = (bf16[512,256]{1,0:T(8,128)(2,1)S(1)}, bf16[512,256]{1,0:T(8,128)(2,1)S(1)}, u32[]{:S(2)}, u32[]{:S(2)}) collective-permute-start(bf16[512,256]{1,0:T(8,128)(2,1)S(1)} %get-tuple-element.49.own_ref), channel_id=1, source_target_pairs={{0,4},{2,6},{4,8},{6,10},{8,12},{10,14},{1,5},{3,7},{5,9},{7,11},{... | collective-permute-start | bytes 786440 | tf_op jit(solution)/shard_map/ppermute | solution.py:410
  15.8 10.1 %collective-permute-start.2 = (bf16[512,256]{1,0:T(8,128)(2,1)S(1)}, bf16[512,256]{1,0:T(8,128)(2,1)S(1)}, u32[]{:S(2)}, u32[]{:S(2)}) collective-permute-start(bf16[512,256]{1,0:T(8,128)(2,1)S(1)} %broadcast_select_fusion.2), channel_id=1, source_target_pairs={{0,2},{2,0},{4,6},{6,4},{8,10},{10,8},{12,14},{14,12},{1,3},{3,1},... | collective-permute-start | bytes 786440 | tf_op jit(solution)/shard_map/ppermute | solution.py:418
  16.4 22.0 %collective-permute-start.7 = (bf16[1024,256]{1,0:T(8,128)(2,1)S(1)}, bf16[1024,256]{1,0:T(8,128)(2,1)S(1)}, u32[]{:S(2)}, u32[]{:S(2)}) collective-permute-start(bf16[1024,256]{1,0:T(8,128)(2,1)S(1)} %pad_maximum_fusion), channel_id=1, source_target_pairs={{0,4},{2,6},{4,8},{6,10},{8,12},{10,14},{1,5},{3,7},{5,9},{7,11},{... | collective-permute-start | bytes 1572872 | tf_op jit(solution)/shard_map/ppermute | solution.py:421
  20.4 10.1 %collective-permute-start.4 = (bf16[512,256]{1,0:T(8,128)(2,1)S(1)}, bf16[512,256]{1,0:T(8,128)(2,1)S(1)}, u32[]{:S(2)}, u32[]{:S(2)}) collective-permute-start(bf16[512,256]{1,0:T(8,128)(2,1)S(1)} %broadcast_select_fusion.1), channel_id=1, source_target_pairs={{0,2},{2,0},{4,6},{6,4},{8,10},{10,8},{12,14},{14,12},{1,3},{3,1},... | collective-permute-start | bytes 786440 | tf_op jit(solution)/shard_map/ppermute | solution.py:418
  24.3 11.6 %collective-permute-start.6 = (bf16[512,256]{1,0:T(8,128)(2,1)S(1)}, bf16[512,256]{1,0:T(8,128)(2,1)S(1)}, u32[]{:S(2)}, u32[]{:S(2)}) collective-permute-start(bf16[512,256]{1,0:T(8,128)(2,1)S(1)} %broadcast_select_fusion), channel_id=1, source_target_pairs={{0,2},{2,0},{4,6},{6,4},{8,10},{10,8},{12,14},{14,12},{1,3},{3,1},... | collective-permute-start | bytes 786440 | tf_op jit(solution)/shard_map/ppermute | solution.py:418
  27.7 12.9 %collective-permute-start.9 = (bf16[512,256]{1,0:T(8,128)(2,1)S(1)}, bf16[512,256]{1,0:T(8,128)(2,1)S(1)}, u32[]{:S(2)}, u32[]{:S(2)}) collective-permute-start(bf16[512,256]{1,0:T(8,128)(2,1)S(1)} %shard_map.57.refs_0_), channel_id=1, source_target_pairs={{0,1},{1,0},{2,3},{3,2},{4,5},{5,4},{6,7},{7,6},{8,9},{9,8},{10,11... | collective-permute-start | bytes 786440 | tf_op jit(solution)/shard_map/ppermute | solution.py:436
  32.4 8.3 %slice-start = ((s8[11010048]{0:T(1024)(128)(4,1)}), s8[4194304]{0:T(1024)(128)(4,1)S(1)}, s32[]{:S(2)}) async-start(s8[11010048]{0:T(1024)(128)(4,1)} %bitcast.1), calls=%async_computation | async-start | bytes 8388608
  32.4 8.3 %slice-start.1 = ((s8[11010048]{0:T(1024)(128)(4,1)}), s8[4194304]{0:T(1024)(128)(4,1)S(1)}, s32[]{:S(2)}) async-start(s8[11010048]{0:T(1024)(128)(4,1)} %bitcast.1), calls=%async_computation.1 | async-start | bytes 8388608
  37.8 2.9 %collective-permute-start.11 = (bf16[512,256]{1,0:T(8,128)(2,1)S(1)}, bf16[512,256]{1,0:T(8,128)(2,1)S(1)}, u32[]{:S(2)}, u32[]{:S(2)}) collective-permute-start(bf16[512,256]{1,0:T(8,128)(2,1)S(1)} %shard_map.61.refs_2_), channel_id=1, source_target_pairs={{0,1},{1,0},{2,3},{3,2},{4,5},{5,4},{6,7},{7,6},{8,9},{9,8},{10,11... | collective-permute-start | bytes 786440 | tf_op jit(solution)/shard_map/ppermute | solution.py:436
  37.8 2.8 %collective-permute-start.10 = (bf16[512,256]{1,0:T(8,128)(2,1)S(1)}, bf16[512,256]{1,0:T(8,128)(2,1)S(1)}, u32[]{:S(2)}, u32[]{:S(2)}) collective-permute-start(bf16[512,256]{1,0:T(8,128)(2,1)S(1)} %shard_map.58.refs_1_), channel_id=1, source_target_pairs={{0,1},{1,0},{2,3},{3,2},{4,5},{5,4},{6,7},{7,6},{8,9},{9,8},{10,11... | collective-permute-start | bytes 786440 | tf_op jit(solution)/shard_map/ppermute | solution.py:436
  38.4 2.7 %slice-start.2 = ((s8[11010048]{0:T(1024)(128)(4,1)}), s8[2621440]{0:T(1024)(128)(4,1)S(1)}, s32[]{:S(2)}) async-start(s8[11010048]{0:T(1024)(128)(4,1)} %bitcast.1), calls=%async_computation.2 | async-start | bytes 5242880
  40.5 2.0 %collective-permute-start.12 = (bf16[512,256]{1,0:T(8,128)(2,1)S(1)}, bf16[512,256]{1,0:T(8,128)(2,1)S(1)}, u32[]{:S(2)}, u32[]{:S(2)}) collective-permute-start(bf16[512,256]{1,0:T(8,128)(2,1)S(1)} %get-tuple-element.59.refs_3_), channel_id=1, source_target_pairs={{0,1},{1,0},{2,3},{3,2},{4,5},{5,4},{6,7},{7,6},{8,9},{9,8},{10,11... | collective-permute-start | bytes 786440 | tf_op jit(solution)/shard_map/ppermute | solution.py:436

commit v7 on v6

--- a/solution.py
+++ b/solution.py
@@ -244,6 +244,7 @@
     count = len(own)
     rows, width = own[0].shape
     columns = upper_w.shape[1]
+    tile *= 2 if columns % (2 * tile) == 0 else 1
     depth = count * width
 
     def kernel(*refs):
@@ -265,7 +266,7 @@
         out_specs=vmem,
         out_shape=pltpu.VMEM((rows, columns), jnp.float32),
         scratch_shapes=[pltpu.VMEM((rows, depth), jnp.bfloat16)],
-        compiler_params=pltpu.CompilerParams(vmem_limit_bytes=6 * MIB),
+        compiler_params=pltpu.CompilerParams(vmem_limit_bytes=10 * MIB),
         cost_estimate=pl.CostEstimate(flops=1024, bytes_accessed=1024, transcendentals=0),
     )(*[in_vmem(x) for x in own], upper_w)
 
@@ -408,9 +409,8 @@
     pair = [(i, i ^ 1) for i in range(peers)]
     odd = seq_index % 2 == 1
     far = [lax.ppermute(x, "seq", two_on) for x in own[:-1]]
-    queries, far[0] = lax.optimization_barrier((queries, far[0]))
+    queries, segments, far[0] = lax.optimization_barrier((queries, segments, far[0]))
     marks, queries = prepare(seq_index.astype(jnp.int32).reshape(1), segments, queries)
-    far[1], marks = lax.optimization_barrier((far[1], marks))
     upper_w = out_weight
     upper_w, marks = lax.optimization_barrier((upper_w, marks))
     upper_w = stage(upper_w)

time: 52.8 us -> 52.4 us (level)
    ppermute x1, starting transfers between devices: 2.73 us -> 3.44 us  [shards(): last = lax.ppermute(last, 'seq', two_on)]
  transfers between devices with their start and end apart: 13 -> 13, of which waited for: 2 -> 2; matrix products, arithmetic and copies ran while one was open for 2% -> 2% of each run, Pallas kernels for 31% -> 30%
where the time goes in v7:
time: 52.4 us; the launch traced here: 52.1 us
  Pallas kernels  26.9 us (51%)
  starting transfers between devices  20.5 us (39%)
  waiting for transfers between devices  3.11 us (6%)
  local copies, waits for them, and re-layouts  1.17 us (2%)
    ppermute x3, starting transfers between devices, shards(): far = [lax.ppermute(x, 'seq', two_on) for x in own[:-1]]  11.5 us
    pallas_call x1, Pallas kernels, project(): pl.pallas_call(kernel, in_specs=[vmem] * (2 * count + 1) + [hbm] + [vmem]...  9.95 us
    pallas_call x4, Pallas kernels, attend(): pl.pallas_call(kernel, in_specs=specs, out_specs=[vmem] * len(outs), out_...  7.58 us
    ppermute x1, starting transfers between devices, shards(): last = lax.ppermute(last, 'seq', two_on)  3.44 us
    pallas_call x1, Pallas kernels, project_own(): pl.pallas_call(kernel, in_specs=[vmem] * (count + 1), out_specs=vmem, out...  2.99 us
    ppermute x3, waiting for transfers between devices, shards(): lax.ppermute(jnp.where(odd, f, x), 'seq', pair)  2.89 us
    ppermute x3, starting transfers between devices, shards(): lax.ppermute(jnp.where(odd, f, x), 'seq', pair)  2.73 us
    pallas_call x1, Pallas kernels, stage(): pl.pallas_call(functools.partial(stage_kernel, skip=skip), in_specs=[pl.B...  2.35 us
  transfers between devices with their start and end apart: 13, of which 2 were waited for; matrix products, arithmetic and copies ran while one was open for 2% of the time, Pallas kernels for 30%

profile of v7, /device:TPU:0, one launch (start us, length us, event | category | flops | bytes accessed | tf_op | source)
XLA Modules:
  0.0 52.1 jit_solution(3567141211395736743)
XLA Ops:
  0.0 1.4 %shard_map.55 = (bf16[512,256]{1,0:T(8,128)(2,1)S(1)}, bf16[512,256]{1,0:T(8,128)(2,1)S(1)}, bf16[512,256]{1,0:T(8,128)(2,1)S(1)}, bf16[512,256]{1,0:T(8,128)(2,1)S(1)}) custom-call(bf16[512,512]{1,0:T(8,128)(2,1)} %keys_ref.1, bf16[512,512]{1,0:T(8,128)(2,1)} %values_ref.1), custom_call_target="tpu_custom_call" | custom-call | bytes 2097152 | tf_op jit(solution)/shard_map/pallas_call | solution.py:125
  1.4 0.5 collective-permute-start.8
  1.9 4.5 %collective-permute-start = (bf16[512,256]{1,0:T(8,128)(2,1)S(1)}, bf16[512,256]{1,0:T(8,128)(2,1)S(1)}, u32[]{:S(2)}, u32[]{:S(2)}) collective-permute-start(bf16[512,256]{1,0:T(8,128)(2,1)S(1)} %get-tuple-element.35.own_ref), channel_id=1, source_target_pairs={{0,4},{2,6},{4,8},{6,10},{8,12},{10,14},{1,5},{3,7},{5,9},{7,11},{... | collective-permute-start | bytes 786440 | tf_op jit(solution)/shard_map/ppermute | solution.py:411
  6.4 1.6 %collective-permute-start.2 = (bf16[512,256]{1,0:T(8,128)(2,1)S(1)}, bf16[512,256]{1,0:T(8,128)(2,1)S(1)}, u32[]{:S(2)}, u32[]{:S(2)}) collective-permute-start(bf16[512,256]{1,0:T(8,128)(2,1)S(1)} %get-tuple-element.42.own_ref), channel_id=1, source_target_pairs={{0,2},{2,0},{4,6},{6,4},{8,10},{10,8},{12,14},{14,12},{1,3},{3,1},... | collective-permute-start | bytes 786440 | tf_op jit(solution)/shard_map/ppermute | solution.py:419
  8.0 3.5 %collective-permute-start.3 = (bf16[512,256]{1,0:T(8,128)(2,1)S(1)}, bf16[512,256]{1,0:T(8,128)(2,1)S(1)}, u32[]{:S(2)}, u32[]{:S(2)}) collective-permute-start(bf16[512,256]{1,0:T(8,128)(2,1)S(1)} %get-tuple-element.46.own_ref), channel_id=1, source_target_pairs={{0,4},{2,6},{4,8},{6,10},{8,12},{10,14},{1,5},{3,7},{5,9},{7,11},{... | collective-permute-start | bytes 786440 | tf_op jit(solution)/shard_map/ppermute | solution.py:411
  11.5 3.5 %collective-permute-start.5 = (bf16[512,256]{1,0:T(8,128)(2,1)S(1)}, bf16[512,256]{1,0:T(8,128)(2,1)S(1)}, u32[]{:S(2)}, u32[]{:S(2)}) collective-permute-start(bf16[512,256]{1,0:T(8,128)(2,1)S(1)} %get-tuple-element.47.own_ref), channel_id=1, source_target_pairs={{0,4},{2,6},{4,8},{6,10},{8,12},{10,14},{1,5},{3,7},{5,9},{7,11},{... | collective-permute-start | bytes 786440 | tf_op jit(solution)/shard_map/ppermute | solution.py:411
  15.0 0.0 collective-permute-done.far_ref
  15.0 0.7 %reshape.7.seg_ref = s32[8,512]{1,0:T(8,128)S(1)} reshape(s32[4096]{0:T(1024)} %param.8) | data formatting | bytes 32768 | tf_op jit(solution)/shard_map/reshape | solution.py:169
  15.8 0.6 %collective-permute-start.1 = (bf16[512,256]{1,0:T(8,128)(2,1)S(1)}, bf16[512,256]{1,0:T(8,128)(2,1)S(1)}, u32[]{:S(2)}, u32[]{:S(2)}) collective-permute-start(bf16[512,256]{1,0:T(8,128)(2,1)S(1)} %broadcast_select_fusion.2), channel_id=1, source_target_pairs={{0,2},{2,0},{4,6},{6,4},{8,10},{10,8},{12,14},{14,12},{1,3},{3,1},... | collective-permute-start | bytes 786440 | tf_op jit(solution)/shard_map/ppermute | solution.py:418
  16.3 0.0 collective-permute-done.2
  16.4 3.4 %collective-permute-start.7 = (bf16[1024,256]{1,0:T(8,128)(2,1)S(1)}, bf16[1024,256]{1,0:T(8,128)(2,1)S(1)}, u32[]{:S(2)}, u32[]{:S(2)}) collective-permute-start(bf16[1024,256]{1,0:T(8,128)(2,1)S(1)} %pad_maximum_fusion), channel_id=1, source_target_pairs={{0,4},{2,6},{4,8},{6,10},{8,12},{10,14},{1,5},{3,7},{5,9},{7,11},{... | collective-permute-start | bytes 1572872 | tf_op jit(solution)/shard_map/ppermute | solution.py:421
  19.8 0.0 collective-permute-done.3.far_ref
  19.9 0.6 %collective-permute-start.4 = (bf16[512,256]{1,0:T(8,128)(2,1)S(1)}, bf16[512,256]{1,0:T(8,128)(2,1)S(1)}, u32[]{:S(2)}, u32[]{:S(2)}) collective-permute-start(bf16[512,256]{1,0:T(8,128)(2,1)S(1)} %broadcast_select_fusion.1), channel_id=1, source_target_pairs={{0,2},{2,0},{4,6},{6,4},{8,10},{10,8},{12,14},{14,12},{1,3},{3,1},... | collective-permute-start | bytes 786440 | tf_op jit(solution)/shard_map/ppermute | solution.py:418
  20.4 1.2 %shard_map.56 = (bf16[1536,128]{1,0:T(8,128)(2,1)S(1)}, bf16[512,1024]{1,0:T(8,128)(2,1)S(1)}) custom-call(s32[1]{0:T(128)} %bitcast.index_ref, s32[8,512]{1,0:T(8,128)S(1)} %reshape.7.seg_ref, bf16[512,1024]{1,0:T(8,128)(2,1)} %q_ref), custom_call_target="tpu_custom_call" | custom-call | flops 1024 | bytes 1024 | tf_op jit(solution)/shard_map/pallas_call | solution.py:154
  21.7 2.3 %shard_map.59.refs_2_ = bf16[512,4608]{1,0:T(8,128)(2,1)S(1)} custom-call(bf16[1024,5376]{1,0:T(8,128)(2,1)} %refs_8_), custom_call_target="tpu_custom_call" | custom-call | flops 1024 | bytes 1024 | tf_op jit(solution)/shard_map/pallas_call | solution.py:232
  24.0 0.2 collective-permute-done.5.far_ref
  24.3 1.6 %collective-permute-start.6 = (bf16[512,256]{1,0:T(8,128)(2,1)S(1)}, bf16[512,256]{1,0:T(8,128)(2,1)S(1)}, u32[]{:S(2)}, u32[]{:S(2)}) collective-permute-start(bf16[512,256]{1,0:T(8,128)(2,1)S(1)} %broadcast_select_fusion), channel_id=1, source_target_pairs={{0,2},{2,0},{4,6},{6,4},{8,10},{10,8},{12,14},{14,12},{1,3},{3,1},... | collective-permute-start | bytes 786440 | tf_op jit(solution)/shard_map/ppermute | solution.py:418
  25.9 0.0 collective-permute-done.1.near_ref
  25.9 1.8 %shard_map.57.refs_0_ = bf16[512,256]{1,0:T(8,128)(2,1)S(1)} custom-call(bf16[512,1024]{1,0:T(8,128)(2,1)S(1)} %get-tuple-element.40.q_ref, bf16[1536,128]{1,0:T(8,128)(2,1)S(1)} %get-tuple-element.55.mark_ref, bf16[512,256]{1,0:T(8,128)(2,1)S(1)} %get-tuple-element.35.own_ref, bf16[512,256]{1,0:T(8,128)(2,1)S(1)} %collective-permute-done.1.near_ref, ...), custom_call_target="tpu_custom_call" | custom-call | flops 1024 | bytes 1024 | tf_op jit(solution)/shard_map/pallas_call | solution.py:211
  27.7 0.1 collective-permute-start.9
  27.8 2.9 %collective-permute-done.4.near_ref = bf16[512,256]{1,0:T(8,128)(2,1)S(1)} collective-permute-done((bf16[512,256]{1,0:T(8,128)(2,1)S(1)}, bf16[512,256]{1,0:T(8,128)(2,1)S(1)}, u32[]{:S(2)}, u32[]{:S(2)}) %collective-permute-start.4) | collective-permute-done | bytes 262176 | tf_op jit(solution)/shard_map/ppermute | solution.py:418
  30.7 1.8 %shard_map.58.refs_1_ = bf16[512,256]{1,0:T(8,128)(2,1)S(1)} custom-call(bf16[512,1024]{1,0:T(8,128)(2,1)S(1)} %get-tuple-element.40.q_ref, bf16[1536,128]{1,0:T(8,128)(2,1)S(1)} %get-tuple-element.55.mark_ref, bf16[512,256]{1,0:T(8,128)(2,1)S(1)} %get-tuple-element.46.own_ref, bf16[512,256]{1,0:T(8,128)(2,1)S(1)} %collective-permute-done.4.near_ref, ...), custom_call_target="tpu_custom_call" | custom-call | flops 1024 | bytes 1024 | tf_op jit(solution)/shard_map/pallas_call | solution.py:211
  32.5 0.0 slice-start
  32.5 0.0 slice-start.1
  32.5 3.0 %shard_map.60.refs_11_ = f32[512,4608]{1,0:T(8,128)S(1)} custom-call(bf16[512,256]{1,0:T(8,128)(2,1)S(1)} %shard_map.57.refs_0_, bf16[512,256]{1,0:T(8,128)(2,1)S(1)} %shard_map.58.refs_1_, bf16[512,4608]{1,0:T(8,128)(2,1)S(1)} %shard_map.59.refs_2_), custom_call_target="tpu_custom_call" | custom-call | flops 1024 | bytes 1024 | tf_op jit(solution)/shard_map/pallas_call | solution.py:263
  35.5 0.0 collective-permute-done.6.near_ref
  35.6 1.8 %shard_map.61.refs_2_ = bf16[512,256]{1,0:T(8,128)(2,1)S(1)} custom-call(bf16[512,1024]{1,0:T(8,128)(2,1)S(1)} %get-tuple-element.40.q_ref, bf16[1536,128]{1,0:T(8,128)(2,1)S(1)} %get-tuple-element.55.mark_ref, bf16[512,256]{1,0:T(8,128)(2,1)S(1)} %get-tuple-element.47.own_ref, bf16[512,256]{1,0:T(8,128)(2,1)S(1)} %collective-permute-done.6.near_ref, ...), custom_call_target="tpu_custom_call" | custom-call | flops 1024 | bytes 1024 | tf_op jit(solution)/shard_map/pallas_call | solution.py:211
  37.4 0.1 collective-permute-start.11
  37.5 0.5 collective-permute-start.10
  38.0 0.0 collective-permute-done.7
  38.0 0.0 collective-permute-done.8.refs_0_.refs_9_
  38.0 0.0 slice-start.2
  38.0 2.1 %shard_map.62 = (bf16[512,256]{1,0:T(8,128)(2,1)S(1)}, bf16[1024,768]{1,0:T(8,128)(2,1)S(1)}, bf16[1024,768]{1,0:T(8,128)(2,1)S(1)}) custom-call(bf16[512,1024]{1,0:T(8,128)(2,1)S(1)} %get-tuple-element.40.q_ref, bf16[1536,128]{1,0:T(8,128)(2,1)S(1)} %get-tuple-element.55.mark_ref, bf16[512,256]{1,0:T(8,128)(2,1)S(1)} %get-tuple-element.42.own_ref, ...), custom_call_target="tpu_custom_call" | custom-call | flops 1024 | bytes 1024 | tf_op jit(solution)/shard_map/pallas_call | solution.py:211
  40.1 0.1 collective-permute-start.12
  40.3 0.0 collective-permute-done.9.refs_3_.refs_4_
  40.3 0.0 collective-permute-done.11.refs_5_.refs_6_
  40.3 0.0 collective-permute-done.10.refs_4_.refs_5_
  40.3 0.0 slice-done
  40.3 0.0 slice-done.1
  40.3 0.4 slice-done.2
  40.7 1.4 %shard_map.63.refs_10_ = f32[512,768]{1,0:T(8,128)S(1)} custom-call(bf16[512,256]{1,0:T(8,128)(2,1)S(1)} %shard_map.57.refs_0_, bf16[512,256]{1,0:T(8,128)(2,1)S(1)} %shard_map.58.refs_1_, bf16[512,256]{1,0:T(8,128)(2,1)S(1)} %shard_map.61.refs_2_, bf16[512,256]{1,0:T(8,128)(2,1)S(1)} %collective-permute-done.9.refs_3_.refs_4_, ...), custom_call_target="tpu_custom_call" | custom-call | flops 1207959552 | bytes 4194304 | tf_op jit(solution)/shard_map/pallas_call | solution.py:293
  42.1 0.0 collective-permute-done.12.refs_7_
  42.1 9.9 %shard_map.64 = bf16[512,5376]{1,0:T(8,128)(2,1)} custom-call(bf16[512,256]{1,0:T(8,128)(2,1)S(1)} %shard_map.57.refs_0_, bf16[512,256]{1,0:T(8,128)(2,1)S(1)} %shard_map.58.refs_1_, bf16[512,256]{1,0:T(8,128)(2,1)S(1)} %shard_map.61.refs_2_, bf16[512,256]{1,0:T(8,128)(2,1)S(1)} %get-tuple-element.57.refs_3_, ...), custom_call_target="tpu_custom_call" | custom-call | flops 11274289152 | bytes 33554432 | tf_op jit(solution)/shard_map/pallas_call | solution.py:377
  (6 shorter events, 0.2 us)
Async XLA Ops:
  1.4 36.6 %collective-permute-start.8 = (bf16[1024,5376]{1,0:T(8,128)(2,1)}, bf16[1024,5376]{1,0:T(8,128)(2,1)}, u32[]{:S(2)}, u32[]{:S(2)}) collective-permute-start(bf16[1024,5376]{1,0:T(8,128)(2,1)} %refs_8_), channel_id=1, source_target_pairs={{0,1},{1,0},{2,3},{3,2},{4,5},{5,4},{6,7},{7,6},{8,9},{9,8},{10,11... | collective-permute-start | bytes 33030152 | tf_op jit(solution)/shard_map/ppermute | solution.py:407
  1.9 13.1 %collective-permute-start = (bf16[512,256]{1,0:T(8,128)(2,1)S(1)}, bf16[512,256]{1,0:T(8,128)(2,1)S(1)}, u32[]{:S(2)}, u32[]{:S(2)}) collective-permute-start(bf16[512,256]{1,0:T(8,128)(2,1)S(1)} %get-tuple-element.35.own_ref), channel_id=1, source_target_pairs={{0,4},{2,6},{4,8},{6,10},{8,12},{10,14},{1,5},{3,7},{5,9},{7,11},{... | collective-permute-start | bytes 786440 | tf_op jit(solution)/shard_map/ppermute | solution.py:411
  6.4 9.9 %collective-permute-start.2 = (bf16[512,256]{1,0:T(8,128)(2,1)S(1)}, bf16[512,256]{1,0:T(8,128)(2,1)S(1)}, u32[]{:S(2)}, u32[]{:S(2)}) collective-permute-start(bf16[512,256]{1,0:T(8,128)(2,1)S(1)} %get-tuple-element.42.own_ref), channel_id=1, source_target_pairs={{0,2},{2,0},{4,6},{6,4},{8,10},{10,8},{12,14},{14,12},{1,3},{3,1},... | collective-permute-start | bytes 786440 | tf_op jit(solution)/shard_map/ppermute | solution.py:419
  8.0 11.8 %collective-permute-start.3 = (bf16[512,256]{1,0:T(8,128)(2,1)S(1)}, bf16[512,256]{1,0:T(8,128)(2,1)S(1)}, u32[]{:S(2)}, u32[]{:S(2)}) collective-permute-start(bf16[512,256]{1,0:T(8,128)(2,1)S(1)} %get-tuple-element.46.own_ref), channel_id=1, source_target_pairs={{0,4},{2,6},{4,8},{6,10},{8,12},{10,14},{1,5},{3,7},{5,9},{7,11},{... | collective-permute-start | bytes 786440 | tf_op jit(solution)/shard_map/ppermute | solution.py:411
  11.5 12.8 %collective-permute-start.5 = (bf16[512,256]{1,0:T(8,128)(2,1)S(1)}, bf16[512,256]{1,0:T(8,128)(2,1)S(1)}, u32[]{:S(2)}, u32[]{:S(2)}) collective-permute-start(bf16[512,256]{1,0:T(8,128)(2,1)S(1)} %get-tuple-element.47.own_ref), channel_id=1, source_target_pairs={{0,4},{2,6},{4,8},{6,10},{8,12},{10,14},{1,5},{3,7},{5,9},{7,11},{... | collective-permute-start | bytes 786440 | tf_op jit(solution)/shard_map/ppermute | solution.py:411
  15.8 10.1 %collective-permute-start.1 = (bf16[512,256]{1,0:T(8,128)(2,1)S(1)}, bf16[512,256]{1,0:T(8,128)(2,1)S(1)}, u32[]{:S(2)}, u32[]{:S(2)}) collective-permute-start(bf16[512,256]{1,0:T(8,128)(2,1)S(1)} %broadcast_select_fusion.2), channel_id=1, source_target_pairs={{0,2},{2,0},{4,6},{6,4},{8,10},{10,8},{12,14},{14,12},{1,3},{3,1},... | collective-permute-start | bytes 786440 | tf_op jit(solution)/shard_map/ppermute | solution.py:418
  16.4 21.6 %collective-permute-start.7 = (bf16[1024,256]{1,0:T(8,128)(2,1)S(1)}, bf16[1024,256]{1,0:T(8,128)(2,1)S(1)}, u32[]{:S(2)}, u32[]{:S(2)}) collective-permute-start(bf16[1024,256]{1,0:T(8,128)(2,1)S(1)} %pad_maximum_fusion), channel_id=1, source_target_pairs={{0,4},{2,6},{4,8},{6,10},{8,12},{10,14},{1,5},{3,7},{5,9},{7,11},{... | collective-permute-start | bytes 1572872 | tf_op jit(solution)/shard_map/ppermute | solution.py:421
  19.9 10.8 %collective-permute-start.4 = (bf16[512,256]{1,0:T(8,128)(2,1)S(1)}, bf16[512,256]{1,0:T(8,128)(2,1)S(1)}, u32[]{:S(2)}, u32[]{:S(2)}) collective-permute-start(bf16[512,256]{1,0:T(8,128)(2,1)S(1)} %broadcast_select_fusion.1), channel_id=1, source_target_pairs={{0,2},{2,0},{4,6},{6,4},{8,10},{10,8},{12,14},{14,12},{1,3},{3,1},... | collective-permute-start | bytes 786440 | tf_op jit(solution)/shard_map/ppermute | solution.py:418
  24.3 11.3 %collective-permute-start.6 = (bf16[512,256]{1,0:T(8,128)(2,1)S(1)}, bf16[512,256]{1,0:T(8,128)(2,1)S(1)}, u32[]{:S(2)}, u32[]{:S(2)}) collective-permute-start(bf16[512,256]{1,0:T(8,128)(2,1)S(1)} %broadcast_select_fusion), channel_id=1, source_target_pairs={{0,2},{2,0},{4,6},{6,4},{8,10},{10,8},{12,14},{14,12},{1,3},{3,1},... | collective-permute-start | bytes 786440 | tf_op jit(solution)/shard_map/ppermute | solution.py:418
  27.7 12.6 %collective-permute-start.9 = (bf16[512,256]{1,0:T(8,128)(2,1)S(1)}, bf16[512,256]{1,0:T(8,128)(2,1)S(1)}, u32[]{:S(2)}, u32[]{:S(2)}) collective-permute-start(bf16[512,256]{1,0:T(8,128)(2,1)S(1)} %shard_map.57.refs_0_), channel_id=1, source_target_pairs={{0,1},{1,0},{2,3},{3,2},{4,5},{5,4},{6,7},{7,6},{8,9},{9,8},{10,11... | collective-permute-start | bytes 786440 | tf_op jit(solution)/shard_map/ppermute | solution.py:436
  32.5 7.8 %slice-start = ((s8[11010048]{0:T(1024)(128)(4,1)}), s8[4194304]{0:T(1024)(128)(4,1)S(1)}, s32[]{:S(2)}) async-start(s8[11010048]{0:T(1024)(128)(4,1)} %bitcast.1), calls=%async_computation | async-start | bytes 8388608
  32.5 7.8 %slice-start.1 = ((s8[11010048]{0:T(1024)(128)(4,1)}), s8[4194304]{0:T(1024)(128)(4,1)S(1)}, s32[]{:S(2)}) async-start(s8[11010048]{0:T(1024)(128)(4,1)} %bitcast.1), calls=%async_computation.1 | async-start | bytes 8388608
  37.4 2.9 %collective-permute-start.11 = (bf16[512,256]{1,0:T(8,128)(2,1)S(1)}, bf16[512,256]{1,0:T(8,128)(2,1)S(1)}, u32[]{:S(2)}, u32[]{:S(2)}) collective-permute-start(bf16[512,256]{1,0:T(8,128)(2,1)S(1)} %shard_map.61.refs_2_), channel_id=1, source_target_pairs={{0,1},{1,0},{2,3},{3,2},{4,5},{5,4},{6,7},{7,6},{8,9},{9,8},{10,11... | collective-permute-start | bytes 786440 | tf_op jit(solution)/shard_map/ppermute | solution.py:436
  37.5 2.8 %collective-permute-start.10 = (bf16[512,256]{1,0:T(8,128)(2,1)S(1)}, bf16[512,256]{1,0:T(8,128)(2,1)S(1)}, u32[]{:S(2)}, u32[]{:S(2)}) collective-permute-start(bf16[512,256]{1,0:T(8,128)(2,1)S(1)} %shard_map.58.refs_1_), channel_id=1, source_target_pairs={{0,1},{1,0},{2,3},{3,2},{4,5},{5,4},{6,7},{7,6},{8,9},{9,8},{10,11... | collective-permute-start | bytes 786440 | tf_op jit(solution)/shard_map/ppermute | solution.py:436
  38.0 2.7 %slice-start.2 = ((s8[11010048]{0:T(1024)(128)(4,1)}), s8[2621440]{0:T(1024)(128)(4,1)S(1)}, s32[]{:S(2)}) async-start(s8[11010048]{0:T(1024)(128)(4,1)} %bitcast.1), calls=%async_computation.2 | async-start | bytes 5242880
  40.1 2.0 %collective-permute-start.12 = (bf16[512,256]{1,0:T(8,128)(2,1)S(1)}, bf16[512,256]{1,0:T(8,128)(2,1)S(1)}, u32[]{:S(2)}, u32[]{:S(2)}) collective-permute-start(bf16[512,256]{1,0:T(8,128)(2,1)S(1)} %get-tuple-element.57.refs_3_), channel_id=1, source_target_pairs={{0,1},{1,0},{2,3},{3,2},{4,5},{5,4},{6,7},{7,6},{8,9},{9,8},{10,11... | collective-permute-start | bytes 786440 | tf_op jit(solution)/shard_map/ppermute | solution.py:436

commit v8 on v7

--- a/solution.py
+++ b/solution.py
@@ -141,13 +141,16 @@
     def kernel(index_ref, seg_ref, q_ref, mark_ref, q_out, sem):
         copy = pltpu.make_async_copy(q_ref, q_out, sem)
         copy.start()
-        ids = lax.broadcasted_iota(jnp.int32, (HEAD_SIZE, rows), 0)
+        ids = lax.broadcasted_iota(jnp.int32, (HEAD_SIZE, HEAD_SIZE), 0)
+        pieces = rows // HEAD_SIZE
         for b in range(blocks):
             block = index_ref[0] + b - (blocks - 1)
-            seen = seg_ref[pl.ds(jnp.maximum(block, 0), 1), :]
-            hit = (seen == ids) & (block >= 0)
-            mark = jnp.where(hit, MARK, 0.0)
-            mark_ref[b * rows : (b + 1) * rows, :] = mark.T.astype(jnp.bfloat16)
+            for p in range(pieces):
+                seen = seg_ref[pl.ds(jnp.maximum(block, 0) * pieces + p, 1), :]
+                hit = (seen == ids) & (block >= 0)
+                mark = jnp.where(hit, MARK, 0.0)
+                at = b * rows + p * HEAD_SIZE
+                mark_ref[at : at + HEAD_SIZE, :] = mark.T.astype(jnp.bfloat16)
         copy.wait()
 
     vmem = pl.BlockSpec(memory_space=pltpu.VMEM)
@@ -166,7 +169,7 @@
         scratch_shapes=[pltpu.SemaphoreType.DMA],
         compiler_params=pltpu.CompilerParams(vmem_limit_bytes=4 * MIB),
         cost_estimate=pl.CostEstimate(flops=1024, bytes_accessed=1024, transcendentals=0),
-    )(seq_index, segments.reshape(slab // rows, rows), in_hbm(queries))
+    )(seq_index, segments.reshape(slab // HEAD_SIZE, HEAD_SIZE), in_hbm(queries))
 
 
 def column_tile(columns):

time: 52.4 us -> 51.7 us (0.987)
  waiting for transfers between devices: 3.11 us -> 2.2 us
    reshape x1 -> x0, local copies, waits for them, and re-layouts: 0.72 us -> none  [prepare(): segments.reshape(slab // rows, rows)]
    ppermute x3, waiting for transfers between devices: 2.89 us -> 2.17 us  [shards(): lax.ppermute(jnp.where(odd, f, x), 'seq', pair)]
    unnamed x6 -> x8, local copies, waits for them, and re-layouts: 0.44 us -> 1.16 us
  transfers between devices with their start and end apart: 13 -> 13, of which waited for: 2 -> 1; matrix products, arithmetic and copies ran while one was open for 2% -> 0% of each run, Pallas kernels for 30% -> 30%
where the time goes in v8:
time: 51.7 us; the launch traced here: 51.4 us
  Pallas kernels  26.9 us (52%)
  starting transfers between devices  20.7 us (40%)
  waiting for transfers between devices  2.2 us (4%)
  local copies, waits for them, and re-layouts  1.16 us (2%)
    ppermute x3, starting transfers between devices, shards(): far = [lax.ppermute(x, 'seq', two_on) for x in own[:-1]]  11.5 us
    pallas_call x1, Pallas kernels, project(): pl.pallas_call(kernel, in_specs=[vmem] * (2 * count + 1) + [hbm] + [vmem]...  9.95 us
    pallas_call x4, Pallas kernels, attend(): pl.pallas_call(kernel, in_specs=specs, out_specs=[vmem] * len(outs), out_...  7.58 us
    ppermute x1, starting transfers between devices, shards(): last = lax.ppermute(last, 'seq', two_on)  3.44 us
    pallas_call x1, Pallas kernels, project_own(): pl.pallas_call(kernel, in_specs=[vmem] * (count + 1), out_specs=vmem, out...  2.99 us
    ppermute x3, starting transfers between devices, shards(): lax.ppermute(jnp.where(odd, f, x), 'seq', pair)  2.92 us
    pallas_call x1, Pallas kernels, stage(): pl.pallas_call(functools.partial(stage_kernel, skip=skip), in_specs=[pl.B...  2.35 us
    ppermute x3, waiting for transfers between devices, shards(): lax.ppermute(jnp.where(odd, f, x), 'seq', pair)  2.17 us
  transfers between devices with their start and end apart: 13, of which 1 were waited for; matrix products, arithmetic and copies ran while one was open for 0% of the time, Pallas kernels for 30%

profile of v8, /device:TPU:0, one launch (start us, length us, event | category | flops | bytes accessed | tf_op | source)
XLA Modules:
  0.0 51.4 jit_solution(10834915103081078936)
XLA Ops:
  0.0 1.4 %shard_map.55 = (bf16[512,256]{1,0:T(8,128)(2,1)S(1)}, bf16[512,256]{1,0:T(8,128)(2,1)S(1)}, bf16[512,256]{1,0:T(8,128)(2,1)S(1)}, bf16[512,256]{1,0:T(8,128)(2,1)S(1)}) custom-call(bf16[512,512]{1,0:T(8,128)(2,1)} %keys_ref.1, bf16[512,512]{1,0:T(8,128)(2,1)} %values_ref.1), custom_call_target="tpu_custom_call" | custom-call | bytes 2097152 | tf_op jit(solution)/shard_map/pallas_call | solution.py:125
  1.4 0.5 %collective-permute-start.8 = (bf16[1024,5376]{1,0:T(8,128)(2,1)}, bf16[1024,5376]{1,0:T(8,128)(2,1)}, u32[]{:S(2)}, u32[]{:S(2)}) collective-permute-start(bf16[1024,5376]{1,0:T(8,128)(2,1)} %refs_8_), channel_id=1, source_target_pairs={{0,1},{1,0},{2,3},{3,2},{4,5},{5,4},{6,7},{7,6},{8,9},{9,8},{10,11... | collective-permute-start | bytes 33030152 | tf_op jit(solution)/shard_map/ppermute | solution.py:410
  1.9 4.5 %collective-permute-start = (bf16[512,256]{1,0:T(8,128)(2,1)S(1)}, bf16[512,256]{1,0:T(8,128)(2,1)S(1)}, u32[]{:S(2)}, u32[]{:S(2)}) collective-permute-start(bf16[512,256]{1,0:T(8,128)(2,1)S(1)} %get-tuple-element.35.own_ref), channel_id=1, source_target_pairs={{0,4},{2,6},{4,8},{6,10},{8,12},{10,14},{1,5},{3,7},{5,9},{7,11},{... | collective-permute-start | bytes 786440 | tf_op jit(solution)/shard_map/ppermute | solution.py:414
  6.4 1.6 %collective-permute-start.2 = (bf16[512,256]{1,0:T(8,128)(2,1)S(1)}, bf16[512,256]{1,0:T(8,128)(2,1)S(1)}, u32[]{:S(2)}, u32[]{:S(2)}) collective-permute-start(bf16[512,256]{1,0:T(8,128)(2,1)S(1)} %get-tuple-element.42.own_ref), channel_id=1, source_target_pairs={{0,2},{2,0},{4,6},{6,4},{8,10},{10,8},{12,14},{14,12},{1,3},{3,1},... | collective-permute-start | bytes 786440 | tf_op jit(solution)/shard_map/ppermute | solution.py:422
  8.0 3.5 %collective-permute-start.3 = (bf16[512,256]{1,0:T(8,128)(2,1)S(1)}, bf16[512,256]{1,0:T(8,128)(2,1)S(1)}, u32[]{:S(2)}, u32[]{:S(2)}) collective-permute-start(bf16[512,256]{1,0:T(8,128)(2,1)S(1)} %get-tuple-element.46.own_ref), channel_id=1, source_target_pairs={{0,4},{2,6},{4,8},{6,10},{8,12},{10,14},{1,5},{3,7},{5,9},{7,11},{... | collective-permute-start | bytes 786440 | tf_op jit(solution)/shard_map/ppermute | solution.py:414
  11.5 3.5 %collective-permute-start.5 = (bf16[512,256]{1,0:T(8,128)(2,1)S(1)}, bf16[512,256]{1,0:T(8,128)(2,1)S(1)}, u32[]{:S(2)}, u32[]{:S(2)}) collective-permute-start(bf16[512,256]{1,0:T(8,128)(2,1)S(1)} %get-tuple-element.47.own_ref), channel_id=1, source_target_pairs={{0,4},{2,6},{4,8},{6,10},{8,12},{10,14},{1,5},{3,7},{5,9},{7,11},{... | collective-permute-start | bytes 786440 | tf_op jit(solution)/shard_map/ppermute | solution.py:414
  15.0 0.0 collective-permute-done.far_ref
  15.0 0.6 %collective-permute-start.1 = (bf16[512,256]{1,0:T(8,128)(2,1)S(1)}, bf16[512,256]{1,0:T(8,128)(2,1)S(1)}, u32[]{:S(2)}, u32[]{:S(2)}) collective-permute-start(bf16[512,256]{1,0:T(8,128)(2,1)S(1)} %broadcast_select_fusion.2), channel_id=1, source_target_pairs={{0,2},{2,0},{4,6},{6,4},{8,10},{10,8},{12,14},{14,12},{1,3},{3,1},... | collective-permute-start | bytes 786440 | tf_op jit(solution)/shard_map/ppermute | solution.py:421
  15.6 0.0 collective-permute-done.2
  15.7 3.4 %collective-permute-start.7 = (bf16[1024,256]{1,0:T(8,128)(2,1)S(1)}, bf16[1024,256]{1,0:T(8,128)(2,1)S(1)}, u32[]{:S(2)}, u32[]{:S(2)}) collective-permute-start(bf16[1024,256]{1,0:T(8,128)(2,1)S(1)} %pad_maximum_fusion), channel_id=1, source_target_pairs={{0,4},{2,6},{4,8},{6,10},{8,12},{10,14},{1,5},{3,7},{5,9},{7,11},{... | collective-permute-start | bytes 1572872 | tf_op jit(solution)/shard_map/ppermute | solution.py:424
  19.1 0.0 collective-permute-done.3.far_ref
  19.1 1.1 %collective-permute-start.4 = (bf16[512,256]{1,0:T(8,128)(2,1)S(1)}, bf16[512,256]{1,0:T(8,128)(2,1)S(1)}, u32[]{:S(2)}, u32[]{:S(2)}) collective-permute-start(bf16[512,256]{1,0:T(8,128)(2,1)S(1)} %broadcast_select_fusion.1), channel_id=1, source_target_pairs={{0,2},{2,0},{4,6},{6,4},{8,10},{10,8},{12,14},{14,12},{1,3},{3,1},... | collective-permute-start | bytes 786440 | tf_op jit(solution)/shard_map/ppermute | solution.py:421
  20.2 0.0 copy-start
  20.3 0.7 %copy-done = s32[4096]{0:T(1024)S(1)} copy-done((s32[4096]{0:T(1024)S(1)}, s32[4096]{0:T(1024)}, u32[]{:S(2)}) %copy-start) | copy-done | bytes 16408
  21.0 1.2 %shard_map.56 = (bf16[1536,128]{1,0:T(8,128)(2,1)S(1)}, bf16[512,1024]{1,0:T(8,128)(2,1)S(1)}) custom-call(s32[1]{0:T(128)} %bitcast.index_ref, s32[32,128]{1,0:T(8,128)S(1)} %bitcast.4, bf16[512,1024]{1,0:T(8,128)(2,1)} %q_ref), custom_call_target="tpu_custom_call" | custom-call | flops 1024 | bytes 1024 | tf_op jit(solution)/shard_map/pallas_call | solution.py:157
  22.2 2.3 %shard_map.59.refs_2_ = bf16[512,4608]{1,0:T(8,128)(2,1)S(1)} custom-call(bf16[1024,5376]{1,0:T(8,128)(2,1)} %refs_8_), custom_call_target="tpu_custom_call" | custom-call | flops 1024 | bytes 1024 | tf_op jit(solution)/shard_map/pallas_call | solution.py:235
  24.6 0.0 collective-permute-done.5.far_ref
  24.6 1.2 %collective-permute-start.6 = (bf16[512,256]{1,0:T(8,128)(2,1)S(1)}, bf16[512,256]{1,0:T(8,128)(2,1)S(1)}, u32[]{:S(2)}, u32[]{:S(2)}) collective-permute-start(bf16[512,256]{1,0:T(8,128)(2,1)S(1)} %broadcast_select_fusion), channel_id=1, source_target_pairs={{0,2},{2,0},{4,6},{6,4},{8,10},{10,8},{12,14},{14,12},{1,3},{3,1},... | collective-permute-start | bytes 786440 | tf_op jit(solution)/shard_map/ppermute | solution.py:421
  25.9 0.0 collective-permute-done.1.near_ref
  25.9 1.8 %shard_map.57.refs_0_ = bf16[512,256]{1,0:T(8,128)(2,1)S(1)} custom-call(bf16[512,1024]{1,0:T(8,128)(2,1)S(1)} %get-tuple-element.40.q_ref, bf16[1536,128]{1,0:T(8,128)(2,1)S(1)} %get-tuple-element.55.mark_ref, bf16[512,256]{1,0:T(8,128)(2,1)S(1)} %get-tuple-element.35.own_ref, bf16[512,256]{1,0:T(8,128)(2,1)S(1)} %collective-permute-done.1.near_ref, ...), custom_call_target="tpu_custom_call" | custom-call | flops 1024 | bytes 1024 | tf_op jit(solution)/shard_map/pallas_call | solution.py:214
  27.7 0.1 collective-permute-start.9
  27.8 2.2 %collective-permute-done.4.near_ref = bf16[512,256]{1,0:T(8,128)(2,1)S(1)} collective-permute-done((bf16[512,256]{1,0:T(8,128)(2,1)S(1)}, bf16[512,256]{1,0:T(8,128)(2,1)S(1)}, u32[]{:S(2)}, u32[]{:S(2)}) %collective-permute-start.4) | collective-permute-done | bytes 262176 | tf_op jit(solution)/shard_map/ppermute | solution.py:421
  30.0 1.8 %shard_map.58.refs_1_ = bf16[512,256]{1,0:T(8,128)(2,1)S(1)} custom-call(bf16[512,1024]{1,0:T(8,128)(2,1)S(1)} %get-tuple-element.40.q_ref, bf16[1536,128]{1,0:T(8,128)(2,1)S(1)} %get-tuple-element.55.mark_ref, bf16[512,256]{1,0:T(8,128)(2,1)S(1)} %get-tuple-element.46.own_ref, bf16[512,256]{1,0:T(8,128)(2,1)S(1)} %collective-permute-done.4.near_ref, ...), custom_call_target="tpu_custom_call" | custom-call | flops 1024 | bytes 1024 | tf_op jit(solution)/shard_map/pallas_call | solution.py:214
  31.8 0.0 slice-start
  31.8 0.0 slice-start.1
  31.8 3.0 %shard_map.60.refs_11_ = f32[512,4608]{1,0:T(8,128)S(1)} custom-call(bf16[512,256]{1,0:T(8,128)(2,1)S(1)} %shard_map.57.refs_0_, bf16[512,256]{1,0:T(8,128)(2,1)S(1)} %shard_map.58.refs_1_, bf16[512,4608]{1,0:T(8,128)(2,1)S(1)} %shard_map.59.refs_2_), custom_call_target="tpu_custom_call" | custom-call | flops 1024 | bytes 1024 | tf_op jit(solution)/shard_map/pallas_call | solution.py:266
  34.8 0.0 collective-permute-done.6.near_ref
  34.8 1.8 %shard_map.61.refs_2_ = bf16[512,256]{1,0:T(8,128)(2,1)S(1)} custom-call(bf16[512,1024]{1,0:T(8,128)(2,1)S(1)} %get-tuple-element.40.q_ref, bf16[1536,128]{1,0:T(8,128)(2,1)S(1)} %get-tuple-element.55.mark_ref, bf16[512,256]{1,0:T(8,128)(2,1)S(1)} %get-tuple-element.47.own_ref, bf16[512,256]{1,0:T(8,128)(2,1)S(1)} %collective-permute-done.6.near_ref, ...), custom_call_target="tpu_custom_call" | custom-call | flops 1024 | bytes 1024 | tf_op jit(solution)/shard_map/pallas_call | solution.py:214
  36.7 0.1 collective-permute-start.11
  36.7 0.5 collective-permute-start.10
  37.2 0.0 collective-permute-done.7
  37.3 0.0 collective-permute-done.8.refs_0_.refs_9_
  37.3 0.0 slice-start.2
  37.3 2.1 %shard_map.62 = (bf16[512,256]{1,0:T(8,128)(2,1)S(1)}, bf16[1024,768]{1,0:T(8,128)(2,1)S(1)}, bf16[1024,768]{1,0:T(8,128)(2,1)S(1)}) custom-call(bf16[512,1024]{1,0:T(8,128)(2,1)S(1)} %get-tuple-element.40.q_ref, bf16[1536,128]{1,0:T(8,128)(2,1)S(1)} %get-tuple-element.55.mark_ref, bf16[512,256]{1,0:T(8,128)(2,1)S(1)} %get-tuple-element.42.own_ref, ...), custom_call_target="tpu_custom_call" | custom-call | flops 1024 | bytes 1024 | tf_op jit(solution)/shard_map/pallas_call | solution.py:214
  39.4 0.1 collective-permute-start.12
  39.6 0.0 collective-permute-done.9.refs_3_.refs_4_
  39.6 0.0 collective-permute-done.11.refs_5_.refs_6_
  39.6 0.0 collective-permute-done.10.refs_4_.refs_5_
  39.6 0.0 slice-done
  39.6 0.0 slice-done.1
  39.6 0.4 slice-done.2
  40.0 1.4 %shard_map.63.refs_10_ = f32[512,768]{1,0:T(8,128)S(1)} custom-call(bf16[512,256]{1,0:T(8,128)(2,1)S(1)} %shard_map.57.refs_0_, bf16[512,256]{1,0:T(8,128)(2,1)S(1)} %shard_map.58.refs_1_, bf16[512,256]{1,0:T(8,128)(2,1)S(1)} %shard_map.61.refs_2_, bf16[512,256]{1,0:T(8,128)(2,1)S(1)} %collective-permute-done.9.refs_3_.refs_4_, ...), custom_call_target="tpu_custom_call" | custom-call | flops 1207959552 | bytes 4194304 | tf_op jit(solution)/shard_map/pallas_call | solution.py:296
  41.4 0.0 collective-permute-done.12.refs_7_
  41.4 9.9 %shard_map.64 = bf16[512,5376]{1,0:T(8,128)(2,1)} custom-call(bf16[512,256]{1,0:T(8,128)(2,1)S(1)} %shard_map.57.refs_0_, bf16[512,256]{1,0:T(8,128)(2,1)S(1)} %shard_map.58.refs_1_, bf16[512,256]{1,0:T(8,128)(2,1)S(1)} %shard_map.61.refs_2_, bf16[512,256]{1,0:T(8,128)(2,1)S(1)} %get-tuple-element.57.refs_3_, ...), custom_call_target="tpu_custom_call" | custom-call | flops 11274289152 | bytes 33554432 | tf_op jit(solution)/shard_map/pallas_call | solution.py:380
  (6 shorter events, 0.2 us)
Async XLA Ops:
  1.4 35.9 %collective-permute-start.8 = (bf16[1024,5376]{1,0:T(8,128)(2,1)}, bf16[1024,5376]{1,0:T(8,128)(2,1)}, u32[]{:S(2)}, u32[]{:S(2)}) collective-permute-start(bf16[1024,5376]{1,0:T(8,128)(2,1)} %refs_8_), channel_id=1, source_target_pairs={{0,1},{1,0},{2,3},{3,2},{4,5},{5,4},{6,7},{7,6},{8,9},{9,8},{10,11... | collective-permute-start | bytes 33030152 | tf_op jit(solution)/shard_map/ppermute | solution.py:410
  1.9 13.1 %collective-permute-start = (bf16[512,256]{1,0:T(8,128)(2,1)S(1)}, bf16[512,256]{1,0:T(8,128)(2,1)S(1)}, u32[]{:S(2)}, u32[]{:S(2)}) collective-permute-start(bf16[512,256]{1,0:T(8,128)(2,1)S(1)} %get-tuple-element.35.own_ref), channel_id=1, source_target_pairs={{0,4},{2,6},{4,8},{6,10},{8,12},{10,14},{1,5},{3,7},{5,9},{7,11},{... | collective-permute-start | bytes 786440 | tf_op jit(solution)/shard_map/ppermute | solution.py:414
  6.4 9.2 %collective-permute-start.2 = (bf16[512,256]{1,0:T(8,128)(2,1)S(1)}, bf16[512,256]{1,0:T(8,128)(2,1)S(1)}, u32[]{:S(2)}, u32[]{:S(2)}) collective-permute-start(bf16[512,256]{1,0:T(8,128)(2,1)S(1)} %get-tuple-element.42.own_ref), channel_id=1, source_target_pairs={{0,2},{2,0},{4,6},{6,4},{8,10},{10,8},{12,14},{14,12},{1,3},{3,1},... | collective-permute-start | bytes 786440 | tf_op jit(solution)/shard_map/ppermute | solution.py:422
  8.0 11.1 %collective-permute-start.3 = (bf16[512,256]{1,0:T(8,128)(2,1)S(1)}, bf16[512,256]{1,0:T(8,128)(2,1)S(1)}, u32[]{:S(2)}, u32[]{:S(2)}) collective-permute-start(bf16[512,256]{1,0:T(8,128)(2,1)S(1)} %get-tuple-element.46.own_ref), channel_id=1, source_target_pairs={{0,4},{2,6},{4,8},{6,10},{8,12},{10,14},{1,5},{3,7},{5,9},{7,11},{... | collective-permute-start | bytes 786440 | tf_op jit(solution)/shard_map/ppermute | solution.py:414
  11.5 13.1 %collective-permute-start.5 = (bf16[512,256]{1,0:T(8,128)(2,1)S(1)}, bf16[512,256]{1,0:T(8,128)(2,1)S(1)}, u32[]{:S(2)}, u32[]{:S(2)}) collective-permute-start(bf16[512,256]{1,0:T(8,128)(2,1)S(1)} %get-tuple-element.47.own_ref), channel_id=1, source_target_pairs={{0,4},{2,6},{4,8},{6,10},{8,12},{10,14},{1,5},{3,7},{5,9},{7,11},{... | collective-permute-start | bytes 786440 | tf_op jit(solution)/shard_map/ppermute | solution.py:414
  15.0 10.8 %collective-permute-start.1 = (bf16[512,256]{1,0:T(8,128)(2,1)S(1)}, bf16[512,256]{1,0:T(8,128)(2,1)S(1)}, u32[]{:S(2)}, u32[]{:S(2)}) collective-permute-start(bf16[512,256]{1,0:T(8,128)(2,1)S(1)} %broadcast_select_fusion.2), channel_id=1, source_target_pairs={{0,2},{2,0},{4,6},{6,4},{8,10},{10,8},{12,14},{14,12},{1,3},{3,1},... | collective-permute-start | bytes 786440 | tf_op jit(solution)/shard_map/ppermute | solution.py:421
  15.7 21.6 %collective-permute-start.7 = (bf16[1024,256]{1,0:T(8,128)(2,1)S(1)}, bf16[1024,256]{1,0:T(8,128)(2,1)S(1)}, u32[]{:S(2)}, u32[]{:S(2)}) collective-permute-start(bf16[1024,256]{1,0:T(8,128)(2,1)S(1)} %pad_maximum_fusion), channel_id=1, source_target_pairs={{0,4},{2,6},{4,8},{6,10},{8,12},{10,14},{1,5},{3,7},{5,9},{7,11},{... | collective-permute-start | bytes 1572872 | tf_op jit(solution)/shard_map/ppermute | solution.py:424
  19.1 10.8 %collective-permute-start.4 = (bf16[512,256]{1,0:T(8,128)(2,1)S(1)}, bf16[512,256]{1,0:T(8,128)(2,1)S(1)}, u32[]{:S(2)}, u32[]{:S(2)}) collective-permute-start(bf16[512,256]{1,0:T(8,128)(2,1)S(1)} %broadcast_select_fusion.1), channel_id=1, source_target_pairs={{0,2},{2,0},{4,6},{6,4},{8,10},{10,8},{12,14},{14,12},{1,3},{3,1},... | collective-permute-start | bytes 786440 | tf_op jit(solution)/shard_map/ppermute | solution.py:421
  20.2 0.7 %copy-start = (s32[4096]{0:T(1024)S(1)}, s32[4096]{0:T(1024)}, u32[]{:S(2)}) copy-start(s32[4096]{0:T(1024)} %param.8) | copy-start | bytes 49156
  24.6 10.2 %collective-permute-start.6 = (bf16[512,256]{1,0:T(8,128)(2,1)S(1)}, bf16[512,256]{1,0:T(8,128)(2,1)S(1)}, u32[]{:S(2)}, u32[]{:S(2)}) collective-permute-start(bf16[512,256]{1,0:T(8,128)(2,1)S(1)} %broadcast_select_fusion), channel_id=1, source_target_pairs={{0,2},{2,0},{4,6},{6,4},{8,10},{10,8},{12,14},{14,12},{1,3},{3,1},... | collective-permute-start | bytes 786440 | tf_op jit(solution)/shard_map/ppermute | solution.py:421
  27.7 11.8 %collective-permute-start.9 = (bf16[512,256]{1,0:T(8,128)(2,1)S(1)}, bf16[512,256]{1,0:T(8,128)(2,1)S(1)}, u32[]{:S(2)}, u32[]{:S(2)}) collective-permute-start(bf16[512,256]{1,0:T(8,128)(2,1)S(1)} %shard_map.57.refs_0_), channel_id=1, source_target_pairs={{0,1},{1,0},{2,3},{3,2},{4,5},{5,4},{6,7},{7,6},{8,9},{9,8},{10,11... | collective-permute-start | bytes 786440 | tf_op jit(solution)/shard_map/ppermute | solution.py:439
  31.8 7.8 %slice-start = ((s8[11010048]{0:T(1024)(128)(4,1)}), s8[4194304]{0:T(1024)(128)(4,1)S(1)}, s32[]{:S(2)}) async-start(s8[11010048]{0:T(1024)(128)(4,1)} %bitcast.2), calls=%async_computation | async-start | bytes 8388608
  31.8 7.8 %slice-start.1 = ((s8[11010048]{0:T(1024)(128)(4,1)}), s8[4194304]{0:T(1024)(128)(4,1)S(1)}, s32[]{:S(2)}) async-start(s8[11010048]{0:T(1024)(128)(4,1)} %bitcast.2), calls=%async_computation.1 | async-start | bytes 8388608
  36.7 2.9 %collective-permute-start.11 = (bf16[512,256]{1,0:T(8,128)(2,1)S(1)}, bf16[512,256]{1,0:T(8,128)(2,1)S(1)}, u32[]{:S(2)}, u32[]{:S(2)}) collective-permute-start(bf16[512,256]{1,0:T(8,128)(2,1)S(1)} %shard_map.61.refs_2_), channel_id=1, source_target_pairs={{0,1},{1,0},{2,3},{3,2},{4,5},{5,4},{6,7},{7,6},{8,9},{9,8},{10,11... | collective-permute-start | bytes 786440 | tf_op jit(solution)/shard_map/ppermute | solution.py:439
  36.7 2.8 %collective-permute-start.10 = (bf16[512,256]{1,0:T(8,128)(2,1)S(1)}, bf16[512,256]{1,0:T(8,128)(2,1)S(1)}, u32[]{:S(2)}, u32[]{:S(2)}) collective-permute-start(bf16[512,256]{1,0:T(8,128)(2,1)S(1)} %shard_map.58.refs_1_), channel_id=1, source_target_pairs={{0,1},{1,0},{2,3},{3,2},{4,5},{5,4},{6,7},{7,6},{8,9},{9,8},{10,11... | collective-permute-start | bytes 786440 | tf_op jit(solution)/shard_map/ppermute | solution.py:439
  37.3 2.7 %slice-start.2 = ((s8[11010048]{0:T(1024)(128)(4,1)}), s8[2621440]{0:T(1024)(128)(4,1)S(1)}, s32[]{:S(2)}) async-start(s8[11010048]{0:T(1024)(128)(4,1)} %bitcast.2), calls=%async_computation.2 | async-start | bytes 5242880
  39.4 2.0 %collective-permute-start.12 = (bf16[512,256]{1,0:T(8,128)(2,1)S(1)}, bf16[512,256]{1,0:T(8,128)(2,1)S(1)}, u32[]{:S(2)}, u32[]{:S(2)}) collective-permute-start(bf16[512,256]{1,0:T(8,128)(2,1)S(1)} %get-tuple-element.57.refs_3_), channel_id=1, source_target_pairs={{0,1},{1,0},{2,3},{3,2},{4,5},{5,4},{6,7},{7,6},{8,9},{9,8},{10,11... | collective-permute-start | bytes 786440 | tf_op jit(solution)/shard_map/ppermute | solution.py:439

commit v9 on v8

--- a/solution.py
+++ b/solution.py
@@ -255,9 +255,8 @@
         for i, ref in enumerate(own_refs):
             row[:, i * width : (i + 1) * width] = ref[...]
 
-        @pl.loop(0, columns // tile)
-        def _(n):
-            place = pl.ds(pl.multiple_of(n * tile, tile), tile)
+        for n in range(columns // tile):
+            place = slice(n * tile, (n + 1) * tile)
             out_ref[:, place] = jnp.dot(
                 row[...], upper_w_ref[:, place], preferred_element_type=jnp.float32
             )
@@ -400,6 +399,7 @@
 
 def shards(queries, keys, values, segments, out_weight):
     rows = queries.shape[0]
+    assert ATTENTION_SPAN == 2 * rows
     heads_kv = keys.shape[1] // HEAD_SIZE
     peers = lax.axis_size("seq")
     seq_index = lax.axis_index("seq")

time: 51.7 us -> 51.3 us (level)
  no operation moved by 1% of the time
where the time goes in v9:
time: 51.3 us; the launch traced here: 51 us
  Pallas kernels  26.5 us (52%)
  starting transfers between devices  20.7 us (40%)
  waiting for transfers between devices  2.2 us (4%)
  local copies, waits for them, and re-layouts  1.16 us (2%)
    ppermute x3, starting transfers between devices, shards(): far = [lax.ppermute(x, 'seq', two_on) for x in own[:-1]]  11.5 us
    pallas_call x1, Pallas kernels, project(): pl.pallas_call(kernel, in_specs=[vmem] * (2 * count + 1) + [hbm] + [vmem]...  9.95 us
    pallas_call x4, Pallas kernels, attend(): pl.pallas_call(kernel, in_specs=specs, out_specs=[vmem] * len(outs), out_...  7.58 us
    ppermute x1, starting transfers between devices, shards(): last = lax.ppermute(last, 'seq', two_on)  3.44 us
    ppermute x3, starting transfers between devices, shards(): lax.ppermute(jnp.where(odd, f, x), 'seq', pair)  2.92 us
    pallas_call x1, Pallas kernels, project_own(): pl.pallas_call(kernel, in_specs=[vmem] * (count + 1), out_specs=vmem, out...  2.62 us
    pallas_call x1, Pallas kernels, stage(): pl.pallas_call(functools.partial(stage_kernel, skip=skip), in_specs=[pl.B...  2.35 us
    ppermute x3, waiting for transfers between devices, shards(): lax.ppermute(jnp.where(odd, f, x), 'seq', pair)  2.17 us
  transfers between devices with their start and end apart: 13, of which 1 were waited for; matrix products, arithmetic and copies ran while one was open for 0% of the time, Pallas kernels for 30%

profile of v9, /device:TPU:0, one launch (start us, length us, event | category | flops | bytes accessed | tf_op | source)
XLA Modules:
  0.0 51.0 jit_solution(8642509984207490942)
XLA Ops:
  0.0 1.4 %shard_map.55 = (bf16[512,256]{1,0:T(8,128)(2,1)S(1)}, bf16[512,256]{1,0:T(8,128)(2,1)S(1)}, bf16[512,256]{1,0:T(8,128)(2,1)S(1)}, bf16[512,256]{1,0:T(8,128)(2,1)S(1)}) custom-call(bf16[512,512]{1,0:T(8,128)(2,1)} %keys_ref.1, bf16[512,512]{1,0:T(8,128)(2,1)} %values_ref.1), custom_call_target="tpu_custom_call" | custom-call | bytes 2097152 | tf_op jit(solution)/shard_map/pallas_call | solution.py:125
  1.4 0.5 %collective-permute-start.8 = (bf16[1024,5376]{1,0:T(8,128)(2,1)}, bf16[1024,5376]{1,0:T(8,128)(2,1)}, u32[]{:S(2)}, u32[]{:S(2)}) collective-permute-start(bf16[1024,5376]{1,0:T(8,128)(2,1)} %refs_8_), channel_id=1, source_target_pairs={{0,1},{1,0},{2,3},{3,2},{4,5},{5,4},{6,7},{7,6},{8,9},{9,8},{10,11... | collective-permute-start | bytes 33030152 | tf_op jit(solution)/shard_map/ppermute | solution.py:410
  1.9 4.5 %collective-permute-start = (bf16[512,256]{1,0:T(8,128)(2,1)S(1)}, bf16[512,256]{1,0:T(8,128)(2,1)S(1)}, u32[]{:S(2)}, u32[]{:S(2)}) collective-permute-start(bf16[512,256]{1,0:T(8,128)(2,1)S(1)} %get-tuple-element.35.own_ref), channel_id=1, source_target_pairs={{0,4},{2,6},{4,8},{6,10},{8,12},{10,14},{1,5},{3,7},{5,9},{7,11},{... | collective-permute-start | bytes 786440 | tf_op jit(solution)/shard_map/ppermute | solution.py:414
  6.4 1.6 %collective-permute-start.2 = (bf16[512,256]{1,0:T(8,128)(2,1)S(1)}, bf16[512,256]{1,0:T(8,128)(2,1)S(1)}, u32[]{:S(2)}, u32[]{:S(2)}) collective-permute-start(bf16[512,256]{1,0:T(8,128)(2,1)S(1)} %get-tuple-element.42.own_ref), channel_id=1, source_target_pairs={{0,2},{2,0},{4,6},{6,4},{8,10},{10,8},{12,14},{14,12},{1,3},{3,1},... | collective-permute-start | bytes 786440 | tf_op jit(solution)/shard_map/ppermute | solution.py:422
  8.0 3.5 %collective-permute-start.3 = (bf16[512,256]{1,0:T(8,128)(2,1)S(1)}, bf16[512,256]{1,0:T(8,128)(2,1)S(1)}, u32[]{:S(2)}, u32[]{:S(2)}) collective-permute-start(bf16[512,256]{1,0:T(8,128)(2,1)S(1)} %get-tuple-element.46.own_ref), channel_id=1, source_target_pairs={{0,4},{2,6},{4,8},{6,10},{8,12},{10,14},{1,5},{3,7},{5,9},{7,11},{... | collective-permute-start | bytes 786440 | tf_op jit(solution)/shard_map/ppermute | solution.py:414
  11.5 3.5 %collective-permute-start.5 = (bf16[512,256]{1,0:T(8,128)(2,1)S(1)}, bf16[512,256]{1,0:T(8,128)(2,1)S(1)}, u32[]{:S(2)}, u32[]{:S(2)}) collective-permute-start(bf16[512,256]{1,0:T(8,128)(2,1)S(1)} %get-tuple-element.47.own_ref), channel_id=1, source_target_pairs={{0,4},{2,6},{4,8},{6,10},{8,12},{10,14},{1,5},{3,7},{5,9},{7,11},{... | collective-permute-start | bytes 786440 | tf_op jit(solution)/shard_map/ppermute | solution.py:414
  15.0 0.0 collective-permute-done.far_ref
  15.0 0.6 %collective-permute-start.1 = (bf16[512,256]{1,0:T(8,128)(2,1)S(1)}, bf16[512,256]{1,0:T(8,128)(2,1)S(1)}, u32[]{:S(2)}, u32[]{:S(2)}) collective-permute-start(bf16[512,256]{1,0:T(8,128)(2,1)S(1)} %broadcast_select_fusion.2), channel_id=1, source_target_pairs={{0,2},{2,0},{4,6},{6,4},{8,10},{10,8},{12,14},{14,12},{1,3},{3,1},... | collective-permute-start | bytes 786440 | tf_op jit(solution)/shard_map/ppermute | solution.py:421
  15.6 0.0 collective-permute-done.2
  15.7 3.4 %collective-permute-start.7 = (bf16[1024,256]{1,0:T(8,128)(2,1)S(1)}, bf16[1024,256]{1,0:T(8,128)(2,1)S(1)}, u32[]{:S(2)}, u32[]{:S(2)}) collective-permute-start(bf16[1024,256]{1,0:T(8,128)(2,1)S(1)} %pad_maximum_fusion), channel_id=1, source_target_pairs={{0,4},{2,6},{4,8},{6,10},{8,12},{10,14},{1,5},{3,7},{5,9},{7,11},{... | collective-permute-start | bytes 1572872 | tf_op jit(solution)/shard_map/ppermute | solution.py:424
  19.1 0.0 collective-permute-done.3.far_ref
  19.1 1.1 %collective-permute-start.4 = (bf16[512,256]{1,0:T(8,128)(2,1)S(1)}, bf16[512,256]{1,0:T(8,128)(2,1)S(1)}, u32[]{:S(2)}, u32[]{:S(2)}) collective-permute-start(bf16[512,256]{1,0:T(8,128)(2,1)S(1)} %broadcast_select_fusion.1), channel_id=1, source_target_pairs={{0,2},{2,0},{4,6},{6,4},{8,10},{10,8},{12,14},{14,12},{1,3},{3,1},... | collective-permute-start | bytes 786440 | tf_op jit(solution)/shard_map/ppermute | solution.py:421
  20.2 0.0 copy-start
  20.3 0.7 %copy-done = s32[4096]{0:T(1024)S(1)} copy-done((s32[4096]{0:T(1024)S(1)}, s32[4096]{0:T(1024)}, u32[]{:S(2)}) %copy-start) | copy-done | bytes 16408
  21.0 1.2 %shard_map.56 = (bf16[1536,128]{1,0:T(8,128)(2,1)S(1)}, bf16[512,1024]{1,0:T(8,128)(2,1)S(1)}) custom-call(s32[1]{0:T(128)} %bitcast.index_ref, s32[32,128]{1,0:T(8,128)S(1)} %bitcast.4, bf16[512,1024]{1,0:T(8,128)(2,1)} %q_ref), custom_call_target="tpu_custom_call" | custom-call | flops 1024 | bytes 1024 | tf_op jit(solution)/shard_map/pallas_call | solution.py:157
  22.2 2.3 %shard_map.59.refs_2_ = bf16[512,4608]{1,0:T(8,128)(2,1)S(1)} custom-call(bf16[1024,5376]{1,0:T(8,128)(2,1)} %refs_8_), custom_call_target="tpu_custom_call" | custom-call | flops 1024 | bytes 1024 | tf_op jit(solution)/shard_map/pallas_call | solution.py:235
  24.6 0.0 collective-permute-done.5.far_ref
  24.6 1.2 %collective-permute-start.6 = (bf16[512,256]{1,0:T(8,128)(2,1)S(1)}, bf16[512,256]{1,0:T(8,128)(2,1)S(1)}, u32[]{:S(2)}, u32[]{:S(2)}) collective-permute-start(bf16[512,256]{1,0:T(8,128)(2,1)S(1)} %broadcast_select_fusion), channel_id=1, source_target_pairs={{0,2},{2,0},{4,6},{6,4},{8,10},{10,8},{12,14},{14,12},{1,3},{3,1},... | collective-permute-start | bytes 786440 | tf_op jit(solution)/shard_map/ppermute | solution.py:421
  25.9 0.0 collective-permute-done.1.near_ref
  25.9 1.8 %shard_map.57.refs_0_ = bf16[512,256]{1,0:T(8,128)(2,1)S(1)} custom-call(bf16[512,1024]{1,0:T(8,128)(2,1)S(1)} %get-tuple-element.40.q_ref, bf16[1536,128]{1,0:T(8,128)(2,1)S(1)} %get-tuple-element.55.mark_ref, bf16[512,256]{1,0:T(8,128)(2,1)S(1)} %get-tuple-element.35.own_ref, bf16[512,256]{1,0:T(8,128)(2,1)S(1)} %collective-permute-done.1.near_ref, ...), custom_call_target="tpu_custom_call" | custom-call | flops 1024 | bytes 1024 | tf_op jit(solution)/shard_map/pallas_call | solution.py:214
  27.7 0.1 collective-permute-start.9
  27.8 2.2 %collective-permute-done.4.near_ref = bf16[512,256]{1,0:T(8,128)(2,1)S(1)} collective-permute-done((bf16[512,256]{1,0:T(8,128)(2,1)S(1)}, bf16[512,256]{1,0:T(8,128)(2,1)S(1)}, u32[]{:S(2)}, u32[]{:S(2)}) %collective-permute-start.4) | collective-permute-done | bytes 262176 | tf_op jit(solution)/shard_map/ppermute | solution.py:421
  30.0 1.8 %shard_map.58.refs_1_ = bf16[512,256]{1,0:T(8,128)(2,1)S(1)} custom-call(bf16[512,1024]{1,0:T(8,128)(2,1)S(1)} %get-tuple-element.40.q_ref, bf16[1536,128]{1,0:T(8,128)(2,1)S(1)} %get-tuple-element.55.mark_ref, bf16[512,256]{1,0:T(8,128)(2,1)S(1)} %get-tuple-element.46.own_ref, bf16[512,256]{1,0:T(8,128)(2,1)S(1)} %collective-permute-done.4.near_ref, ...), custom_call_target="tpu_custom_call" | custom-call | flops 1024 | bytes 1024 | tf_op jit(solution)/shard_map/pallas_call | solution.py:214
  31.8 0.0 slice-start
  31.8 0.0 slice-start.1
  31.8 2.6 %shard_map.60.refs_11_ = f32[512,4608]{1,0:T(8,128)S(1)} custom-call(bf16[512,256]{1,0:T(8,128)(2,1)S(1)} %shard_map.57.refs_0_, bf16[512,256]{1,0:T(8,128)(2,1)S(1)} %shard_map.58.refs_1_, bf16[512,4608]{1,0:T(8,128)(2,1)S(1)} %shard_map.59.refs_2_), custom_call_target="tpu_custom_call" | custom-call | flops 1024 | bytes 1024 | tf_op jit(solution)/shard_map/pallas_call | solution.py:265
  34.4 0.0 collective-permute-done.6.near_ref
  34.5 1.8 %shard_map.61.refs_2_ = bf16[512,256]{1,0:T(8,128)(2,1)S(1)} custom-call(bf16[512,1024]{1,0:T(8,128)(2,1)S(1)} %get-tuple-element.40.q_ref, bf16[1536,128]{1,0:T(8,128)(2,1)S(1)} %get-tuple-element.55.mark_ref, bf16[512,256]{1,0:T(8,128)(2,1)S(1)} %get-tuple-element.47.own_ref, bf16[512,256]{1,0:T(8,128)(2,1)S(1)} %collective-permute-done.6.near_ref, ...), custom_call_target="tpu_custom_call" | custom-call | flops 1024 | bytes 1024 | tf_op jit(solution)/shard_map/pallas_call | solution.py:214
  36.3 0.1 collective-permute-start.11
  36.4 0.5 collective-permute-start.10
  36.9 0.0 collective-permute-done.7
  36.9 0.0 collective-permute-done.8.refs_0_.refs_9_
  36.9 0.0 slice-start.2
  36.9 2.1 %shard_map.62 = (bf16[512,256]{1,0:T(8,128)(2,1)S(1)}, bf16[1024,768]{1,0:T(8,128)(2,1)S(1)}, bf16[1024,768]{1,0:T(8,128)(2,1)S(1)}) custom-call(bf16[512,1024]{1,0:T(8,128)(2,1)S(1)} %get-tuple-element.40.q_ref, bf16[1536,128]{1,0:T(8,128)(2,1)S(1)} %get-tuple-element.55.mark_ref, bf16[512,256]{1,0:T(8,128)(2,1)S(1)} %get-tuple-element.42.own_ref, ...), custom_call_target="tpu_custom_call" | custom-call | flops 1024 | bytes 1024 | tf_op jit(solution)/shard_map/pallas_call | solution.py:214
  39.0 0.1 collective-permute-start.12
  39.2 0.0 collective-permute-done.9.refs_3_.refs_4_
  39.2 0.0 collective-permute-done.11.refs_5_.refs_6_
  39.2 0.0 collective-permute-done.10.refs_4_.refs_5_
  39.2 0.0 slice-done
  39.2 0.0 slice-done.1
  39.2 0.4 slice-done.2
  39.6 1.4 %shard_map.63.refs_10_ = f32[512,768]{1,0:T(8,128)S(1)} custom-call(bf16[512,256]{1,0:T(8,128)(2,1)S(1)} %shard_map.57.refs_0_, bf16[512,256]{1,0:T(8,128)(2,1)S(1)} %shard_map.58.refs_1_, bf16[512,256]{1,0:T(8,128)(2,1)S(1)} %shard_map.61.refs_2_, bf16[512,256]{1,0:T(8,128)(2,1)S(1)} %collective-permute-done.9.refs_3_.refs_4_, ...), custom_call_target="tpu_custom_call" | custom-call | flops 1207959552 | bytes 4194304 | tf_op jit(solution)/shard_map/pallas_call | solution.py:295
  41.0 0.0 collective-permute-done.12.refs_7_
  41.0 9.9 %shard_map.64 = bf16[512,5376]{1,0:T(8,128)(2,1)} custom-call(bf16[512,256]{1,0:T(8,128)(2,1)S(1)} %shard_map.57.refs_0_, bf16[512,256]{1,0:T(8,128)(2,1)S(1)} %shard_map.58.refs_1_, bf16[512,256]{1,0:T(8,128)(2,1)S(1)} %shard_map.61.refs_2_, bf16[512,256]{1,0:T(8,128)(2,1)S(1)} %get-tuple-element.57.refs_3_, ...), custom_call_target="tpu_custom_call" | custom-call | flops 11274289152 | bytes 33554432 | tf_op jit(solution)/shard_map/pallas_call | solution.py:379
  (6 shorter events, 0.2 us)
Async XLA Ops:
  1.4 35.5 %collective-permute-start.8 = (bf16[1024,5376]{1,0:T(8,128)(2,1)}, bf16[1024,5376]{1,0:T(8,128)(2,1)}, u32[]{:S(2)}, u32[]{:S(2)}) collective-permute-start(bf16[1024,5376]{1,0:T(8,128)(2,1)} %refs_8_), channel_id=1, source_target_pairs={{0,1},{1,0},{2,3},{3,2},{4,5},{5,4},{6,7},{7,6},{8,9},{9,8},{10,11... | collective-permute-start | bytes 33030152 | tf_op jit(solution)/shard_map/ppermute | solution.py:410
  1.9 13.1 %collective-permute-start = (bf16[512,256]{1,0:T(8,128)(2,1)S(1)}, bf16[512,256]{1,0:T(8,128)(2,1)S(1)}, u32[]{:S(2)}, u32[]{:S(2)}) collective-permute-start(bf16[512,256]{1,0:T(8,128)(2,1)S(1)} %get-tuple-element.35.own_ref), channel_id=1, source_target_pairs={{0,4},{2,6},{4,8},{6,10},{8,12},{10,14},{1,5},{3,7},{5,9},{7,11},{... | collective-permute-start | bytes 786440 | tf_op jit(solution)/shard_map/ppermute | solution.py:414
  6.4 9.2 %collective-permute-start.2 = (bf16[512,256]{1,0:T(8,128)(2,1)S(1)}, bf16[512,256]{1,0:T(8,128)(2,1)S(1)}, u32[]{:S(2)}, u32[]{:S(2)}) collective-permute-start(bf16[512,256]{1,0:T(8,128)(2,1)S(1)} %get-tuple-element.42.own_ref), channel_id=1, source_target_pairs={{0,2},{2,0},{4,6},{6,4},{8,10},{10,8},{12,14},{14,12},{1,3},{3,1},... | collective-permute-start | bytes 786440 | tf_op jit(solution)/shard_map/ppermute | solution.py:422
  8.0 11.1 %collective-permute-start.3 = (bf16[512,256]{1,0:T(8,128)(2,1)S(1)}, bf16[512,256]{1,0:T(8,128)(2,1)S(1)}, u32[]{:S(2)}, u32[]{:S(2)}) collective-permute-start(bf16[512,256]{1,0:T(8,128)(2,1)S(1)} %get-tuple-element.46.own_ref), channel_id=1, source_target_pairs={{0,4},{2,6},{4,8},{6,10},{8,12},{10,14},{1,5},{3,7},{5,9},{7,11},{... | collective-permute-start | bytes 786440 | tf_op jit(solution)/shard_map/ppermute | solution.py:414
  11.5 13.1 %collective-permute-start.5 = (bf16[512,256]{1,0:T(8,128)(2,1)S(1)}, bf16[512,256]{1,0:T(8,128)(2,1)S(1)}, u32[]{:S(2)}, u32[]{:S(2)}) collective-permute-start(bf16[512,256]{1,0:T(8,128)(2,1)S(1)} %get-tuple-element.47.own_ref), channel_id=1, source_target_pairs={{0,4},{2,6},{4,8},{6,10},{8,12},{10,14},{1,5},{3,7},{5,9},{7,11},{... | collective-permute-start | bytes 786440 | tf_op jit(solution)/shard_map/ppermute | solution.py:414
  15.0 10.8 %collective-permute-start.1 = (bf16[512,256]{1,0:T(8,128)(2,1)S(1)}, bf16[512,256]{1,0:T(8,128)(2,1)S(1)}, u32[]{:S(2)}, u32[]{:S(2)}) collective-permute-start(bf16[512,256]{1,0:T(8,128)(2,1)S(1)} %broadcast_select_fusion.2), channel_id=1, source_target_pairs={{0,2},{2,0},{4,6},{6,4},{8,10},{10,8},{12,14},{14,12},{1,3},{3,1},... | collective-permute-start | bytes 786440 | tf_op jit(solution)/shard_map/ppermute | solution.py:421
  15.7 21.2 %collective-permute-start.7 = (bf16[1024,256]{1,0:T(8,128)(2,1)S(1)}, bf16[1024,256]{1,0:T(8,128)(2,1)S(1)}, u32[]{:S(2)}, u32[]{:S(2)}) collective-permute-start(bf16[1024,256]{1,0:T(8,128)(2,1)S(1)} %pad_maximum_fusion), channel_id=1, source_target_pairs={{0,4},{2,6},{4,8},{6,10},{8,12},{10,14},{1,5},{3,7},{5,9},{7,11},{... | collective-permute-start | bytes 1572872 | tf_op jit(solution)/shard_map/ppermute | solution.py:424
  19.1 10.8 %collective-permute-start.4 = (bf16[512,256]{1,0:T(8,128)(2,1)S(1)}, bf16[512,256]{1,0:T(8,128)(2,1)S(1)}, u32[]{:S(2)}, u32[]{:S(2)}) collective-permute-start(bf16[512,256]{1,0:T(8,128)(2,1)S(1)} %broadcast_select_fusion.1), channel_id=1, source_target_pairs={{0,2},{2,0},{4,6},{6,4},{8,10},{10,8},{12,14},{14,12},{1,3},{3,1},... | collective-permute-start | bytes 786440 | tf_op jit(solution)/shard_map/ppermute | solution.py:421
  20.2 0.7 %copy-start = (s32[4096]{0:T(1024)S(1)}, s32[4096]{0:T(1024)}, u32[]{:S(2)}) copy-start(s32[4096]{0:T(1024)} %param.8) | copy-start | bytes 49156
  24.6 9.8 %collective-permute-start.6 = (bf16[512,256]{1,0:T(8,128)(2,1)S(1)}, bf16[512,256]{1,0:T(8,128)(2,1)S(1)}, u32[]{:S(2)}, u32[]{:S(2)}) collective-permute-start(bf16[512,256]{1,0:T(8,128)(2,1)S(1)} %broadcast_select_fusion), channel_id=1, source_target_pairs={{0,2},{2,0},{4,6},{6,4},{8,10},{10,8},{12,14},{14,12},{1,3},{3,1},... | collective-permute-start | bytes 786440 | tf_op jit(solution)/shard_map/ppermute | solution.py:421
  27.7 11.5 %collective-permute-start.9 = (bf16[512,256]{1,0:T(8,128)(2,1)S(1)}, bf16[512,256]{1,0:T(8,128)(2,1)S(1)}, u32[]{:S(2)}, u32[]{:S(2)}) collective-permute-start(bf16[512,256]{1,0:T(8,128)(2,1)S(1)} %shard_map.57.refs_0_), channel_id=1, source_target_pairs={{0,1},{1,0},{2,3},{3,2},{4,5},{5,4},{6,7},{7,6},{8,9},{9,8},{10,11... | collective-permute-start | bytes 786440 | tf_op jit(solution)/shard_map/ppermute | solution.py:439
  31.8 7.4 %slice-start = ((s8[11010048]{0:T(1024)(128)(4,1)}), s8[4194304]{0:T(1024)(128)(4,1)S(1)}, s32[]{:S(2)}) async-start(s8[11010048]{0:T(1024)(128)(4,1)} %bitcast.2), calls=%async_computation | async-start | bytes 8388608
  31.8 7.4 %slice-start.1 = ((s8[11010048]{0:T(1024)(128)(4,1)}), s8[4194304]{0:T(1024)(128)(4,1)S(1)}, s32[]{:S(2)}) async-start(s8[11010048]{0:T(1024)(128)(4,1)} %bitcast.2), calls=%async_computation.1 | async-start | bytes 8388608
  36.3 2.9 %collective-permute-start.11 = (bf16[512,256]{1,0:T(8,128)(2,1)S(1)}, bf16[512,256]{1,0:T(8,128)(2,1)S(1)}, u32[]{:S(2)}, u32[]{:S(2)}) collective-permute-start(bf16[512,256]{1,0:T(8,128)(2,1)S(1)} %shard_map.61.refs_2_), channel_id=1, source_target_pairs={{0,1},{1,0},{2,3},{3,2},{4,5},{5,4},{6,7},{7,6},{8,9},{9,8},{10,11... | collective-permute-start | bytes 786440 | tf_op jit(solution)/shard_map/ppermute | solution.py:439
  36.4 2.8 %collective-permute-start.10 = (bf16[512,256]{1,0:T(8,128)(2,1)S(1)}, bf16[512,256]{1,0:T(8,128)(2,1)S(1)}, u32[]{:S(2)}, u32[]{:S(2)}) collective-permute-start(bf16[512,256]{1,0:T(8,128)(2,1)S(1)} %shard_map.58.refs_1_), channel_id=1, source_target_pairs={{0,1},{1,0},{2,3},{3,2},{4,5},{5,4},{6,7},{7,6},{8,9},{9,8},{10,11... | collective-permute-start | bytes 786440 | tf_op jit(solution)/shard_map/ppermute | solution.py:439
  36.9 2.7 %slice-start.2 = ((s8[11010048]{0:T(1024)(128)(4,1)}), s8[2621440]{0:T(1024)(128)(4,1)S(1)}, s32[]{:S(2)}) async-start(s8[11010048]{0:T(1024)(128)(4,1)} %bitcast.2), calls=%async_computation.2 | async-start | bytes 5242880
  39.0 2.0 %collective-permute-start.12 = (bf16[512,256]{1,0:T(8,128)(2,1)S(1)}, bf16[512,256]{1,0:T(8,128)(2,1)S(1)}, u32[]{:S(2)}, u32[]{:S(2)}) collective-permute-start(bf16[512,256]{1,0:T(8,128)(2,1)S(1)} %get-tuple-element.57.refs_3_), channel_id=1, source_target_pairs={{0,1},{1,0},{2,3},{3,2},{4,5},{5,4},{6,7},{7,6},{8,9},{9,8},{10,11... | collective-permute-start | bytes 786440 | tf_op jit(solution)/shard_map/ppermute | solution.py:439

commit v10 on v9

--- a/solution.py
+++ b/solution.py
@@ -281,15 +281,17 @@
 
     def kernel(*refs):
         own_refs, other_refs = refs[:count], refs[count : 2 * count]
-        own_w_ref, ready_ref, out_ref, row, other_row = refs[2 * count :]
+        own_w_ref, ready_ref, out_ref, row, other_row, other_sum = refs[2 * count :]
         for into, group in ((row, own_refs), (other_row, other_refs)):
             for i, ref in enumerate(group):
                 into[:, i * width : (i + 1) * width] = ref[...]
-        term = jnp.dot(row[...], own_w_ref[:depth, :tile], preferred_element_type=jnp.float32)
-        other_term = jnp.dot(
+        out_ref[...] = jnp.dot(
+            row[...], own_w_ref[:depth, :tile], preferred_element_type=jnp.float32
+        )
+        other_sum[...] = jnp.dot(
             other_row[...], ready_ref[:depth, :], preferred_element_type=jnp.float32
         )
-        out_ref[...] = term + other_term
+        out_ref[...] = out_ref[...] + other_sum[...]
 
     vmem = pl.BlockSpec(memory_space=pltpu.VMEM)
     return pl.pallas_call(
@@ -297,7 +299,8 @@
         in_specs=[vmem] * (2 * count + 2),
         out_specs=vmem,
         out_shape=pltpu.VMEM((rows, tile), jnp.float32),
-        scratch_shapes=[pltpu.VMEM((rows, depth), jnp.bfloat16)] * 2,
+        scratch_shapes=[pltpu.VMEM((rows, depth), jnp.bfloat16)] * 2
+        + [pltpu.VMEM((rows, tile), jnp.float32)],
         compiler_params=pltpu.CompilerParams(vmem_limit_bytes=8 * MIB),
         cost_estimate=pl.CostEstimate(
             flops=4 * rows * depth * tile, bytes_accessed=4 * MIB, transcendentals=0
@@ -318,7 +321,7 @@
         own_w_ref, other_w_ref, *refs = refs[2 * count :]
         base_ref, own_base_ref, *refs = refs
         ready_refs, refs = refs[: len(ready)], refs[len(ready) :]
-        out_ref, row, other_row, other_base, held, out_sem, w_buf, w_sem = refs
+        out_ref, row, other_row, own_sum, other_base, held, out_sem, w_buf, w_sem = refs
 
         def place(n):
             return pl.ds(pl.multiple_of(n * tile, tile), tile)
@@ -343,15 +346,16 @@
 
         def multiply_first(weight):
             down = slice(depth - own_refs[-1].shape[1], depth)
-            total = dot(row, own_w_ref, down, place(0)) + dot(other_row, weight, down)
-            finish(0, total + base_ref[...])
+            own_sum[...] = dot(row, own_w_ref, down, place(0))
+            other_base[...] = dot(other_row, weight, down)
+            finish(0, (own_sum[...] + other_base[...]) + base_ref[...])
 
         def multiply(n, weight):
             half, rest = slice(0, depth // 2), slice(depth // 2, depth)
             other_base[...] = dot(other_row, weight, half)
-            term = own_base_ref[:, place(n - 1)] + dot(row, own_w_ref, rest, place(n))
-            other_term = other_base[...] + dot(other_row, weight, rest)
-            finish(n, term + other_term)
+            own_sum[...] = own_base_ref[:, place(n - 1)] + dot(row, own_w_ref, rest, place(n))
+            other_base[...] = other_base[...] + dot(other_row, weight, rest)
+            finish(n, own_sum[...] + other_base[...])
 
         for n in range(len(ready), tiles):
             coming(n).start()
@@ -385,12 +389,13 @@
             pltpu.VMEM((rows, depth), jnp.bfloat16),
             pltpu.VMEM((rows, depth), jnp.bfloat16),
             pltpu.VMEM((rows, tile), jnp.float32),
+            pltpu.VMEM((rows, tile), jnp.float32),
             pltpu.VMEM((rows, columns), jnp.bfloat16),
             pltpu.SemaphoreType.DMA((tiles,)),
             pltpu.VMEM((late, depth, tile), jnp.bfloat16),
             pltpu.SemaphoreType.DMA((late,)),
         ],
-        compiler_params=pltpu.CompilerParams(vmem_limit_bytes=24 * MIB),
+        compiler_params=pltpu.CompilerParams(vmem_limit_bytes=26 * MIB),
         cost_estimate=pl.CostEstimate(
             flops=4 * rows * depth * columns, bytes_accessed=32 * MIB, transcendentals=0
         ),

time: 51.3 us -> 52.1 us (1.016)
  Pallas kernels: 26.5 us -> 27.2 us
    pallas_call x1, Pallas kernels: 9.95 us -> 10.7 us  [project(): pl.pallas_call(kernel, in_specs=[vmem] * (2 * count + 1) + [hbm] + [vmem]...]
  transfers between devices with their start and end apart: 13 -> 13, of which waited for: 1 -> 1; matrix products, arithmetic and copies ran while one was open for 0% -> 0% of each run, Pallas kernels for 30% -> 29%
where the time goes in v10:
time: 52.1 us; the launch traced here: 51.8 us
  Pallas kernels  27.2 us (52%)
  starting transfers between devices  20.7 us (40%)
  waiting for transfers between devices  2.22 us (4%)
  local copies, waits for them, and re-layouts  1.16 us (2%)
    ppermute x3, starting transfers between devices, shards(): far = [lax.ppermute(x, 'seq', two_on) for x in own[:-1]]  11.5 us
    pallas_call x1, Pallas kernels, project(): pl.pallas_call(kernel, in_specs=[vmem] * (2 * count + 1) + [hbm] + [vmem]...  10.7 us
    pallas_call x4, Pallas kernels, attend(): pl.pallas_call(kernel, in_specs=specs, out_specs=[vmem] * len(outs), out_...  7.56 us
    ppermute x1, starting transfers between devices, shards(): last = lax.ppermute(last, 'seq', two_on)  3.44 us
    ppermute x3, starting transfers between devices, shards(): lax.ppermute(jnp.where(odd, f, x), 'seq', pair)  2.92 us
    pallas_call x1, Pallas kernels, project_own(): pl.pallas_call(kernel, in_specs=[vmem] * (count + 1), out_specs=vmem, out...  2.62 us
    pallas_call x1, Pallas kernels, stage(): pl.pallas_call(functools.partial(stage_kernel, skip=skip), in_specs=[pl.B...  2.35 us
    ppermute x3, waiting for transfers between devices, shards(): lax.ppermute(jnp.where(odd, f, x), 'seq', pair)  2.2 us
  transfers between devices with their start and end apart: 13, of which 1 were waited for; matrix products, arithmetic and copies ran while one was open for 0% of the time, Pallas kernels for 29%

profile of v10, /device:TPU:0, one launch (start us, length us, event | category | flops | bytes accessed | tf_op | source)
XLA Modules:
  0.0 51.8 jit_solution(4291860644964318064)
XLA Ops:
  0.0 1.4 %shard_map.55 = (bf16[512,256]{1,0:T(8,128)(2,1)S(1)}, bf16[512,256]{1,0:T(8,128)(2,1)S(1)}, bf16[512,256]{1,0:T(8,128)(2,1)S(1)}, bf16[512,256]{1,0:T(8,128)(2,1)S(1)}) custom-call(bf16[512,512]{1,0:T(8,128)(2,1)} %keys_ref.1, bf16[512,512]{1,0:T(8,128)(2,1)} %values_ref.1), custom_call_target="tpu_custom_call" | custom-call | bytes 2097152 | tf_op jit(solution)/shard_map/pallas_call | solution.py:125
  1.4 0.5 %collective-permute-start.8 = (bf16[1024,5376]{1,0:T(8,128)(2,1)}, bf16[1024,5376]{1,0:T(8,128)(2,1)}, u32[]{:S(2)}, u32[]{:S(2)}) collective-permute-start(bf16[1024,5376]{1,0:T(8,128)(2,1)} %refs_8_), channel_id=1, source_target_pairs={{0,1},{1,0},{2,3},{3,2},{4,5},{5,4},{6,7},{7,6},{8,9},{9,8},{10,11... | collective-permute-start | bytes 33030152 | tf_op jit(solution)/shard_map/ppermute | solution.py:415
  1.9 4.5 %collective-permute-start = (bf16[512,256]{1,0:T(8,128)(2,1)S(1)}, bf16[512,256]{1,0:T(8,128)(2,1)S(1)}, u32[]{:S(2)}, u32[]{:S(2)}) collective-permute-start(bf16[512,256]{1,0:T(8,128)(2,1)S(1)} %get-tuple-element.35.own_ref), channel_id=1, source_target_pairs={{0,4},{2,6},{4,8},{6,10},{8,12},{10,14},{1,5},{3,7},{5,9},{7,11},{... | collective-permute-start | bytes 786440 | tf_op jit(solution)/shard_map/ppermute | solution.py:419
  6.4 1.6 %collective-permute-start.2 = (bf16[512,256]{1,0:T(8,128)(2,1)S(1)}, bf16[512,256]{1,0:T(8,128)(2,1)S(1)}, u32[]{:S(2)}, u32[]{:S(2)}) collective-permute-start(bf16[512,256]{1,0:T(8,128)(2,1)S(1)} %get-tuple-element.42.own_ref), channel_id=1, source_target_pairs={{0,2},{2,0},{4,6},{6,4},{8,10},{10,8},{12,14},{14,12},{1,3},{3,1},... | collective-permute-start | bytes 786440 | tf_op jit(solution)/shard_map/ppermute | solution.py:427
  8.0 3.5 %collective-permute-start.3 = (bf16[512,256]{1,0:T(8,128)(2,1)S(1)}, bf16[512,256]{1,0:T(8,128)(2,1)S(1)}, u32[]{:S(2)}, u32[]{:S(2)}) collective-permute-start(bf16[512,256]{1,0:T(8,128)(2,1)S(1)} %get-tuple-element.46.own_ref), channel_id=1, source_target_pairs={{0,4},{2,6},{4,8},{6,10},{8,12},{10,14},{1,5},{3,7},{5,9},{7,11},{... | collective-permute-start | bytes 786440 | tf_op jit(solution)/shard_map/ppermute | solution.py:419
  11.5 3.5 %collective-permute-start.5 = (bf16[512,256]{1,0:T(8,128)(2,1)S(1)}, bf16[512,256]{1,0:T(8,128)(2,1)S(1)}, u32[]{:S(2)}, u32[]{:S(2)}) collective-permute-start(bf16[512,256]{1,0:T(8,128)(2,1)S(1)} %get-tuple-element.47.own_ref), channel_id=1, source_target_pairs={{0,4},{2,6},{4,8},{6,10},{8,12},{10,14},{1,5},{3,7},{5,9},{7,11},{... | collective-permute-start | bytes 786440 | tf_op jit(solution)/shard_map/ppermute | solution.py:419
  15.0 0.0 collective-permute-done.far_ref
  15.0 0.6 %collective-permute-start.1 = (bf16[512,256]{1,0:T(8,128)(2,1)S(1)}, bf16[512,256]{1,0:T(8,128)(2,1)S(1)}, u32[]{:S(2)}, u32[]{:S(2)}) collective-permute-start(bf16[512,256]{1,0:T(8,128)(2,1)S(1)} %broadcast_select_fusion.2), channel_id=1, source_target_pairs={{0,2},{2,0},{4,6},{6,4},{8,10},{10,8},{12,14},{14,12},{1,3},{3,1},... | collective-permute-start | bytes 786440 | tf_op jit(solution)/shard_map/ppermute | solution.py:426
  15.6 0.0 collective-permute-done.2
  15.7 3.4 %collective-permute-start.7 = (bf16[1024,256]{1,0:T(8,128)(2,1)S(1)}, bf16[1024,256]{1,0:T(8,128)(2,1)S(1)}, u32[]{:S(2)}, u32[]{:S(2)}) collective-permute-start(bf16[1024,256]{1,0:T(8,128)(2,1)S(1)} %pad_maximum_fusion), channel_id=1, source_target_pairs={{0,4},{2,6},{4,8},{6,10},{8,12},{10,14},{1,5},{3,7},{5,9},{7,11},{... | collective-permute-start | bytes 1572872 | tf_op jit(solution)/shard_map/ppermute | solution.py:429
  19.1 0.0 collective-permute-done.3.far_ref
  19.1 1.1 %collective-permute-start.4 = (bf16[512,256]{1,0:T(8,128)(2,1)S(1)}, bf16[512,256]{1,0:T(8,128)(2,1)S(1)}, u32[]{:S(2)}, u32[]{:S(2)}) collective-permute-start(bf16[512,256]{1,0:T(8,128)(2,1)S(1)} %broadcast_select_fusion.1), channel_id=1, source_target_pairs={{0,2},{2,0},{4,6},{6,4},{8,10},{10,8},{12,14},{14,12},{1,3},{3,1},... | collective-permute-start | bytes 786440 | tf_op jit(solution)/shard_map/ppermute | solution.py:426
  20.2 0.0 copy-start
  20.3 0.7 %copy-done = s32[4096]{0:T(1024)S(1)} copy-done((s32[4096]{0:T(1024)S(1)}, s32[4096]{0:T(1024)}, u32[]{:S(2)}) %copy-start) | copy-done | bytes 16408
  21.0 1.2 %shard_map.56 = (bf16[1536,128]{1,0:T(8,128)(2,1)S(1)}, bf16[512,1024]{1,0:T(8,128)(2,1)S(1)}) custom-call(s32[1]{0:T(128)} %bitcast.index_ref, s32[32,128]{1,0:T(8,128)S(1)} %bitcast.4, bf16[512,1024]{1,0:T(8,128)(2,1)} %q_ref), custom_call_target="tpu_custom_call" | custom-call | flops 1024 | bytes 1024 | tf_op jit(solution)/shard_map/pallas_call | solution.py:157
  22.2 2.3 %shard_map.59.refs_2_ = bf16[512,4608]{1,0:T(8,128)(2,1)S(1)} custom-call(bf16[1024,5376]{1,0:T(8,128)(2,1)} %refs_8_), custom_call_target="tpu_custom_call" | custom-call | flops 1024 | bytes 1024 | tf_op jit(solution)/shard_map/pallas_call | solution.py:235
  24.6 0.0 collective-permute-done.5.far_ref
  24.6 1.2 %collective-permute-start.6 = (bf16[512,256]{1,0:T(8,128)(2,1)S(1)}, bf16[512,256]{1,0:T(8,128)(2,1)S(1)}, u32[]{:S(2)}, u32[]{:S(2)}) collective-permute-start(bf16[512,256]{1,0:T(8,128)(2,1)S(1)} %broadcast_select_fusion), channel_id=1, source_target_pairs={{0,2},{2,0},{4,6},{6,4},{8,10},{10,8},{12,14},{14,12},{1,3},{3,1},... | collective-permute-start | bytes 786440 | tf_op jit(solution)/shard_map/ppermute | solution.py:426
  25.9 0.0 collective-permute-done.1.near_ref
  25.9 1.8 %shard_map.57.refs_0_ = bf16[512,256]{1,0:T(8,128)(2,1)S(1)} custom-call(bf16[512,1024]{1,0:T(8,128)(2,1)S(1)} %get-tuple-element.40.q_ref, bf16[1536,128]{1,0:T(8,128)(2,1)S(1)} %get-tuple-element.55.mark_ref, bf16[512,256]{1,0:T(8,128)(2,1)S(1)} %get-tuple-element.35.own_ref, bf16[512,256]{1,0:T(8,128)(2,1)S(1)} %collective-permute-done.1.near_ref, ...), custom_call_target="tpu_custom_call" | custom-call | flops 1024 | bytes 1024 | tf_op jit(solution)/shard_map/pallas_call | solution.py:214
  27.7 0.1 collective-permute-start.9
  27.8 2.2 %collective-permute-done.4.near_ref = bf16[512,256]{1,0:T(8,128)(2,1)S(1)} collective-permute-done((bf16[512,256]{1,0:T(8,128)(2,1)S(1)}, bf16[512,256]{1,0:T(8,128)(2,1)S(1)}, u32[]{:S(2)}, u32[]{:S(2)}) %collective-permute-start.4) | collective-permute-done | bytes 262176 | tf_op jit(solution)/shard_map/ppermute | solution.py:426
  30.0 1.8 %shard_map.58.refs_1_ = bf16[512,256]{1,0:T(8,128)(2,1)S(1)} custom-call(bf16[512,1024]{1,0:T(8,128)(2,1)S(1)} %get-tuple-element.40.q_ref, bf16[1536,128]{1,0:T(8,128)(2,1)S(1)} %get-tuple-element.55.mark_ref, bf16[512,256]{1,0:T(8,128)(2,1)S(1)} %get-tuple-element.46.own_ref, bf16[512,256]{1,0:T(8,128)(2,1)S(1)} %collective-permute-done.4.near_ref, ...), custom_call_target="tpu_custom_call" | custom-call | flops 1024 | bytes 1024 | tf_op jit(solution)/shard_map/pallas_call | solution.py:214
  31.8 0.0 slice-start
  31.8 0.0 slice-start.1
  31.8 2.6 %shard_map.60.refs_11_ = f32[512,4608]{1,0:T(8,128)S(1)} custom-call(bf16[512,256]{1,0:T(8,128)(2,1)S(1)} %shard_map.57.refs_0_, bf16[512,256]{1,0:T(8,128)(2,1)S(1)} %shard_map.58.refs_1_, bf16[512,4608]{1,0:T(8,128)(2,1)S(1)} %shard_map.59.refs_2_), custom_call_target="tpu_custom_call" | custom-call | flops 1024 | bytes 1024 | tf_op jit(solution)/shard_map/pallas_call | solution.py:265
  34.4 0.0 collective-permute-done.6.near_ref
  34.5 1.8 %shard_map.61.refs_2_ = bf16[512,256]{1,0:T(8,128)(2,1)S(1)} custom-call(bf16[512,1024]{1,0:T(8,128)(2,1)S(1)} %get-tuple-element.40.q_ref, bf16[1536,128]{1,0:T(8,128)(2,1)S(1)} %get-tuple-element.55.mark_ref, bf16[512,256]{1,0:T(8,128)(2,1)S(1)} %get-tuple-element.47.own_ref, bf16[512,256]{1,0:T(8,128)(2,1)S(1)} %collective-permute-done.6.near_ref, ...), custom_call_target="tpu_custom_call" | custom-call | flops 1024 | bytes 1024 | tf_op jit(solution)/shard_map/pallas_call | solution.py:214
  36.3 0.1 collective-permute-start.11
  36.4 0.5 collective-permute-start.10
  36.9 0.0 collective-permute-done.7
  36.9 0.0 collective-permute-done.8.refs_0_.refs_9_
  36.9 0.0 slice-start.2
  36.9 2.1 %shard_map.62 = (bf16[512,256]{1,0:T(8,128)(2,1)S(1)}, bf16[1024,768]{1,0:T(8,128)(2,1)S(1)}, bf16[1024,768]{1,0:T(8,128)(2,1)S(1)}) custom-call(bf16[512,1024]{1,0:T(8,128)(2,1)S(1)} %get-tuple-element.40.q_ref, bf16[1536,128]{1,0:T(8,128)(2,1)S(1)} %get-tuple-element.55.mark_ref, bf16[512,256]{1,0:T(8,128)(2,1)S(1)} %get-tuple-element.42.own_ref, ...), custom_call_target="tpu_custom_call" | custom-call | flops 1024 | bytes 1024 | tf_op jit(solution)/shard_map/pallas_call | solution.py:214
  39.0 0.1 collective-permute-start.12
  39.2 0.0 collective-permute-done.9.refs_3_.refs_4_
  39.2 0.0 collective-permute-done.11.refs_5_.refs_6_
  39.2 0.0 collective-permute-done.10.refs_4_.refs_5_
  39.2 0.0 slice-done
  39.2 0.0 slice-done.1
  39.2 0.4 slice-done.2
  39.6 1.4 %shard_map.63.refs_10_ = f32[512,768]{1,0:T(8,128)S(1)} custom-call(bf16[512,256]{1,0:T(8,128)(2,1)S(1)} %shard_map.57.refs_0_, bf16[512,256]{1,0:T(8,128)(2,1)S(1)} %shard_map.58.refs_1_, bf16[512,256]{1,0:T(8,128)(2,1)S(1)} %shard_map.61.refs_2_, bf16[512,256]{1,0:T(8,128)(2,1)S(1)} %collective-permute-done.9.refs_3_.refs_4_, ...), custom_call_target="tpu_custom_call" | custom-call | flops 1207959552 | bytes 4194304 | tf_op jit(solution)/shard_map/pallas_call | solution.py:297
  41.0 0.0 collective-permute-done.12.refs_7_
  41.0 10.7 %shard_map.64 = bf16[512,5376]{1,0:T(8,128)(2,1)} custom-call(bf16[512,256]{1,0:T(8,128)(2,1)S(1)} %shard_map.57.refs_0_, bf16[512,256]{1,0:T(8,128)(2,1)S(1)} %shard_map.58.refs_1_, bf16[512,256]{1,0:T(8,128)(2,1)S(1)} %shard_map.61.refs_2_, bf16[512,256]{1,0:T(8,128)(2,1)S(1)} %get-tuple-element.57.refs_3_, ...), custom_call_target="tpu_custom_call" | custom-call | flops 11274289152 | bytes 33554432 | tf_op jit(solution)/shard_map/pallas_call | solution.py:383
  (6 shorter events, 0.2 us)
Async XLA Ops:
  1.4 35.5 %collective-permute-start.8 = (bf16[1024,5376]{1,0:T(8,128)(2,1)}, bf16[1024,5376]{1,0:T(8,128)(2,1)}, u32[]{:S(2)}, u32[]{:S(2)}) collective-permute-start(bf16[1024,5376]{1,0:T(8,128)(2,1)} %refs_8_), channel_id=1, source_target_pairs={{0,1},{1,0},{2,3},{3,2},{4,5},{5,4},{6,7},{7,6},{8,9},{9,8},{10,11... | collective-permute-start | bytes 33030152 | tf_op jit(solution)/shard_map/ppermute | solution.py:415
  1.9 13.1 %collective-permute-start = (bf16[512,256]{1,0:T(8,128)(2,1)S(1)}, bf16[512,256]{1,0:T(8,128)(2,1)S(1)}, u32[]{:S(2)}, u32[]{:S(2)}) collective-permute-start(bf16[512,256]{1,0:T(8,128)(2,1)S(1)} %get-tuple-element.35.own_ref), channel_id=1, source_target_pairs={{0,4},{2,6},{4,8},{6,10},{8,12},{10,14},{1,5},{3,7},{5,9},{7,11},{... | collective-permute-start | bytes 786440 | tf_op jit(solution)/shard_map/ppermute | solution.py:419
  6.4 9.2 %collective-permute-start.2 = (bf16[512,256]{1,0:T(8,128)(2,1)S(1)}, bf16[512,256]{1,0:T(8,128)(2,1)S(1)}, u32[]{:S(2)}, u32[]{:S(2)}) collective-permute-start(bf16[512,256]{1,0:T(8,128)(2,1)S(1)} %get-tuple-element.42.own_ref), channel_id=1, source_target_pairs={{0,2},{2,0},{4,6},{6,4},{8,10},{10,8},{12,14},{14,12},{1,3},{3,1},... | collective-permute-start | bytes 786440 | tf_op jit(solution)/shard_map/ppermute | solution.py:427
  8.0 11.1 %collective-permute-start.3 = (bf16[512,256]{1,0:T(8,128)(2,1)S(1)}, bf16[512,256]{1,0:T(8,128)(2,1)S(1)}, u32[]{:S(2)}, u32[]{:S(2)}) collective-permute-start(bf16[512,256]{1,0:T(8,128)(2,1)S(1)} %get-tuple-element.46.own_ref), channel_id=1, source_target_pairs={{0,4},{2,6},{4,8},{6,10},{8,12},{10,14},{1,5},{3,7},{5,9},{7,11},{... | collective-permute-start | bytes 786440 | tf_op jit(solution)/shard_map/ppermute | solution.py:419
  11.5 13.1 %collective-permute-start.5 = (bf16[512,256]{1,0:T(8,128)(2,1)S(1)}, bf16[512,256]{1,0:T(8,128)(2,1)S(1)}, u32[]{:S(2)}, u32[]{:S(2)}) collective-permute-start(bf16[512,256]{1,0:T(8,128)(2,1)S(1)} %get-tuple-element.47.own_ref), channel_id=1, source_target_pairs={{0,4},{2,6},{4,8},{6,10},{8,12},{10,14},{1,5},{3,7},{5,9},{7,11},{... | collective-permute-start | bytes 786440 | tf_op jit(solution)/shard_map/ppermute | solution.py:419
  15.0 10.8 %collective-permute-start.1 = (bf16[512,256]{1,0:T(8,128)(2,1)S(1)}, bf16[512,256]{1,0:T(8,128)(2,1)S(1)}, u32[]{:S(2)}, u32[]{:S(2)}) collective-permute-start(bf16[512,256]{1,0:T(8,128)(2,1)S(1)} %broadcast_select_fusion.2), channel_id=1, source_target_pairs={{0,2},{2,0},{4,6},{6,4},{8,10},{10,8},{12,14},{14,12},{1,3},{3,1},... | collective-permute-start | bytes 786440 | tf_op jit(solution)/shard_map/ppermute | solution.py:426
  15.7 21.2 %collective-permute-start.7 = (bf16[1024,256]{1,0:T(8,128)(2,1)S(1)}, bf16[1024,256]{1,0:T(8,128)(2,1)S(1)}, u32[]{:S(2)}, u32[]{:S(2)}) collective-permute-start(bf16[1024,256]{1,0:T(8,128)(2,1)S(1)} %pad_maximum_fusion), channel_id=1, source_target_pairs={{0,4},{2,6},{4,8},{6,10},{8,12},{10,14},{1,5},{3,7},{5,9},{7,11},{... | collective-permute-start | bytes 1572872 | tf_op jit(solution)/shard_map/ppermute | solution.py:429
  19.1 10.8 %collective-permute-start.4 = (bf16[512,256]{1,0:T(8,128)(2,1)S(1)}, bf16[512,256]{1,0:T(8,128)(2,1)S(1)}, u32[]{:S(2)}, u32[]{:S(2)}) collective-permute-start(bf16[512,256]{1,0:T(8,128)(2,1)S(1)} %broadcast_select_fusion.1), channel_id=1, source_target_pairs={{0,2},{2,0},{4,6},{6,4},{8,10},{10,8},{12,14},{14,12},{1,3},{3,1},... | collective-permute-start | bytes 786440 | tf_op jit(solution)/shard_map/ppermute | solution.py:426
  20.2 0.7 %copy-start = (s32[4096]{0:T(1024)S(1)}, s32[4096]{0:T(1024)}, u32[]{:S(2)}) copy-start(s32[4096]{0:T(1024)} %param.8) | copy-start | bytes 49156
  24.6 9.8 %collective-permute-start.6 = (bf16[512,256]{1,0:T(8,128)(2,1)S(1)}, bf16[512,256]{1,0:T(8,128)(2,1)S(1)}, u32[]{:S(2)}, u32[]{:S(2)}) collective-permute-start(bf16[512,256]{1,0:T(8,128)(2,1)S(1)} %broadcast_select_fusion), channel_id=1, source_target_pairs={{0,2},{2,0},{4,6},{6,4},{8,10},{10,8},{12,14},{14,12},{1,3},{3,1},... | collective-permute-start | bytes 786440 | tf_op jit(solution)/shard_map/ppermute | solution.py:426
  27.7 11.5 %collective-permute-start.9 = (bf16[512,256]{1,0:T(8,128)(2,1)S(1)}, bf16[512,256]{1,0:T(8,128)(2,1)S(1)}, u32[]{:S(2)}, u32[]{:S(2)}) collective-permute-start(bf16[512,256]{1,0:T(8,128)(2,1)S(1)} %shard_map.57.refs_0_), channel_id=1, source_target_pairs={{0,1},{1,0},{2,3},{3,2},{4,5},{5,4},{6,7},{7,6},{8,9},{9,8},{10,11... | collective-permute-start | bytes 786440 | tf_op jit(solution)/shard_map/ppermute | solution.py:444
  31.8 7.4 %slice-start = ((s8[11010048]{0:T(1024)(128)(4,1)}), s8[4194304]{0:T(1024)(128)(4,1)S(1)}, s32[]{:S(2)}) async-start(s8[11010048]{0:T(1024)(128)(4,1)} %bitcast.2), calls=%async_computation | async-start | bytes 8388608
  31.8 7.4 %slice-start.1 = ((s8[11010048]{0:T(1024)(128)(4,1)}), s8[4194304]{0:T(1024)(128)(4,1)S(1)}, s32[]{:S(2)}) async-start(s8[11010048]{0:T(1024)(128)(4,1)} %bitcast.2), calls=%async_computation.1 | async-start | bytes 8388608
  36.3 2.9 %collective-permute-start.11 = (bf16[512,256]{1,0:T(8,128)(2,1)S(1)}, bf16[512,256]{1,0:T(8,128)(2,1)S(1)}, u32[]{:S(2)}, u32[]{:S(2)}) collective-permute-start(bf16[512,256]{1,0:T(8,128)(2,1)S(1)} %shard_map.61.refs_2_), channel_id=1, source_target_pairs={{0,1},{1,0},{2,3},{3,2},{4,5},{5,4},{6,7},{7,6},{8,9},{9,8},{10,11... | collective-permute-start | bytes 786440 | tf_op jit(solution)/shard_map/ppermute | solution.py:444
  36.4 2.8 %collective-permute-start.10 = (bf16[512,256]{1,0:T(8,128)(2,1)S(1)}, bf16[512,256]{1,0:T(8,128)(2,1)S(1)}, u32[]{:S(2)}, u32[]{:S(2)}) collective-permute-start(bf16[512,256]{1,0:T(8,128)(2,1)S(1)} %shard_map.58.refs_1_), channel_id=1, source_target_pairs={{0,1},{1,0},{2,3},{3,2},{4,5},{5,4},{6,7},{7,6},{8,9},{9,8},{10,11... | collective-permute-start | bytes 786440 | tf_op jit(solution)/shard_map/ppermute | solution.py:444
  36.9 2.7 %slice-start.2 = ((s8[11010048]{0:T(1024)(128)(4,1)}), s8[2621440]{0:T(1024)(128)(4,1)S(1)}, s32[]{:S(2)}) async-start(s8[11010048]{0:T(1024)(128)(4,1)} %bitcast.2), calls=%async_computation.2 | async-start | bytes 5242880
  39.0 2.0 %collective-permute-start.12 = (bf16[512,256]{1,0:T(8,128)(2,1)S(1)}, bf16[512,256]{1,0:T(8,128)(2,1)S(1)}, u32[]{:S(2)}, u32[]{:S(2)}) collective-permute-start(bf16[512,256]{1,0:T(8,128)(2,1)S(1)} %get-tuple-element.57.refs_3_), channel_id=1, source_target_pairs={{0,1},{1,0},{2,3},{3,2},{4,5},{5,4},{6,7},{7,6},{8,9},{9,8},{10,11... | collective-permute-start | bytes 786440 | tf_op jit(solution)/shard_map/ppermute | solution.py:444
